TPU v7x, 256 devices: a whole 4x4x8 slice. The times are simulated.
256 devices in a mesh: pts: 64 (over z, y, core), cent: 4 (over x).
Axes of the slice: x: 4, y: 4, z: 8, core: 2. Of those that a mesh axis runs over, the one named last changes fastest.
Arguments:
- points: bfloat16 [524288, 512], P(('pts', 'cent')), may hold values from -128 to 128
- centroids: bfloat16 [65536, 512], P('pts'), may hold values from -32 to 32
- candidates: int32 [32768, 2], P(('pts', 'cent')), may hold values from 0 to 255, all different within a row; in each aligned block of 128 rows (0 to 127, 128 to 255, ...) at most 2 rows name the same one
Outputs:
- new_centroids: bfloat16 [65536, 512], P('pts')
- point_lse: float32 [524288], P(('pts', 'cent'))
Inputs may be any that keep to these rules, and one draw needn't show every extreme that they name: `candidates`: within the 128 point blocks of one device, no centroid block is named more than 2 times; the two ids of a point block differ.
All inputs are finite; a program needn't handle non-finite values.
Results may differ from a plain program's by a relative error of at most 0.006.
Values may be sent and summed in bfloat16 or wider, within the bound.
No kernel may reach another device: no remote copies, remote signals or barrier semaphores. Data moves between devices by JAX's collectives and lax.ppermute only.
A program may use at most 64 MiB of HBM per device.

v0:
```python
import math

import jax
import jax.numpy as jnp
from jax import lax
from jax.sharding import PartitionSpec as P

CB = 256
PB = 16
ITERS = 2


def split_up(value, dim, length):
    shape = value.shape
    parts = value.reshape(*shape[:dim], length, shape[dim] // length, *shape[dim + 1 :])
    return jnp.moveaxis(parts, dim, 0)


def laid_out(parts, dim):
    shape = list(parts.shape[1:])
    shape[dim] *= parts.shape[0]
    return jnp.moveaxis(parts, 0, dim).reshape(shape)


def one_exchange(value, axis, axes, splits, concats):
    sizes = [lax.axis_size(a) for a in axes]
    parts = split_up(value, splits[0], sizes[0])
    parts = jnp.moveaxis(split_up(parts, splits[1] + 1, sizes[1]), 0, 1)
    inside = parts.shape[2:]
    parts = parts.reshape(-1, *inside)
    parts = lax.all_to_all(parts, axis, split_axis=0, concat_axis=0, tiled=True)
    parts = laid_out(parts.reshape(*sizes, *inside), concats[0] + 1)
    return laid_out(parts, concats[1])


def sent_to_all(value, axis):
    copies = jnp.broadcast_to(value, (lax.axis_size(axis), *value.shape))
    return lax.all_to_all(copies, axis, split_axis=0, concat_axis=0, tiled=True)


def collect(value, axis, dim):
    parts = sent_to_all(value, axis)
    return laid_out(parts, dim)


def stable_lse(scores, reduce_axis):
    highest = jnp.max(scores, axis=reduce_axis, keepdims=True)
    summed = jnp.sum(jnp.exp(scores - highest), axis=reduce_axis)
    return jnp.squeeze(highest, reduce_axis) + jnp.log(summed)


def make_scoring(centre_table, centre_norms, inverse_root):

    def scoring(package):
        slot_rows, slot_flags = package
        leading = slot_rows.shape[0]
        flat_rows = slot_rows.reshape(leading, -1, slot_rows.shape[-1])
        products = jnp.einsum(
            "lsd,lmd->lsm", flat_rows, centre_table, preferred_element_type=jnp.float32
        )
        scores = inverse_root * (2.0 * products - centre_norms[:, None, :])
        scores = scores.reshape(slot_rows.shape[:-1] + (centre_table.shape[1],))
        return (slot_rows, slot_flags, scores, stable_lse(scores, scores.ndim - 1))

    return scoring


def send_slots(package):
    return (
        one_exchange(package[0], ("pts", "cent"), ("pts", "cent"), (1, 2), (1, 2)),
        one_exchange(package[1], ("pts", "cent"), ("pts", "cent"), (1, 2), (1, 2)),
    )


def on_device(points, centroids, candidates):
    feature_width = points.shape[1]
    inverse_root = 1.0 / math.sqrt(feature_width)
    owners = lax.axis_size("pts")
    spread = lax.axis_size("cent")
    held_blocks = centroids.shape[0] // CB
    point_blocks = candidates.shape[0]
    total_blocks = held_blocks * owners
    capacity = max(2, 2 * point_blocks // total_blocks + 1)
    slot_count = held_blocks * owners * capacity
    grouped = points.reshape(point_blocks, PB, feature_width)
    picked = candidates.reshape(-1)
    entry_count = picked.shape[0]
    labels = jnp.arange(total_blocks, dtype=jnp.int32)
    member = (picked[:, None] == labels[None, :]).astype(jnp.bfloat16)
    entry_index = jnp.arange(entry_count, dtype=jnp.int32)
    earlier = (entry_index[None, :] < entry_index[:, None]).astype(jnp.bfloat16)
    prior_hits = jnp.dot(earlier, member, preferred_element_type=jnp.float32)
    arrival = jnp.sum(prior_hits * member.astype(jnp.float32), axis=1).astype(jnp.int32)
    owned = held_blocks // spread
    owner_device = picked // owned
    local_block = picked % owned
    position = (local_block * (owners * spread) + owner_device) * capacity + arrival
    slot_shape = (owned, owners, spread, capacity)
    first_owned = lax.axis_index("cent") * (owned * CB)
    current = lax.dynamic_slice_in_dim(centroids, first_owned, owned * CB, 0)
    places = jnp.arange(slot_count, dtype=jnp.int32)
    source = (
        jnp.sum(
            jnp.where(position[:, None] == places[None, :], entry_index[:, None] + 1, 0), axis=0
        )
        - 1
    )
    filled = source >= 0
    home_block = jnp.maximum(source, 0) // 2
    outgoing = jnp.where(filled[:, None, None], grouped[home_block], jnp.zeros((), jnp.bfloat16))
    outgoing = outgoing.reshape(slot_shape + (PB, feature_width))
    slot_marks = jnp.broadcast_to(filled[:, None], (slot_count, PB)).astype(jnp.bfloat16)
    slot_marks = slot_marks.reshape(slot_shape + (PB,))
    point_lse = jnp.zeros((point_blocks, PB), jnp.float32)
    arrived = outgoing
    arrived_marks = slot_marks
    for iteration in range(ITERS):
        centre_table = current.reshape(-1, CB, feature_width)
        centre_norms = jnp.sum(jnp.square(centre_table.astype(jnp.float32)), axis=2)
        scoring = make_scoring(centre_table, centre_norms, inverse_root)
        arrived, arrived_marks = send_slots((outgoing, slot_marks))
        arrived, arrived_marks, scores, partial_value = scoring((arrived, arrived_marks))
        returned = one_exchange(partial_value, ("pts", "cent"), ("pts", "cent"), (1, 2), (1, 2))
        per_entry = returned.reshape(slot_count, PB)[position]
        paired = per_entry.reshape(point_blocks, 2, PB)
        point_lse = stable_lse(paired, 1)
        outward = jnp.where(filled[:, None], point_lse[home_block], jnp.zeros((), jnp.float32))
        outward = outward.reshape(slot_shape + (PB,))
        inward = one_exchange(outward, ("pts", "cent"), ("pts", "cent"), (1, 2), (1, 2))
        weights = jnp.exp(scores - inward[..., None]) * arrived_marks.astype(jnp.float32)[..., None]
        leading = weights.shape[0]
        flat_weights = weights.reshape(leading, -1, CB)
        masses = jnp.sum(flat_weights, axis=1).reshape(leading * CB)
        rounded = flat_weights.astype(jnp.bfloat16)
        flat_rows = arrived.reshape(leading, -1, feature_width)
        weighted = jnp.einsum(
            "lsm,lsd->lmd", rounded, flat_rows, preferred_element_type=jnp.float32
        )
        weighted = weighted.reshape(leading * CB, feature_width)
        current = ((weighted + current.astype(jnp.float32)) / (masses[:, None] + 1.0)).astype(
            jnp.bfloat16
        )
    current = collect(current, "cent", 0)
    return (current, point_lse.reshape(-1))


def solution(mesh):
    return jax.shard_map(
        on_device,
        mesh=mesh,
        in_specs=(P(("pts", "cent"), None), P("pts", None), P(("pts", "cent"), None)),
        out_specs=(P("pts", None), P(("pts", "cent"))),
        check_vma=False,
    )
```

profile of v0, /device:TPU:1, one launch (start us, length us, event | category | flops | bytes accessed | tf_op | source)
XLA Modules:
  0.0 399.2 jit_solution(8623770165428468237)
XLA Ops:
  0.6 0.9 copy.13
  1.7 0.3 fusion.34
  2.2 0.2 ge.17
  2.4 13.2 %gather_fusion = bf16[512,16,512]{2,1,0:T(8,128)(2,1)} fusion(bf16[128,16,512]{2,1,0:T(8,128)(2,1)S(1)} %bitcast.78, s32[1024]{0:T(1024)S(1)} %pad_clamp_fusion.1), kind=kCustom, calls=%fused_computation | custom fusion | bytes 16779264 | tf_op jit(solution)/shard_map/gather | solution.py:110
  15.6 7.2 %broadcast_select_fusion = bf16[256,1,1,1,2,16,512]{6,5,4,3,2,1,0:T(8,128)(2,1)} fusion(bf16[256,1,1,1,2,16,512]{6,5,4,3,2,1,0:T(8,128)(2,1)} %bitcast.79, pred[256,2]{1,0:T(8,128)(4,1)S(1)} %ge.17), kind=kLoop, calls=%fused_computation.15 | loop fusion | flops 4194304 | bytes 16777728 | tf_op jit(solution)/shard_map/jit(_where)/select_n | solution.py:110
  22.8 16.6 %all-to-all-start = ((bf16[256,1,1,1,2,16,512]{6,5,4,3,2,1,0:T(8,128)(2,1)}), bf16[256,1,1,1,2,16,512]{6,5,4,3,2,1,0:T(8,128)(2,1)}, u32[]{:S(2)}, u32[]{:S(2)}) async-start(bf16[256,1,1,1,2,16,512]{6,5,4,3,2,1,0:T(8,128)(2,1)} %broadcast_select_fusion), calls=%async_computation | async-start | bytes 16777216 | tf_op jit(solution)/shard_map/all_to_all | solution.py:31
  39.8 1.1 fusion.35
  40.9 185.6 %all-to-all-done = bf16[256,1,1,1,2,16,512]{6,5,4,3,2,1,0:T(8,128)(2,1)} async-done(((bf16[256,1,1,1,2,16,512]{6,5,4,3,2,1,0:T(8,128)(2,1)}), bf16[256,1,1,1,2,16,512]{6,5,4,3,2,1,0:T(8,128)(2,1)}, u32[]{:S(2)}, u32[]{:S(2)}) %all-to-all-start) | async-done | bytes 8388640 | tf_op jit(solution)/shard_map/all_to_all | solution.py:31
  226.4 5.8 %fusion.42 = (f32[8192]{0:T(1024)S(1)}, f32[8192,256]{0,1:T(8,128)S(1)}) fusion(f32[256]{0:T(256)S(1)} %fusion.35, bf16[8192,512]{1,0:T(8,128)(2,1)} %bitcast.8, bf16[1024,512]{1,0:T(8,128)(2,1)} %param.4, s32[]{:T(128)S(6)} %select_n.96), kind=kOutput, calls=%fused_computation.69 | convolution fusion | flops 2155864064 | bytes 17073156 | tf_op jit(solution)/shard_map/lsd,lmd->lsm/dot_general | solution.py:58
  232.2 3.2 copy-done.1
  235.5 1.2 exponential_reduce_fusion.1
  236.7 1.1 add.161
  237.8 6.9 %all-to-all-start.1 = ((f32[256,1,1,1,2,16]{5,4,3,2,1,0:T(2,128)}), f32[256,1,1,1,2,16]{5,4,3,2,1,0:T(2,128)S(1)}, u32[]{:S(2)}, u32[]{:S(2)}) async-start(f32[256,1,1,1,2,16]{5,4,3,2,1,0:T(2,128)} %bitcast.13), calls=%async_computation.1 | async-start | bytes 524288 | tf_op jit(solution)/shard_map/all_to_all | solution.py:31
  244.7 15.2 %all-to-all-done.1 = f32[256,1,1,1,2,16]{5,4,3,2,1,0:T(2,128)S(1)} async-done(((f32[256,1,1,1,2,16]{5,4,3,2,1,0:T(2,128)}), f32[256,1,1,1,2,16]{5,4,3,2,1,0:T(2,128)S(1)}, u32[]{:S(2)}, u32[]{:S(2)}) %all-to-all-start.1) | async-done | bytes 32800 | tf_op jit(solution)/shard_map/all_to_all | solution.py:31
  259.9 1.0 broadcast_in_dim.50
  260.9 5.5 %all-to-all-start.3 = ((bf16[256,1,1,1,2,16]{5,4,3,2,1,0:T(2,128)(2,1)}), bf16[256,1,1,1,2,16]{5,4,3,2,1,0:T(2,128)(2,1)S(1)}, u32[]{:S(2)}, u32[]{:S(2)}) async-start(bf16[256,1,1,1,2,16]{5,4,3,2,1,0:T(2,128)(2,1)} %broadcast_in_dim.50), calls=%async_computation.3 | async-start | bytes 262144 | tf_op jit(solution)/shard_map/all_to_all | solution.py:31
  266.4 0.7 gather_fusion.1
  267.2 0.2 reduce_max.37
  267.3 0.2 exponential_reduce_fusion.3
  267.6 1.0 gather_fusion.2
  268.6 1.0 broadcast_select_fusion.2
  269.7 9.7 %all-to-all-done.3 = bf16[256,1,1,1,2,16]{5,4,3,2,1,0:T(2,128)(2,1)S(1)} async-done(((bf16[256,1,1,1,2,16]{5,4,3,2,1,0:T(2,128)(2,1)}), bf16[256,1,1,1,2,16]{5,4,3,2,1,0:T(2,128)(2,1)S(1)}, u32[]{:S(2)}, u32[]{:S(2)}) %all-to-all-start.3) | async-done | bytes 16416 | tf_op jit(solution)/shard_map/all_to_all | solution.py:31
  279.3 5.7 %all-to-all-start.2 = ((f32[256,1,1,1,2,16]{5,4,3,2,1,0:T(2,128)}), f32[256,1,1,1,2,16]{5,4,3,2,1,0:T(2,128)S(1)}, u32[]{:S(2)}, u32[]{:S(2)}) async-start(f32[256,1,1,1,2,16]{5,4,3,2,1,0:T(2,128)} %broadcast_select_fusion.2), calls=%async_computation.2 | async-start | bytes 524288 | tf_op jit(solution)/shard_map/all_to_all | solution.py:31
  285.1 15.2 %all-to-all-done.2 = f32[256,1,1,1,2,16]{5,4,3,2,1,0:T(2,128)S(1)} async-done(((f32[256,1,1,1,2,16]{5,4,3,2,1,0:T(2,128)}), f32[256,1,1,1,2,16]{5,4,3,2,1,0:T(2,128)S(1)}, u32[]{:S(2)}, u32[]{:S(2)}) %all-to-all-start.2) | async-done | bytes 32800 | tf_op jit(solution)/shard_map/all_to_all | solution.py:31
  300.4 0.3 sub.114
  300.7 5.1 %fusion.4 = f32[256]{0:T(256)S(1)} fusion(f32[8192,256]{0,1:T(8,128)} %copy-done.1, f32[8192]{0:T(1024)S(1)} %reshape.484, f32[8192]{0:T(1024)S(1)} %sub.114), kind=kLoop, calls=%fused_computation.16 | loop fusion | flops 6291200 | bytes 8455168 | tf_op jit(solution)/shard_map/reduce_sum | solution.py:133
  305.7 0.7 copy-done.2
  306.4 6.0 %fusion.36 = (f32[256]{0:T(256)S(1)}, bf16[256,512]{1,0:T(8,128)(2,1)S(1)}) fusion(f32[256]{0:T(256)S(1)} %broadcast_add_fusion.1, bf16[1024,512]{1,0:T(8,128)(2,1)} %param.4, s32[]{:T(128)S(6)} %select_n.96, bf16[8192,512]{1,0:T(8,128)(2,1)} %bitcast.8, f32[8192,256]{0,1:T(8,128)S(1)} %copy-done.2, f32[8192]{0:T(1024)S(1)} %reshape.484, f32[8192]{0:T(1024)S(1)} %sub.114), kind=kOutput, calls=%fused_computation.37 | convolution fusion | flops 2154692352 | bytes 17369092 | tf_op jit(solution)/shard_map/lsm,lsd->lmd/dot_general | solution.py:136
  312.4 5.8 %fusion.43 = (f32[8192]{0:T(1024)S(1)}, f32[8192,256]{0,1:T(8,128)S(1)}) fusion(f32[256]{0:T(256)S(1)} %get-tuple-element.6, bf16[8192,512]{1,0:T(8,128)(2,1)} %bitcast.8, bf16[256,512]{1,0:T(8,128)(2,1)S(1)} %get-tuple-element.7), kind=kOutput, calls=%fused_computation.70 | convolution fusion | flops 2155864064 | bytes 17073152 | tf_op jit(solution)/shard_map/lsd,lmd->lsm/dot_general | solution.py:58
  318.2 3.2 copy-done.3
  321.4 1.2 exponential_reduce_fusion
  322.7 0.4 add.168
  323.1 20.7 %all_to_all.37 = f32[256,1,1,1,2,16]{5,4,3,2,1,0:T(2,128)S(1)} all-to-all(f32[256,1,1,1,2,16]{5,4,3,2,1,0:T(2,128)S(1)} %bitcast.88), channel_id=1, replica_groups=mesh['pts'=64,'cent'=4] {'pts','cent'}, dimensions={0} | all-to-all | bytes 65536 | tf_op jit(solution)/shard_map/all_to_all | solution.py:31
  343.7 0.7 gather_fusion.3
  344.5 0.2 reduce_max.39
  344.6 0.2 exponential_reduce_fusion.2
  344.9 1.0 gather_fusion.4
  345.9 0.3 broadcast_select_fusion.1
  346.3 20.6 %all_to_all.38 = f32[256,1,1,1,2,16]{5,4,3,2,1,0:T(2,128)S(1)} all-to-all(f32[256,1,1,1,2,16]{5,4,3,2,1,0:T(2,128)S(1)} %broadcast_select_fusion.1), channel_id=1, replica_groups=mesh['pts'=64,'cent'=4] {'pts','cent'}, dimensions={0} | all-to-all | bytes 65536 | tf_op jit(solution)/shard_map/all_to_all | solution.py:31
  366.9 0.3 sub.123
  367.2 5.1 %fusion.6 = f32[256]{0:T(256)S(1)} fusion(f32[8192,256]{0,1:T(8,128)} %copy-done.3, f32[8192]{0:T(1024)S(1)} %sub.123, f32[8192]{0:T(1024)S(1)} %reshape.484), kind=kLoop, calls=%fused_computation.18 | loop fusion | flops 6291200 | bytes 8455168 | tf_op jit(solution)/shard_map/reduce_sum | solution.py:133
  372.3 0.7 copy-done.4
  373.0 5.9 %fusion.25 = bf16[256,512]{1,0:T(8,128)(2,1)S(1)} fusion(bf16[8192,512]{1,0:T(8,128)(2,1)} %bitcast.8, f32[8192,256]{0,1:T(8,128)S(1)} %copy-done.4, f32[8192]{0:T(1024)S(1)} %sub.123, f32[8192]{0:T(1024)S(1)} %reshape.484, bf16[256,512]{1,0:T(8,128)(2,1)S(1)} %get-tuple-element.7, f32[256]{0:T(256)S(1)} %broadcast_add_fusion), kind=kOutput, calls=%fused_computation.29 | convolution fusion | flops 2154299392 | bytes 17368064 | tf_op jit(solution)/shard_map/lsm,lsd->lmd/dot_general | solution.py:136
  378.9 1.1 broadcast_in_dim.78
  379.9 3.5 all-to-all-start.6
  383.5 0.7 add.172
  384.1 14.1 %all-to-all-done.6 = bf16[4,256,512]{2,1,0:T(8,128)(2,1)S(1)} async-done(((bf16[4,256,512]{2,1,0:T(8,128)(2,1)}), bf16[4,256,512]{2,1,0:T(8,128)(2,1)S(1)}, u32[]{:S(2)}, u32[]{:S(2)}) %all-to-all-start.6) | async-done | bytes 1048608 | tf_op jit(solution)/shard_map/all_to_all | solution.py:38
  398.2 1.0 copy.20
  (29 shorter events, 0.8 us)
Async XLA Ops:
  0.6 1.8 copy-start
  22.8 16.7 %copy-start.5 = (s32[128,2]{0,1:T(2,128)S(1)}, s32[128,2]{0,1:T(2,128)}, u32[]{:S(2)}) copy-start(s32[128,2]{0,1:T(2,128)} %param.5) | copy-start | bytes 3076
  22.8 203.6 %all-to-all-start = ((bf16[256,1,1,1,2,16,512]{6,5,4,3,2,1,0:T(8,128)(2,1)}), bf16[256,1,1,1,2,16,512]{6,5,4,3,2,1,0:T(8,128)(2,1)}, u32[]{:S(2)}, u32[]{:S(2)}) async-start(bf16[256,1,1,1,2,16,512]{6,5,4,3,2,1,0:T(8,128)(2,1)} %broadcast_select_fusion), calls=%async_computation | async-start | bytes 16777216 | tf_op jit(solution)/shard_map/all_to_all | solution.py:31
  232.2 3.2 copy-start.1
  237.8 22.1 %all-to-all-start.1 = ((f32[256,1,1,1,2,16]{5,4,3,2,1,0:T(2,128)}), f32[256,1,1,1,2,16]{5,4,3,2,1,0:T(2,128)S(1)}, u32[]{:S(2)}, u32[]{:S(2)}) async-start(f32[256,1,1,1,2,16]{5,4,3,2,1,0:T(2,128)} %bitcast.13), calls=%async_computation.1 | async-start | bytes 524288 | tf_op jit(solution)/shard_map/all_to_all | solution.py:31
  260.9 18.4 %all-to-all-start.3 = ((bf16[256,1,1,1,2,16]{5,4,3,2,1,0:T(2,128)(2,1)}), bf16[256,1,1,1,2,16]{5,4,3,2,1,0:T(2,128)(2,1)S(1)}, u32[]{:S(2)}, u32[]{:S(2)}) async-start(bf16[256,1,1,1,2,16]{5,4,3,2,1,0:T(2,128)(2,1)} %broadcast_in_dim.50), calls=%async_computation.3 | async-start | bytes 262144 | tf_op jit(solution)/shard_map/all_to_all | solution.py:31
  279.3 21.0 %all-to-all-start.2 = ((f32[256,1,1,1,2,16]{5,4,3,2,1,0:T(2,128)}), f32[256,1,1,1,2,16]{5,4,3,2,1,0:T(2,128)S(1)}, u32[]{:S(2)}, u32[]{:S(2)}) async-start(f32[256,1,1,1,2,16]{5,4,3,2,1,0:T(2,128)} %broadcast_select_fusion.2), calls=%async_computation.2 | async-start | bytes 524288 | tf_op jit(solution)/shard_map/all_to_all | solution.py:31
  300.7 5.8 %copy-start.2 = (f32[8192,256]{0,1:T(8,128)S(1)}, f32[8192,256]{0,1:T(8,128)}, u32[]{:S(2)}) copy-start(f32[8192,256]{0,1:T(8,128)} %copy-done.1) | copy-start | bytes 25165828
  318.2 3.2 copy-start.3
  367.2 5.8 %copy-start.4 = (f32[8192,256]{0,1:T(8,128)S(1)}, f32[8192,256]{0,1:T(8,128)}, u32[]{:S(2)}) copy-start(f32[8192,256]{0,1:T(8,128)} %copy-done.3) | copy-start | bytes 25165828
  379.9 18.3 %all-to-all-start.6 = ((bf16[4,256,512]{2,1,0:T(8,128)(2,1)}), bf16[4,256,512]{2,1,0:T(8,128)(2,1)S(1)}, u32[]{:S(2)}, u32[]{:S(2)}) async-start(bf16[4,256,512]{2,1,0:T(8,128)(2,1)} %broadcast_in_dim.78), calls=%async_computation.6 | async-start | bytes 2097152 | tf_op jit(solution)/shard_map/all_to_all | solution.py:38
where the time goes:
time: 400 us; the launch traced here: 399 us
  waiting for transfers between devices  240 us (60%)
  blocking collectives  41.3 us (10%)
  starting transfers between devices  38.2 us (10%)
  local copies, waits for them, and re-layouts  32 us (8%)
  matrix products  23.8 us (6%)
  other arithmetic  23.3 us (6%)
    all_to_all x4, waiting for transfers between devices, one_exchange(): parts = lax.all_to_all(parts, axis, split_axis=0, concat_axis=0, tiled=True)  226 us
    all_to_all x2, blocking collectives, one_exchange(): parts = lax.all_to_all(parts, axis, split_axis=0, concat_axis=0, tiled=True)  41.3 us
    all_to_all x4, starting transfers between devices, one_exchange(): parts = lax.all_to_all(parts, axis, split_axis=0, concat_axis=0, tiled=True)  34.7 us
    all_to_all x1, waiting for transfers between devices, sent_to_all(): return lax.all_to_all(copies, axis, split_axis=0, concat_axis=0, tiled=True)  14.1 us
    gather x1, local copies, waits for them, and re-layouts, on_device(): grouped[home_block]  13.2 us
    dot_general x2, matrix products, on_device(): jnp.einsum('lsm,lsd->lmd', rounded, flat_rows, preferred_element_type=jnp...  11.9 us
    dot_general x2, matrix products, scoring(): jnp.einsum('lsd,lmd->lsm', flat_rows, centre_table, preferred_element_typ...  11.6 us
    reduce_sum x2, other arithmetic, on_device(): masses = jnp.sum(flat_weights, axis=1).reshape(leading * CB)  10.1 us
  transfers between devices with their start and end apart: 5, of which 5 were waited for; matrix products, arithmetic and copies ran while one was open for 1% of the time, Pallas kernels for 0%

commit v1 on v0

v1 whole, which is shorter than its diff:
```python
import functools
import math

import jax
import jax.numpy as jnp
from jax import lax
from jax.experimental import pallas as pl
from jax.experimental.pallas import tpu as pltpu
from jax.sharding import Mesh, PartitionSpec as P

D = 512
CB = 256
PB = 16
PBD = 128
NCB = 256
ITERS = 2
CAP = 2
COPIES = 4
PEERS = NCB // COPIES
LANES = COPIES * CAP * PB
SLOTS = PEERS * COPIES * CAP
ENTRIES = 2 * PBD
STEP = 16
COLS = STEP * CAP * PB
MSG = CB + 16
EMPTY = 1e30
GROUP = ("zl", "y", "core", "x")
BETA = 1.0 / math.sqrt(D)
F32 = jnp.float32
BF16 = jnp.bfloat16


def exact_dot(a, b):
    return jnp.dot(a, b, precision=lax.Precision.HIGHEST, preferred_element_type=F32)


def iota(shape, dim):
    return lax.broadcasted_iota(jnp.int32, shape, dim)


def pack_kernel(src, points, out):
    base = pl.program_id(0) * out.shape[0]

    def body(i, carry):
        s = src[base + i]
        block = points[jnp.maximum(s, 0)]
        out[i] = jnp.where(s >= 0, block, jnp.zeros_like(block))
        return carry

    lax.fori_loop(0, out.shape[0], body, 0, unroll=8)


def pack(src, points):
    per = 64
    return pl.pallas_call(
        pack_kernel,
        grid_spec=pltpu.PrefetchScalarGridSpec(
            num_scalar_prefetch=1,
            grid=(SLOTS // per,),
            in_specs=[pl.BlockSpec((PBD, PB, D), lambda i, s: (0, 0, 0))],
            out_specs=pl.BlockSpec((per, PB, D), lambda i, s: (i, 0, 0)),
        ),
        out_shape=jax.ShapeDtypeStruct((SLOTS, PB, D), BF16),
        compiler_params=pltpu.CompilerParams(vmem_limit_bytes=16 << 20),
        name="pack_points",
    )(src, points)


def rows_of(rows, label):
    part = rows[:, pl.ds(pl.multiple_of(label * (CAP * PB), CAP * PB), CAP * PB), :]
    return part.reshape(COLS, D)


def norms_of(table):
    wide = table[...].astype(F32)
    return jnp.sum(wide * wide, axis=1, keepdims=True)


def scores_of(table, block, norms):
    products = lax.dot_general(table[...], block, (((1,), (1,)), ((), ())), preferred_element_type=F32)
    return BETA * (2.0 * products - norms)


def label_of(me, s):
    return lax.rem(me + 1 + s, COPIES)


def score_kernel(me, rows, c0, c1, c2, c3, out, norms):
    tables = (c0, c1, c2, c3)

    @pl.when(pl.program_id(0) == 0)
    def _():
        for s in range(COPIES):
            norms[s] = jnp.broadcast_to(norms_of(tables[s]), (CB, 128))

    own = iota((STEP, COLS), 1) // (CAP * PB) == iota((STEP, COLS), 0)
    fold_from, fold_to = iota((COLS, LANES), 0), iota((COLS, LANES), 1)
    total = jnp.zeros((STEP, LANES), F32)
    for s in range(COPIES):
        label = label_of(me[0], s)
        scores = scores_of(tables[s], rows_of(rows, label), norms[s][:, :1])
        highest = jnp.max(scores, axis=0, keepdims=True)
        partial = highest + jnp.log(jnp.sum(jnp.exp(scores - highest), axis=0, keepdims=True))
        fold = fold_from % (CAP * PB) + label * (CAP * PB) == fold_to
        total += exact_dot(jnp.where(own, partial, 0.0), fold.astype(F32))
    out[...] = total


def table_specs():
    return [pl.BlockSpec((CB, D), lambda i, s: (0, 0))] * COPIES


def row_spec():
    return pl.BlockSpec((STEP, LANES, D), lambda i, s: (i, 0, 0))


def score(me, rows, tables):
    return pl.pallas_call(
        score_kernel,
        grid_spec=pltpu.PrefetchScalarGridSpec(
            num_scalar_prefetch=1,
            grid=(PEERS // STEP,),
            in_specs=[row_spec(), *table_specs()],
            out_specs=pl.BlockSpec((STEP, LANES), lambda i, s: (i, 0)),
            scratch_shapes=[pltpu.VMEM((COPIES, CB, 128), F32)],
        ),
        out_shape=jax.ShapeDtypeStruct((PEERS, LANES), F32),
        compiler_params=pltpu.CompilerParams(vmem_limit_bytes=40 << 20),
        name="score_blocks",
    )(me, rows, *tables)


def home_kernel(returned, peer_col, slot_col, peer_row, lse, outward):
    pick = (iota((ENTRIES, PEERS), 1) == peer_col[...]).astype(F32)
    mask = (iota((ENTRIES, LANES), 1) // PB == slot_col[...]).astype(F32)
    fold = (iota((LANES, LANES), 0) % PB == iota((LANES, LANES), 1) % PB).astype(F32)
    mine = exact_dot(exact_dot(pick, returned[...]) * mask, fold)
    first, second = mine[:PBD], mine[PBD:]
    highest = jnp.maximum(first, second)
    total = highest + jnp.log(jnp.exp(first - highest) + jnp.exp(second - highest))
    lse[...] = total
    place = (iota((PEERS, ENTRIES), 0) == peer_row[...]).astype(F32)
    filled = jnp.dot(place.astype(BF16), mask.astype(BF16), preferred_element_type=F32)
    both = jnp.concatenate([total, total], axis=0)
    outward[...] = jnp.where(filled > 0.5, exact_dot(place, both * mask), EMPTY)


def home(returned, peer_col, slot_col, peer_row):
    return pl.pallas_call(
        home_kernel,
        out_shape=(
            jax.ShapeDtypeStruct((PBD, LANES), F32),
            jax.ShapeDtypeStruct((PEERS, LANES), F32),
        ),
        name="join_halves",
    )(returned, peer_col, slot_col, peer_row)


def weigh_kernel(me, rows, c0, c1, c2, c3, inward, message, own_sum, own_mass, norms, sums, masses):
    tables = (c0, c1, c2, c3)

    @pl.when(pl.program_id(0) == 0)
    def _():
        for s in range(COPIES):
            norms[s] = jnp.broadcast_to(norms_of(tables[s]), (CB, 128))
        sums[...] = jnp.zeros_like(sums)
        masses[...] = jnp.zeros_like(masses)

    own = iota((STEP, COLS), 1) // (CAP * PB) == iota((STEP, COLS), 0)
    spread_from, spread_to = iota((LANES, COLS), 0), iota((LANES, COLS), 1)
    for s in range(COPIES):
        label = label_of(me[0], s)
        block = rows_of(rows, label)
        spread = spread_to % (CAP * PB) + label * (CAP * PB) == spread_from
        point_lse = exact_dot(inward[...], spread.astype(F32))
        point_lse = jnp.sum(jnp.where(own, point_lse, 0.0), axis=0, keepdims=True)
        weights = jnp.exp(scores_of(tables[s], block, norms[s][:, :1]) - point_lse)
        sums[s] += jnp.dot(weights.astype(BF16), block, preferred_element_type=F32)
        mass = weights[:, :128]
        for k in range(1, COLS // 128):
            mass += weights[:, k * 128 : (k + 1) * 128]
        masses[s] += mass

    @pl.when(pl.program_id(0) == pl.num_programs(0) - 1)
    def _():
        for s in range(COPIES):
            mass = jnp.sum(masses[s].T, axis=0, keepdims=True)
            if s == COPIES - 1:
                own_sum[...] = sums[s]
                own_mass[...] = jnp.broadcast_to(mass, own_mass.shape)
            else:
                message[s, :CB] = sums[s].astype(BF16)
                coarse = mass.astype(BF16)
                fine = (mass - coarse.astype(F32)).astype(BF16)
                pair = jnp.concatenate([coarse.astype(F32), fine.astype(F32)], axis=1)
                message[s, CB:] = jnp.broadcast_to(pair, (MSG - CB, D)).astype(BF16)


def weigh(me, rows, tables, inward):
    whole = lambda *shape: pl.BlockSpec(shape, lambda i, s: (0,) * len(shape))
    return pl.pallas_call(
        weigh_kernel,
        grid_spec=pltpu.PrefetchScalarGridSpec(
            num_scalar_prefetch=1,
            grid=(PEERS // STEP,),
            in_specs=[row_spec(), *table_specs(), pl.BlockSpec((STEP, LANES), lambda i, s: (i, 0))],
            out_specs=[whole(COPIES - 1, MSG, D), whole(CB, D), whole(8, CB)],
            scratch_shapes=[
                pltpu.VMEM((COPIES, CB, 128), F32),
                pltpu.VMEM((COPIES, CB, D), F32),
                pltpu.VMEM((COPIES, CB, 128), F32),
            ],
        ),
        out_shape=(
            jax.ShapeDtypeStruct((COPIES - 1, MSG, D), BF16),
            jax.ShapeDtypeStruct((CB, D), F32),
            jax.ShapeDtypeStruct((8, CB), F32),
        ),
        compiler_params=pltpu.CompilerParams(vmem_limit_bytes=40 << 20),
        name="weigh_points",
    )(me, rows, *tables, inward)


def finish_kernel(own_sum, own_mass, m0, m1, m2, table, out):
    total, mass = own_sum[...], own_mass[:1]
    for message in (m0, m1, m2):
        total += message[:CB].astype(F32)
        pair = message[CB:].astype(F32)[:1]
        mass += pair[:, :CB] + pair[:, CB:]
    column = jnp.broadcast_to(mass + 1.0, (128, CB)).T[:, :1]
    fresh = ((total + table[...].astype(F32)) / column).astype(BF16)
    out[...] = jnp.broadcast_to(fresh, out.shape)


def finish(own_sum, own_mass, arrived, table, copies):
    return pl.pallas_call(
        finish_kernel,
        out_shape=jax.ShapeDtypeStruct((*copies, CB, D), BF16),
        compiler_params=pltpu.CompilerParams(vmem_limit_bytes=16 << 20),
        name="new_centres",
    )(own_sum, own_mass, *arrived, table)


def shifted(value, by):
    return lax.ppermute(value, "zh", [(i, (i + by) % COPIES) for i in range(COPIES)])


def tables_of(own):
    return [shifted(own, COPIES - 1 - s) for s in range(COPIES - 1)] + [own]


def exchange(value):
    return lax.all_to_all(value, GROUP, split_axis=0, concat_axis=0, tiled=True)


def route(candidates):
    picked = candidates.T.reshape(-1)
    labels = jnp.arange(NCB, dtype=jnp.int32)
    member = (picked[:, None] == labels[None, :]).astype(BF16)
    index = jnp.arange(ENTRIES, dtype=jnp.int32)
    earlier = (index[None, :] < index[:, None]).astype(BF16)
    hits = jnp.dot(earlier, member, preferred_element_type=F32)
    arrival = jnp.sum(hits * member.astype(F32), axis=1).astype(jnp.int32)
    peer = picked % PEERS
    slot = picked // PEERS * CAP + arrival
    position = peer * (COPIES * CAP) + slot
    places = jnp.arange(SLOTS, dtype=jnp.int32)
    source = jnp.sum(jnp.where(position[:, None] == places[None, :], index[:, None] % PBD + 1, 0), axis=0) - 1
    return source, peer, slot


def on_device(points, centroids, candidates):
    me = lax.axis_index("zh").reshape(1)
    own = lax.dynamic_slice_in_dim(centroids, lax.axis_index("x") * CB, CB, 0)
    source, peer, slot = route(candidates)
    outgoing = pack(source, points.reshape(PBD, PB, D))
    tables = tables_of(own)
    rows = exchange(outgoing.reshape(PEERS, LANES, D))
    for iteration in range(ITERS):
        returned = exchange(score(me, rows, tables))
        lse, outward = home(returned, peer[:, None], slot[:, None], peer[None, :])
        message, own_sum, own_mass = weigh(me, rows, tables, exchange(outward))
        arrived = [shifted(message[n - 1], n) for n in range(1, COPIES)]
        last = iteration == ITERS - 1
        own = finish(own_sum, own_mass, arrived, own, (COPIES,) if last else ())
        if not last:
            tables = tables_of(own)
    gathered = lax.all_to_all(own, "x", split_axis=0, concat_axis=0, tiled=True)
    return gathered.reshape(COPIES * CB, D), lse[:, :PB].reshape(-1)


def solution(mesh):
    split = Mesh(mesh.devices.reshape(4, 2, 4, 2, 4), ("zh", "zl", "y", "core", "x"))
    pts = ("zh", "zl", "y", "core")
    return jax.shard_map(
        on_device,
        mesh=split,
        in_specs=(P((*pts, "x"), None), P(pts, None), P((*pts, "x"), None)),
        out_specs=(P(pts, None), P((*pts, "x"))),
        check_vma=False,
    )
```

time: 400 us -> 370 us (0.925)
  Pallas kernels: 0 us -> 56 us
  waiting for transfers between devices: 240 us -> 215 us
  local copies, waits for them, and re-layouts: 32 us -> 7.49 us
  matrix products: 23.8 us -> 1.04 us
  other arithmetic: 23.3 us -> 2.25 us
  starting transfers between devices: 38.2 us -> 46.5 us
    all_to_all x5 -> x3, waiting for transfers between devices: 240 us -> 21.5 us  [the longest x1 14 us: on_device(): gathered = lax.all_to_all(own, 'x', split_axis=0, concat_axis=0, tiled=True)]
    ppermute x0 -> x12, waiting for transfers between devices: none -> 194 us  [shifted(): lax.ppermute(value, 'zh', [(i, (i + by) % COPIES) for i in range(COPIES)])]
    pallas_call x0 -> x9, Pallas kernels: none -> 56 us  [the longest x2 25.4 us: weigh(): pl.pallas_call(weigh_kernel, grid_spec=pltpu.PrefetchScalarGridSpec(num_s...]
    ppermute x0 -> x12, starting transfers between devices: none -> 27.4 us  [shifted(): lax.ppermute(value, 'zh', [(i, (i + by) % COPIES) for i in range(COPIES)])]
    dot_general x5 -> x1, matrix products: 23.8 us -> 1.04 us  [route(): hits = jnp.dot(earlier, member, preferred_element_type=F32)]
    all_to_all x5 -> x3, starting transfers between devices: 38.2 us -> 19.1 us  [the longest x2 15.6 us: exchange(): return lax.all_to_all(value, GROUP, split_axis=0, concat_axis=0, tiled=True)]
    gather x5 -> x0, local copies, waits for them, and re-layouts: 16.8 us -> none  [the longest x1 13.2 us: on_device(): grouped[home_block]]
    reduce_sum x8 -> x1, other arithmetic: 14.2 us -> 0.15 us  [route(): jnp.sum(jnp.where(position[:, None] == places[None, :], index[:, None] %...]
  transfers between devices with their start and end apart: 5 -> 15, of which waited for: 5 -> 14; matrix products, arithmetic and copies ran while one was open for 1% -> 1% of each run, Pallas kernels for 0% -> 0%
where the time goes in v1:
time: 370 us
  waiting for transfers between devices  215 us (58%)
  Pallas kernels  56 us (15%)
  starting transfers between devices  46.5 us (13%)
  blocking collectives  40.2 us (11%)
  local copies, waits for them, and re-layouts  7.49 us (2%)
    ppermute x12, waiting for transfers between devices, shifted(): lax.ppermute(value, 'zh', [(i, (i + by) % COPIES) for i in range(COPIES)])  194 us
    all_to_all x3, blocking collectives, exchange(): return lax.all_to_all(value, GROUP, split_axis=0, concat_axis=0, tiled=True)  40.2 us
    ppermute x12, starting transfers between devices, shifted(): lax.ppermute(value, 'zh', [(i, (i + by) % COPIES) for i in range(COPIES)])  27.4 us
    pallas_call x2, Pallas kernels, weigh(): pl.pallas_call(weigh_kernel, grid_spec=pltpu.PrefetchScalarGridSpec(num_s...  25.4 us
    pallas_call x2, Pallas kernels, score(): pl.pallas_call(score_kernel, grid_spec=pltpu.PrefetchScalarGridSpec(num_s...  21.7 us
    all_to_all x2, starting transfers between devices, exchange(): return lax.all_to_all(value, GROUP, split_axis=0, concat_axis=0, tiled=True)  15.6 us
    all_to_all x1, waiting for transfers between devices, on_device(): gathered = lax.all_to_all(own, 'x', split_axis=0, concat_axis=0, tiled=True)  14 us
    all_to_all x2, waiting for transfers between devices, exchange(): return lax.all_to_all(value, GROUP, split_axis=0, concat_axis=0, tiled=True)  7.55 us
  transfers between devices with their start and end apart: 15, of which 14 were waited for; matrix products, arithmetic and copies ran while one was open for 1% of the time, Pallas kernels for 0%

profile of v1, /device:TPU:1, one launch (start us, length us, event | category | flops | bytes accessed | tf_op | source)
XLA Modules:
  0.0 369.7 jit_solution(17208048902209306580)
XLA Ops:
  0.6 1.0 fusion
  1.7 0.7 fusion.8
  2.6 1.6 copy-done.2
  4.1 2.4 pack_points.1
  6.5 3.2 copy-done.1
  9.8 10.7 %all-to-all-start = ((bf16[64,128,512]{2,1,0:T(8,128)(2,1)}), bf16[64,128,512]{2,1,0:T(8,128)(2,1)}, u32[]{:S(2)}, u32[]{:S(2)}) async-start(bf16[64,128,512]{2,1,0:T(8,128)(2,1)} %bitcast.42), calls=%async_computation | async-start | bytes 16777216 | tf_op jit(solution)/shard_map/all_to_all | solution.py:253
  20.5 5.2 %collective-permute-start = (bf16[256,512]{1,0:T(8,128)(2,1)S(1)}, bf16[256,512]{1,0:T(8,128)(2,1)S(1)}, u32[]{:S(2)}, u32[]{:S(2)}) collective-permute-start(bf16[256,512]{1,0:T(8,128)(2,1)S(1)} %constant_dynamic-slice_fusion.c3.table), channel_id=1, source_target_pairs={{0,192},{64,0},{128,64},{192,128},{1,193},{65,1},{129,65},{193,129... | collective-permute-start | bytes 786440 | tf_op jit(solution)/shard_map/ppermute | solution.py:245
  25.7 1.2 collective-permute-start.1
  26.8 2.1 collective-permute-start.2
  29.2 0.8 fusion.3
  30.1 0.8 collective-permute-done.c0
  30.9 121.0 %collective-permute-done.1.c1 = bf16[256,512]{1,0:T(8,128)(2,1)S(1)} collective-permute-done((bf16[256,512]{1,0:T(8,128)(2,1)S(1)}, bf16[256,512]{1,0:T(8,128)(2,1)S(1)}, u32[]{:S(2)}, u32[]{:S(2)}) %collective-permute-start.1) | collective-permute-done | bytes 262176 | tf_op jit(solution)/shard_map/ppermute | solution.py:245
  151.9 3.0 collective-permute-done.2.c2
  154.9 11.2 %score_blocks.2 = f32[64,128]{1,0:T(8,128)} custom-call(s32[1]{0:T(128)} %bitcast.me, bf16[64,128,512]{2,1,0:T(8,128)(2,1)} %all-to-all-done.rows, bf16[256,512]{1,0:T(8,128)(2,1)S(1)} %collective-permute-done.c0, bf16[256,512]{1,0:T(8,128)(2,1)S(1)} %collective-permute-done.1.c1, bf16[256,512]{1,0:T(8,128)(2,1)S(1)} %collective-permute-done.2.c2, ...), custom_call_target="tpu_custom_call" | custom-call | tf_op jit(solution)/shard_map/score_blocks/pallas_call | solution.py:118
  166.0 5.0 %all-to-all-start.1 = ((f32[64,1,128]{2,1,0:T(1,128)}), f32[64,1,128]{2,1,0:T(1,128)S(1)}, u32[]{:S(2)}, u32[]{:S(2)}) async-start(f32[64,1,128]{2,1,0:T(1,128)} %bitcast.7), calls=%async_computation.1 | async-start | bytes 65536 | tf_op jit(solution)/shard_map/all_to_all | solution.py:253
  171.0 0.6 and_select_fusion.peer_row
  171.6 7.5 %all-to-all-done.1 = f32[64,1,128]{2,1,0:T(1,128)S(1)} async-done(((f32[64,1,128]{2,1,0:T(1,128)}), f32[64,1,128]{2,1,0:T(1,128)S(1)}, u32[]{:S(2)}, u32[]{:S(2)}) %all-to-all-start.1) | async-done | bytes 32800 | tf_op jit(solution)/shard_map/all_to_all | solution.py:253
  179.1 0.6 copy-done.3
  179.7 2.5 join_halves.2
  182.3 12.7 %all_to_all.54 = f32[64,1,128]{2,1,0:T(1,128)S(1)} all-to-all(f32[64,1,128]{2,1,0:T(1,128)} %bitcast.52), channel_id=1, replica_groups=mesh['zh'=4,'zl'=2,'y'=4,'core'=2,'x'=4] {'zl','y','core','x'}, dimensions={0} | all-to-all | bytes 65536 | tf_op jit(solution)/shard_map/all_to_all | solution.py:253
  195.0 12.7 %weigh_points.2 = (bf16[3,272,512]{2,1,0:T(8,128)(2,1)S(1)}, f32[256,512]{1,0:T(8,128)S(1)}, f32[8,256]{1,0:T(8,128)S(1)}) custom-call(s32[1]{0:T(128)} %bitcast.me, bf16[64,128,512]{2,1,0:T(8,128)(2,1)} %all-to-all-done.rows, bf16[256,512]{1,0:T(8,128)(2,1)S(1)} %collective-permute-done.c0, bf16[256,512]{1,0:T(8,128)(2,1)S(1)} %collective-permute-done.1.c1, ...), custom_call_target="tpu_custom_call" | custom-call | tf_op jit(solution)/shard_map/weigh_points/pallas_call | solution.py:201
  207.8 3.7 collective-permute-start.3
  211.4 1.4 collective-permute-start.4
  212.8 2.2 collective-permute-start.5
  215.0 9.3 %collective-permute-done.3.m0 = bf16[272,512]{1,0:T(8,128)(2,1)S(1)} collective-permute-done((bf16[272,512]{1,0:T(8,128)(2,1)S(1)}, bf16[272,512]{1,0:T(8,128)(2,1)S(1)}, u32[]{:S(2)}, u32[]{:S(2)}) %collective-permute-start.3) | collective-permute-done | bytes 278560 | tf_op jit(solution)/shard_map/ppermute | solution.py:245
  224.3 11.9 %collective-permute-done.4.m1 = bf16[272,512]{1,0:T(8,128)(2,1)S(1)} collective-permute-done((bf16[272,512]{1,0:T(8,128)(2,1)S(1)}, bf16[272,512]{1,0:T(8,128)(2,1)S(1)}, u32[]{:S(2)}, u32[]{:S(2)}) %collective-permute-start.4) | collective-permute-done | bytes 278560 | tf_op jit(solution)/shard_map/ppermute | solution.py:245
  236.2 2.2 collective-permute-done.5.m2
  238.4 0.2 new_centres.2.c3.table
  238.7 2.9 collective-permute-start.6
  241.6 4.0 %collective-permute-start.7 = (bf16[256,512]{1,0:T(8,128)(2,1)S(1)}, bf16[256,512]{1,0:T(8,128)(2,1)S(1)}, u32[]{:S(2)}, u32[]{:S(2)}) collective-permute-start(bf16[256,512]{1,0:T(8,128)(2,1)S(1)} %new_centres.2.c3.table), channel_id=1, source_target_pairs={{0,128},{64,192},{128,0},{192,64},{1,129},{65,193},{129,1},{193,65... | collective-permute-start | bytes 786440 | tf_op jit(solution)/shard_map/ppermute | solution.py:245
  245.7 14.7 %collective-permute-done.6.c0 = bf16[256,512]{1,0:T(8,128)(2,1)S(1)} collective-permute-done((bf16[256,512]{1,0:T(8,128)(2,1)S(1)}, bf16[256,512]{1,0:T(8,128)(2,1)S(1)}, u32[]{:S(2)}, u32[]{:S(2)}) %collective-permute-start.6) | collective-permute-done | bytes 262176 | tf_op jit(solution)/shard_map/ppermute | solution.py:245
  260.3 0.7 collective-permute-done.7.c1
  261.0 4.7 %collective-permute-done.8.c2 = bf16[256,512]{1,0:T(8,128)(2,1)S(1)} collective-permute-done((bf16[256,512]{1,0:T(8,128)(2,1)S(1)}, bf16[256,512]{1,0:T(8,128)(2,1)S(1)}, u32[]{:S(2)}, u32[]{:S(2)}) %collective-permute-start.8) | collective-permute-done | bytes 262176 | tf_op jit(solution)/shard_map/ppermute | solution.py:245
  265.7 10.5 %score_blocks.3 = f32[64,128]{1,0:T(8,128)S(1)} custom-call(s32[1]{0:T(128)} %bitcast.me, bf16[64,128,512]{2,1,0:T(8,128)(2,1)} %all-to-all-done.rows, bf16[256,512]{1,0:T(8,128)(2,1)S(1)} %collective-permute-done.6.c0, bf16[256,512]{1,0:T(8,128)(2,1)S(1)} %collective-permute-done.7.c1, bf16[256,512]{1,0:T(8,128)(2,1)S(1)} %collective-permute-done.8.c2, ...), custom_call_target="tpu_custom_call" | custom-call | tf_op jit(solution)/shard_map/score_blocks/pallas_call | solution.py:118
  276.2 14.5 %all_to_all.55 = f32[64,1,128]{2,1,0:T(1,128)} all-to-all(f32[64,1,128]{2,1,0:T(1,128)S(1)} %bitcast.46), channel_id=1, replica_groups=mesh['zh'=4,'zl'=2,'y'=4,'core'=2,'x'=4] {'zl','y','core','x'}, dimensions={0} | all-to-all | bytes 65536 | tf_op jit(solution)/shard_map/all_to_all | solution.py:253
  290.7 2.5 join_halves.3
  293.2 13.0 %all_to_all.56 = f32[64,1,128]{2,1,0:T(1,128)S(1)} all-to-all(f32[64,1,128]{2,1,0:T(1,128)} %bitcast.51), channel_id=1, replica_groups=mesh['zh'=4,'zl'=2,'y'=4,'core'=2,'x'=4] {'zl','y','core','x'}, dimensions={0} | all-to-all | bytes 65536 | tf_op jit(solution)/shard_map/all_to_all | solution.py:253
  306.2 12.7 %weigh_points.3 = (bf16[3,272,512]{2,1,0:T(8,128)(2,1)S(1)}, f32[256,512]{1,0:T(8,128)S(1)}, f32[8,256]{1,0:T(8,128)S(1)}) custom-call(s32[1]{0:T(128)} %bitcast.me, bf16[64,128,512]{2,1,0:T(8,128)(2,1)} %all-to-all-done.rows, bf16[256,512]{1,0:T(8,128)(2,1)S(1)} %collective-permute-done.6.c0, bf16[256,512]{1,0:T(8,128)(2,1)S(1)} %collective-permute-done.7.c1, ...), custom_call_target="tpu_custom_call" | custom-call | tf_op jit(solution)/shard_map/weigh_points/pallas_call | solution.py:201
  319.1 1.7 collective-permute-start.10
  320.8 2.9 collective-permute-start.11
  323.7 13.0 %collective-permute-done.9.m0 = bf16[272,512]{1,0:T(8,128)(2,1)S(1)} collective-permute-done((bf16[272,512]{1,0:T(8,128)(2,1)S(1)}, bf16[272,512]{1,0:T(8,128)(2,1)S(1)}, u32[]{:S(2)}, u32[]{:S(2)}) %collective-permute-start.9) | collective-permute-done | bytes 278560 | tf_op jit(solution)/shard_map/ppermute | solution.py:245
  336.7 3.3 collective-permute-done.10.m1
  340.0 9.3 %collective-permute-done.11.m2 = bf16[272,512]{1,0:T(8,128)(2,1)S(1)} collective-permute-done((bf16[272,512]{1,0:T(8,128)(2,1)S(1)}, bf16[272,512]{1,0:T(8,128)(2,1)S(1)}, u32[]{:S(2)}, u32[]{:S(2)}) %collective-permute-start.11) | collective-permute-done | bytes 278560 | tf_op jit(solution)/shard_map/ppermute | solution.py:245
  349.3 1.2 new_centres.3
  350.5 3.5 all-to-all-start.5
  354.1 0.7 reshape.246
  354.8 14.0 %all-to-all-done.5 = bf16[4,256,512]{2,1,0:T(8,128)(2,1)S(1)} async-done(((bf16[4,256,512]{2,1,0:T(8,128)(2,1)}), bf16[4,256,512]{2,1,0:T(8,128)(2,1)S(1)}, u32[]{:S(2)}, u32[]{:S(2)}) %all-to-all-start.5) | async-done | bytes 1048608 | tf_op jit(solution)/shard_map/all_to_all | solution.py:288
  368.7 1.0 copy.29
  (20 shorter events, 0.7 us)
Async XLA Ops:
  0.6 19.8 %copy-start = (bf16[1024,512]{1,0:T(8,128)(2,1)S(1)}, bf16[1024,512]{1,0:T(8,128)(2,1)}, u32[]{:S(2)}) copy-start(bf16[1024,512]{1,0:T(8,128)(2,1)} %param.4) | copy-start | bytes 3145732
  2.5 1.6 copy-start.2
  6.5 3.2 copy-start.1
  9.8 19.3 %copy-start.5 = (s32[128,2]{0,1:T(2,128)S(1)}, s32[128,2]{0,1:T(2,128)}, u32[]{:S(2)}) copy-start(s32[128,2]{0,1:T(2,128)} %param.5) | copy-start | bytes 3076
  9.8 145.1 %all-to-all-start = ((bf16[64,128,512]{2,1,0:T(8,128)(2,1)}), bf16[64,128,512]{2,1,0:T(8,128)(2,1)}, u32[]{:S(2)}, u32[]{:S(2)}) async-start(bf16[64,128,512]{2,1,0:T(8,128)(2,1)} %bitcast.42), calls=%async_computation | async-start | bytes 16777216 | tf_op jit(solution)/shard_map/all_to_all | solution.py:253
  20.5 10.4 %collective-permute-start = (bf16[256,512]{1,0:T(8,128)(2,1)S(1)}, bf16[256,512]{1,0:T(8,128)(2,1)S(1)}, u32[]{:S(2)}, u32[]{:S(2)}) collective-permute-start(bf16[256,512]{1,0:T(8,128)(2,1)S(1)} %constant_dynamic-slice_fusion.c3.table), channel_id=1, source_target_pairs={{0,192},{64,0},{128,64},{192,128},{1,193},{65,1},{129,65},{193,129... | collective-permute-start | bytes 786440 | tf_op jit(solution)/shard_map/ppermute | solution.py:245
  25.7 126.2 %collective-permute-start.1 = (bf16[256,512]{1,0:T(8,128)(2,1)S(1)}, bf16[256,512]{1,0:T(8,128)(2,1)S(1)}, u32[]{:S(2)}, u32[]{:S(2)}) collective-permute-start(bf16[256,512]{1,0:T(8,128)(2,1)S(1)} %constant_dynamic-slice_fusion.c3.table), channel_id=1, source_target_pairs={{0,128},{64,192},{128,0},{192,64},{1,129},{65,193},{129,1},{193,65... | collective-permute-start | bytes 786440 | tf_op jit(solution)/shard_map/ppermute | solution.py:245
  26.8 128.0 %collective-permute-start.2 = (bf16[256,512]{1,0:T(8,128)(2,1)S(1)}, bf16[256,512]{1,0:T(8,128)(2,1)S(1)}, u32[]{:S(2)}, u32[]{:S(2)}) collective-permute-start(bf16[256,512]{1,0:T(8,128)(2,1)S(1)} %constant_dynamic-slice_fusion.c3.table), channel_id=1, source_target_pairs={{0,64},{64,128},{128,192},{192,0},{1,65},{65,129},{129,193},{193,1... | collective-permute-start | bytes 786440 | tf_op jit(solution)/shard_map/ppermute | solution.py:245
  166.0 13.1 %all-to-all-start.1 = ((f32[64,1,128]{2,1,0:T(1,128)}), f32[64,1,128]{2,1,0:T(1,128)S(1)}, u32[]{:S(2)}, u32[]{:S(2)}) async-start(f32[64,1,128]{2,1,0:T(1,128)} %bitcast.7), calls=%async_computation.1 | async-start | bytes 65536 | tf_op jit(solution)/shard_map/all_to_all | solution.py:253
  179.1 0.6 copy-start.3
  207.8 16.5 %collective-permute-start.3 = (bf16[272,512]{1,0:T(8,128)(2,1)S(1)}, bf16[272,512]{1,0:T(8,128)(2,1)S(1)}, u32[]{:S(2)}, u32[]{:S(2)}) collective-permute-start(bf16[272,512]{1,0:T(8,128)(2,1)S(1)} %get-tuple-element.25), channel_id=1, source_target_pairs={{0,64},{64,128},{128,192},{192,0},{1,65},{65,129},{129,193},{193,1... | collective-permute-start | bytes 835592 | tf_op jit(solution)/shard_map/ppermute | solution.py:245
  211.4 24.8 %collective-permute-start.4 = (bf16[272,512]{1,0:T(8,128)(2,1)S(1)}, bf16[272,512]{1,0:T(8,128)(2,1)S(1)}, u32[]{:S(2)}, u32[]{:S(2)}) collective-permute-start(bf16[272,512]{1,0:T(8,128)(2,1)S(1)} %get-tuple-element.24), channel_id=1, source_target_pairs={{0,128},{64,192},{128,0},{192,64},{1,129},{65,193},{129,1},{193,65... | collective-permute-start | bytes 835592 | tf_op jit(solution)/shard_map/ppermute | solution.py:245
  212.8 25.6 %collective-permute-start.5 = (bf16[272,512]{1,0:T(8,128)(2,1)S(1)}, bf16[272,512]{1,0:T(8,128)(2,1)S(1)}, u32[]{:S(2)}, u32[]{:S(2)}) collective-permute-start(bf16[272,512]{1,0:T(8,128)(2,1)S(1)} %get-tuple-element.23), channel_id=1, source_target_pairs={{0,192},{64,0},{128,64},{192,128},{1,193},{65,1},{129,65},{193,129... | collective-permute-start | bytes 835592 | tf_op jit(solution)/shard_map/ppermute | solution.py:245
  238.7 21.6 %collective-permute-start.6 = (bf16[256,512]{1,0:T(8,128)(2,1)S(1)}, bf16[256,512]{1,0:T(8,128)(2,1)S(1)}, u32[]{:S(2)}, u32[]{:S(2)}) collective-permute-start(bf16[256,512]{1,0:T(8,128)(2,1)S(1)} %new_centres.2.c3.table), channel_id=1, source_target_pairs={{0,192},{64,0},{128,64},{192,128},{1,193},{65,1},{129,65},{193,129... | collective-permute-start | bytes 786440 | tf_op jit(solution)/shard_map/ppermute | solution.py:245
  241.6 19.4 %collective-permute-start.7 = (bf16[256,512]{1,0:T(8,128)(2,1)S(1)}, bf16[256,512]{1,0:T(8,128)(2,1)S(1)}, u32[]{:S(2)}, u32[]{:S(2)}) collective-permute-start(bf16[256,512]{1,0:T(8,128)(2,1)S(1)} %new_centres.2.c3.table), channel_id=1, source_target_pairs={{0,128},{64,192},{128,0},{192,64},{1,129},{65,193},{129,1},{193,65... | collective-permute-start | bytes 786440 | tf_op jit(solution)/shard_map/ppermute | solution.py:245
  245.7 20.0 %collective-permute-start.8 = (bf16[256,512]{1,0:T(8,128)(2,1)S(1)}, bf16[256,512]{1,0:T(8,128)(2,1)S(1)}, u32[]{:S(2)}, u32[]{:S(2)}) collective-permute-start(bf16[256,512]{1,0:T(8,128)(2,1)S(1)} %new_centres.2.c3.table), channel_id=1, source_target_pairs={{0,64},{64,128},{128,192},{192,0},{1,65},{65,129},{129,193},{193,1... | collective-permute-start | bytes 786440 | tf_op jit(solution)/shard_map/ppermute | solution.py:245
  293.2 60.8 %copy-start.4 = (f32[128,128]{1,0:T(8,128)S(1)}, f32[128,128]{1,0:T(8,128)}, u32[]{:S(2)}) copy-start(f32[128,128]{1,0:T(8,128)} %get-tuple-element.19) | copy-start | bytes 196612
  319.0 17.7 %collective-permute-start.9 = (bf16[272,512]{1,0:T(8,128)(2,1)S(1)}, bf16[272,512]{1,0:T(8,128)(2,1)S(1)}, u32[]{:S(2)}, u32[]{:S(2)}) collective-permute-start(bf16[272,512]{1,0:T(8,128)(2,1)S(1)} %get-tuple-element.22), channel_id=1, source_target_pairs={{0,64},{64,128},{128,192},{192,0},{1,65},{65,129},{129,193},{193,1... | collective-permute-start | bytes 835592 | tf_op jit(solution)/shard_map/ppermute | solution.py:245
  319.1 21.0 %collective-permute-start.10 = (bf16[272,512]{1,0:T(8,128)(2,1)S(1)}, bf16[272,512]{1,0:T(8,128)(2,1)S(1)}, u32[]{:S(2)}, u32[]{:S(2)}) collective-permute-start(bf16[272,512]{1,0:T(8,128)(2,1)S(1)} %get-tuple-element.21), channel_id=1, source_target_pairs={{0,128},{64,192},{128,0},{192,64},{1,129},{65,193},{129,1},{193,65... | collective-permute-start | bytes 835592 | tf_op jit(solution)/shard_map/ppermute | solution.py:245
  320.8 28.5 %collective-permute-start.11 = (bf16[272,512]{1,0:T(8,128)(2,1)S(1)}, bf16[272,512]{1,0:T(8,128)(2,1)S(1)}, u32[]{:S(2)}, u32[]{:S(2)}) collective-permute-start(bf16[272,512]{1,0:T(8,128)(2,1)S(1)} %get-tuple-element.20), channel_id=1, source_target_pairs={{0,192},{64,0},{128,64},{192,128},{1,193},{65,1},{129,65},{193,129... | collective-permute-start | bytes 835592 | tf_op jit(solution)/shard_map/ppermute | solution.py:245
  350.5 18.2 %all-to-all-start.5 = ((bf16[4,256,512]{2,1,0:T(8,128)(2,1)}), bf16[4,256,512]{2,1,0:T(8,128)(2,1)S(1)}, u32[]{:S(2)}, u32[]{:S(2)}) async-start(bf16[4,256,512]{2,1,0:T(8,128)(2,1)} %new_centres.3), calls=%async_computation.5 | async-start | bytes 2097152 | tf_op jit(solution)/shard_map/all_to_all | solution.py:288

commit v2 on v1

--- a/solution.py
+++ b/solution.py
@@ -20,12 +20,14 @@
 LANES = COPIES * CAP * PB
 SLOTS = PEERS * COPIES * CAP
 ENTRIES = 2 * PBD
-STEP = 16
+STEP = 64
 COLS = STEP * CAP * PB
 MSG = CB + 16
 EMPTY = 1e30
 GROUP = ("zl", "y", "core", "x")
 BETA = 1.0 / math.sqrt(D)
+LOG2E = 1.0 / math.log(2.0)
+LN2 = math.log(2.0)
 F32 = jnp.float32
 BF16 = jnp.bfloat16
 
@@ -51,7 +53,7 @@
 
 
 def pack(src, points):
-    per = 64
+    per = 128
     return pl.pallas_call(
         pack_kernel,
         grid_spec=pltpu.PrefetchScalarGridSpec(
@@ -61,7 +63,7 @@
             out_specs=pl.BlockSpec((per, PB, D), lambda i, s: (i, 0, 0)),
         ),
         out_shape=jax.ShapeDtypeStruct((SLOTS, PB, D), BF16),
-        compiler_params=pltpu.CompilerParams(vmem_limit_bytes=16 << 20),
+        compiler_params=pltpu.CompilerParams(vmem_limit_bytes=20 << 20),
         name="pack_points",
     )(src, points)
 
@@ -73,12 +75,21 @@
 
 def norms_of(table):
     wide = table[...].astype(F32)
-    return jnp.sum(wide * wide, axis=1, keepdims=True)
+    return (BETA * LOG2E) * jnp.sum(wide * wide, axis=1, keepdims=True)
 
 
 def scores_of(table, block, norms):
     products = lax.dot_general(table[...], block, (((1,), (1,)), ((), ())), preferred_element_type=F32)
-    return BETA * (2.0 * products - norms)
+    return (2.0 * BETA * LOG2E) * products - norms
+
+
+def turned_by(value, groups, per_row):
+    row = iota(value.shape, 0) % COPIES
+    turned = value
+    for k in range(COPIES):
+        turn = lax.rem(groups + per_row * k + 2 * COPIES, COPIES) * (CAP * PB)
+        turned = jnp.where(row == k, pltpu.roll(value, turn, 1), turned)
+    return turned
 
 
 def label_of(me, s):
@@ -93,16 +104,16 @@
         for s in range(COPIES):
             norms[s] = jnp.broadcast_to(norms_of(tables[s]), (CB, 128))
 
-    own = iota((STEP, COLS), 1) // (CAP * PB) == iota((STEP, COLS), 0)
-    fold_from, fold_to = iota((COLS, LANES), 0), iota((COLS, LANES), 1)
+    lanes = iota((STEP, LANES), 1) // (CAP * PB)
     total = jnp.zeros((STEP, LANES), F32)
     for s in range(COPIES):
         label = label_of(me[0], s)
         scores = scores_of(tables[s], rows_of(rows, label), norms[s][:, :1])
         highest = jnp.max(scores, axis=0, keepdims=True)
-        partial = highest + jnp.log(jnp.sum(jnp.exp(scores - highest), axis=0, keepdims=True))
-        fold = fold_from % (CAP * PB) + label * (CAP * PB) == fold_to
-        total += exact_dot(jnp.where(own, partial, 0.0), fold.astype(F32))
+        partial = highest + jnp.log2(jnp.sum(jnp.exp2(scores - highest), axis=0, keepdims=True))
+        partial = partial * LN2
+        tiles = [jnp.broadcast_to(partial[:, k : k + LANES], (COPIES, LANES)) for k in range(0, COLS, LANES)]
+        total = jnp.where(lanes == label, turned_by(jnp.concatenate(tiles, axis=0), label, -1), total)
     out[...] = total
 
 
@@ -166,15 +177,15 @@
         sums[...] = jnp.zeros_like(sums)
         masses[...] = jnp.zeros_like(masses)
 
-    own = iota((STEP, COLS), 1) // (CAP * PB) == iota((STEP, COLS), 0)
-    spread_from, spread_to = iota((LANES, COLS), 0), iota((LANES, COLS), 1)
+    mine = iota((STEP, LANES), 1) // (CAP * PB) == iota((STEP, LANES), 0) % COPIES
+    incoming = inward[...] * LOG2E
     for s in range(COPIES):
         label = label_of(me[0], s)
         block = rows_of(rows, label)
-        spread = spread_to % (CAP * PB) + label * (CAP * PB) == spread_from
-        point_lse = exact_dot(inward[...], spread.astype(F32))
-        point_lse = jnp.sum(jnp.where(own, point_lse, 0.0), axis=0, keepdims=True)
-        weights = jnp.exp(scores_of(tables[s], block, norms[s][:, :1]) - point_lse)
+        turned = jnp.where(mine, turned_by(incoming, -label, 1), 0.0)
+        tiles = [jnp.sum(turned[k : k + COPIES], axis=0, keepdims=True) for k in range(0, STEP, COPIES)]
+        point_lse = jnp.concatenate(tiles, axis=1)
+        weights = jnp.exp2(scores_of(tables[s], block, norms[s][:, :1]) - point_lse)
         sums[s] += jnp.dot(weights.astype(BF16), block, preferred_element_type=F32)
         mass = weights[:, :128]
         for k in range(1, COLS // 128):
@@ -274,7 +285,7 @@
     own = lax.dynamic_slice_in_dim(centroids, lax.axis_index("x") * CB, CB, 0)
     source, peer, slot = route(candidates)
     outgoing = pack(source, points.reshape(PBD, PB, D))
-    tables = tables_of(own)
+    outgoing, *tables = lax.optimization_barrier((outgoing, *tables_of(own)))
     rows = exchange(outgoing.reshape(PEERS, LANES, D))
     for iteration in range(ITERS):
         returned = exchange(score(me, rows, tables))

time: 370 us -> 348 us (0.941)
  Pallas kernels: 56 us -> 38 us
  waiting for transfers between devices: 215 us -> 199 us
  starting transfers between devices: 46.5 us -> 57.9 us
    ppermute x12, waiting for transfers between devices: 194 us -> 72.2 us  [shifted(): lax.ppermute(value, 'zh', [(i, (i + by) % COPIES) for i in range(COPIES)])]
    all_to_all x2, waiting for transfers between devices: 7.55 us -> 113 us  [exchange(): return lax.all_to_all(value, GROUP, split_axis=0, concat_axis=0, tiled=True)]
    pallas_call x2, Pallas kernels: 25.4 us -> 16.4 us  [weigh(): pl.pallas_call(weigh_kernel, grid_spec=pltpu.PrefetchScalarGridSpec(num_s...]
    pallas_call x2, Pallas kernels: 21.7 us -> 12.8 us  [score(): pl.pallas_call(score_kernel, grid_spec=pltpu.PrefetchScalarGridSpec(num_s...]
    all_to_all x2, starting transfers between devices: 15.6 us -> 23.4 us  [exchange(): return lax.all_to_all(value, GROUP, split_axis=0, concat_axis=0, tiled=True)]
  transfers between devices with their start and end apart: 15 -> 15, of which waited for: 14 -> 13; matrix products, arithmetic and copies ran while one was open for 1% -> 1% of each run, Pallas kernels for 0% -> 1%
where the time goes in v2:
time: 348 us
  waiting for transfers between devices  199 us (57%)
  starting transfers between devices  57.9 us (17%)
  blocking collectives  40 us (11%)
  Pallas kernels  38 us (11%)
  local copies, waits for them, and re-layouts  8.69 us (2%)
    all_to_all x2, waiting for transfers between devices, exchange(): return lax.all_to_all(value, GROUP, split_axis=0, concat_axis=0, tiled=True)  113 us
    ppermute x12, waiting for transfers between devices, shifted(): lax.ppermute(value, 'zh', [(i, (i + by) % COPIES) for i in range(COPIES)])  72.2 us
    all_to_all x3, blocking collectives, exchange(): return lax.all_to_all(value, GROUP, split_axis=0, concat_axis=0, tiled=True)  40 us
    ppermute x12, starting transfers between devices, shifted(): lax.ppermute(value, 'zh', [(i, (i + by) % COPIES) for i in range(COPIES)])  30.9 us
    all_to_all x2, starting transfers between devices, exchange(): return lax.all_to_all(value, GROUP, split_axis=0, concat_axis=0, tiled=True)  23.4 us
    pallas_call x2, Pallas kernels, weigh(): pl.pallas_call(weigh_kernel, grid_spec=pltpu.PrefetchScalarGridSpec(num_s...  16.4 us
    all_to_all x1, waiting for transfers between devices, on_device(): gathered = lax.all_to_all(own, 'x', split_axis=0, concat_axis=0, tiled=True)  14 us
    pallas_call x2, Pallas kernels, score(): pl.pallas_call(score_kernel, grid_spec=pltpu.PrefetchScalarGridSpec(num_s...  12.8 us
  transfers between devices with their start and end apart: 15, of which 13 were waited for; matrix products, arithmetic and copies ran while one was open for 1% of the time, Pallas kernels for 1%

profile of v2, /device:TPU:1, one launch (start us, length us, event | category | flops | bytes accessed | tf_op | source)
XLA Modules:
  0.0 347.7 jit_solution(16098263593565790710)
XLA Ops:
  0.6 1.2 copy-done
  1.9 6.9 %collective-permute-start = (bf16[256,512]{1,0:T(8,128)(2,1)S(1)}, bf16[256,512]{1,0:T(8,128)(2,1)S(1)}, u32[]{:S(2)}, u32[]{:S(2)}) collective-permute-start(bf16[256,512]{1,0:T(8,128)(2,1)S(1)} %constant_dynamic-slice_fusion.c3.table), channel_id=1, source_target_pairs={{0,192},{64,0},{128,64},{192,128},{1,193},{65,1},{129,65},{193,129... | collective-permute-start | bytes 786440 | tf_op jit(solution)/shard_map/ppermute | solution.py:256
  8.8 1.0 collective-permute-start.1
  9.8 2.3 collective-permute-start.2
  12.1 1.0 fusion
  13.1 0.7 fusion.8
  13.9 1.6 copy-done.2
  15.5 2.3 pack_points.1
  17.9 3.2 copy-done.1
  21.1 4.2 %collective-permute-done.1.c1 = bf16[256,512]{1,0:T(8,128)(2,1)S(1)} collective-permute-done((bf16[256,512]{1,0:T(8,128)(2,1)S(1)}, bf16[256,512]{1,0:T(8,128)(2,1)S(1)}, u32[]{:S(2)}, u32[]{:S(2)}) %collective-permute-start.1) | collective-permute-done | bytes 262176 | tf_op jit(solution)/shard_map/ppermute | solution.py:256
  25.3 2.8 collective-permute-done.2.c2
  28.1 14.8 %all-to-all-start = ((bf16[64,128,512]{2,1,0:T(8,128)(2,1)}), bf16[64,128,512]{2,1,0:T(8,128)(2,1)}, u32[]{:S(2)}, u32[]{:S(2)}) async-start(bf16[64,128,512]{2,1,0:T(8,128)(2,1)} %bitcast.42), calls=%async_computation | async-start | bytes 16777216 | tf_op jit(solution)/shard_map/all_to_all | solution.py:264
  43.2 0.8 fusion.3
  44.0 105.4 %all-to-all-done.rows = bf16[64,128,512]{2,1,0:T(8,128)(2,1)} async-done(((bf16[64,128,512]{2,1,0:T(8,128)(2,1)}), bf16[64,128,512]{2,1,0:T(8,128)(2,1)}, u32[]{:S(2)}, u32[]{:S(2)}) %all-to-all-start) | async-done | bytes 8388640 | tf_op jit(solution)/shard_map/all_to_all | solution.py:264
  149.4 6.7 %score_blocks.2 = f32[64,128]{1,0:T(8,128)} custom-call(s32[1]{0:T(128)} %bitcast.me, bf16[64,128,512]{2,1,0:T(8,128)(2,1)} %all-to-all-done.rows, bf16[256,512]{1,0:T(8,128)(2,1)S(1)} %collective-permute-done.c0, bf16[256,512]{1,0:T(8,128)(2,1)S(1)} %collective-permute-done.1.c1, bf16[256,512]{1,0:T(8,128)(2,1)S(1)} %collective-permute-done.2.c2, ...), custom_call_target="tpu_custom_call" | custom-call | tf_op jit(solution)/shard_map/score_blocks/pallas_call | solution.py:129
  156.1 8.6 %all-to-all-start.1 = ((f32[64,1,128]{2,1,0:T(1,128)}), f32[64,1,128]{2,1,0:T(1,128)S(1)}, u32[]{:S(2)}, u32[]{:S(2)}) async-start(f32[64,1,128]{2,1,0:T(1,128)} %bitcast.7), calls=%async_computation.1 | async-start | bytes 65536 | tf_op jit(solution)/shard_map/all_to_all | solution.py:264
  165.3 7.5 %all-to-all-done.1 = f32[64,1,128]{2,1,0:T(1,128)S(1)} async-done(((f32[64,1,128]{2,1,0:T(1,128)}), f32[64,1,128]{2,1,0:T(1,128)S(1)}, u32[]{:S(2)}, u32[]{:S(2)}) %all-to-all-start.1) | async-done | bytes 32800 | tf_op jit(solution)/shard_map/all_to_all | solution.py:264
  172.8 0.6 copy-done.3
  173.4 2.5 join_halves.2
  175.9 12.8 %all_to_all.54 = f32[64,1,128]{2,1,0:T(1,128)S(1)} all-to-all(f32[64,1,128]{2,1,0:T(1,128)} %bitcast.52), channel_id=1, replica_groups=mesh['zh'=4,'zl'=2,'y'=4,'core'=2,'x'=4] {'zl','y','core','x'}, dimensions={0} | all-to-all | bytes 65536 | tf_op jit(solution)/shard_map/all_to_all | solution.py:264
  188.6 8.2 %weigh_points.2 = (bf16[3,272,512]{2,1,0:T(8,128)(2,1)S(1)}, f32[256,512]{1,0:T(8,128)S(1)}, f32[8,256]{1,0:T(8,128)S(1)}) custom-call(s32[1]{0:T(128)} %bitcast.me, bf16[64,128,512]{2,1,0:T(8,128)(2,1)} %all-to-all-done.rows, bf16[256,512]{1,0:T(8,128)(2,1)S(1)} %collective-permute-done.c0, bf16[256,512]{1,0:T(8,128)(2,1)S(1)} %collective-permute-done.1.c1, ...), custom_call_target="tpu_custom_call" | custom-call | tf_op jit(solution)/shard_map/weigh_points/pallas_call | solution.py:212
  196.9 2.3 collective-permute-start.3
  199.1 4.0 %collective-permute-start.4 = (bf16[272,512]{1,0:T(8,128)(2,1)S(1)}, bf16[272,512]{1,0:T(8,128)(2,1)S(1)}, u32[]{:S(2)}, u32[]{:S(2)}) collective-permute-start(bf16[272,512]{1,0:T(8,128)(2,1)S(1)} %get-tuple-element.34), channel_id=1, source_target_pairs={{0,128},{64,192},{128,0},{192,64},{1,129},{65,193},{129,1},{193,65... | collective-permute-start | bytes 835592 | tf_op jit(solution)/shard_map/ppermute | solution.py:256
  203.1 2.6 collective-permute-start.5
  205.8 7.9 %collective-permute-done.3.m0 = bf16[272,512]{1,0:T(8,128)(2,1)S(1)} collective-permute-done((bf16[272,512]{1,0:T(8,128)(2,1)S(1)}, bf16[272,512]{1,0:T(8,128)(2,1)S(1)}, u32[]{:S(2)}, u32[]{:S(2)}) %collective-permute-start.3) | collective-permute-done | bytes 278560 | tf_op jit(solution)/shard_map/ppermute | solution.py:256
  213.7 9.8 %collective-permute-done.4.m1 = bf16[272,512]{1,0:T(8,128)(2,1)S(1)} collective-permute-done((bf16[272,512]{1,0:T(8,128)(2,1)S(1)}, bf16[272,512]{1,0:T(8,128)(2,1)S(1)}, u32[]{:S(2)}, u32[]{:S(2)}) %collective-permute-start.4) | collective-permute-done | bytes 278560 | tf_op jit(solution)/shard_map/ppermute | solution.py:256
  223.5 4.7 %collective-permute-done.5.m2 = bf16[272,512]{1,0:T(8,128)(2,1)S(1)} collective-permute-done((bf16[272,512]{1,0:T(8,128)(2,1)S(1)}, bf16[272,512]{1,0:T(8,128)(2,1)S(1)}, u32[]{:S(2)}, u32[]{:S(2)}) %collective-permute-start.5) | collective-permute-done | bytes 278560 | tf_op jit(solution)/shard_map/ppermute | solution.py:256
  228.4 3.4 collective-permute-start.6
  231.8 1.6 collective-permute-start.7
  233.4 2.2 collective-permute-start.8
  235.5 14.8 %collective-permute-done.6.c0 = bf16[256,512]{1,0:T(8,128)(2,1)S(1)} collective-permute-done((bf16[256,512]{1,0:T(8,128)(2,1)S(1)}, bf16[256,512]{1,0:T(8,128)(2,1)S(1)}, u32[]{:S(2)}, u32[]{:S(2)}) %collective-permute-start.6) | collective-permute-done | bytes 262176 | tf_op jit(solution)/shard_map/ppermute | solution.py:256
  250.3 1.5 collective-permute-done.7.c1
  251.8 2.7 collective-permute-done.8.c2
  254.5 6.1 %score_blocks.3 = f32[64,128]{1,0:T(8,128)S(1)} custom-call(s32[1]{0:T(128)} %bitcast.me, bf16[64,128,512]{2,1,0:T(8,128)(2,1)} %all-to-all-done.rows, bf16[256,512]{1,0:T(8,128)(2,1)S(1)} %collective-permute-done.6.c0, bf16[256,512]{1,0:T(8,128)(2,1)S(1)} %collective-permute-done.7.c1, bf16[256,512]{1,0:T(8,128)(2,1)S(1)} %collective-permute-done.8.c2, ...), custom_call_target="tpu_custom_call" | custom-call | tf_op jit(solution)/shard_map/score_blocks/pallas_call | solution.py:129
  260.6 14.3 %all_to_all.55 = f32[64,1,128]{2,1,0:T(1,128)} all-to-all(f32[64,1,128]{2,1,0:T(1,128)S(1)} %bitcast.46), channel_id=1, replica_groups=mesh['zh'=4,'zl'=2,'y'=4,'core'=2,'x'=4] {'zl','y','core','x'}, dimensions={0} | all-to-all | bytes 65536 | tf_op jit(solution)/shard_map/all_to_all | solution.py:264
  274.9 2.5 join_halves.3
  277.4 13.0 %all_to_all.56 = f32[64,1,128]{2,1,0:T(1,128)S(1)} all-to-all(f32[64,1,128]{2,1,0:T(1,128)} %bitcast.51), channel_id=1, replica_groups=mesh['zh'=4,'zl'=2,'y'=4,'core'=2,'x'=4] {'zl','y','core','x'}, dimensions={0} | all-to-all | bytes 65536 | tf_op jit(solution)/shard_map/all_to_all | solution.py:264
  290.3 8.2 %weigh_points.3 = (bf16[3,272,512]{2,1,0:T(8,128)(2,1)S(1)}, f32[256,512]{1,0:T(8,128)S(1)}, f32[8,256]{1,0:T(8,128)S(1)}) custom-call(s32[1]{0:T(128)} %bitcast.me, bf16[64,128,512]{2,1,0:T(8,128)(2,1)} %all-to-all-done.rows, bf16[256,512]{1,0:T(8,128)(2,1)S(1)} %collective-permute-done.6.c0, bf16[256,512]{1,0:T(8,128)(2,1)S(1)} %collective-permute-done.7.c1, ...), custom_call_target="tpu_custom_call" | custom-call | tf_op jit(solution)/shard_map/weigh_points/pallas_call | solution.py:212
  298.6 2.4 collective-permute-start.10
  301.0 1.7 collective-permute-start.11
  302.7 0.6 collective-permute-start.9
  303.3 10.2 %collective-permute-done.10.m1 = bf16[272,512]{1,0:T(8,128)(2,1)S(1)} collective-permute-done((bf16[272,512]{1,0:T(8,128)(2,1)S(1)}, bf16[272,512]{1,0:T(8,128)(2,1)S(1)}, u32[]{:S(2)}, u32[]{:S(2)}) %collective-permute-start.10) | collective-permute-done | bytes 278560 | tf_op jit(solution)/shard_map/ppermute | solution.py:256
  313.5 13.8 %collective-permute-done.11.m2 = bf16[272,512]{1,0:T(8,128)(2,1)S(1)} collective-permute-done((bf16[272,512]{1,0:T(8,128)(2,1)S(1)}, bf16[272,512]{1,0:T(8,128)(2,1)S(1)}, u32[]{:S(2)}, u32[]{:S(2)}) %collective-permute-start.11) | collective-permute-done | bytes 278560 | tf_op jit(solution)/shard_map/ppermute | solution.py:256
  327.3 1.2 new_centres.3
  328.5 3.5 %all-to-all-start.5 = ((bf16[4,256,512]{2,1,0:T(8,128)(2,1)}), bf16[4,256,512]{2,1,0:T(8,128)(2,1)S(1)}, u32[]{:S(2)}, u32[]{:S(2)}) async-start(bf16[4,256,512]{2,1,0:T(8,128)(2,1)} %new_centres.3), calls=%async_computation.5 | async-start | bytes 2097152 | tf_op jit(solution)/shard_map/all_to_all | solution.py:299
  332.0 0.7 reshape.246
  332.7 14.0 %all-to-all-done.5 = bf16[4,256,512]{2,1,0:T(8,128)(2,1)S(1)} async-done(((bf16[4,256,512]{2,1,0:T(8,128)(2,1)}), bf16[4,256,512]{2,1,0:T(8,128)(2,1)S(1)}, u32[]{:S(2)}, u32[]{:S(2)}) %all-to-all-start.5) | async-done | bytes 1048608 | tf_op jit(solution)/shard_map/all_to_all | solution.py:299
  346.7 1.0 copy.29
  (20 shorter events, 1.4 us)
Async XLA Ops:
  0.6 1.2 copy-start
  1.9 19.2 %collective-permute-start = (bf16[256,512]{1,0:T(8,128)(2,1)S(1)}, bf16[256,512]{1,0:T(8,128)(2,1)S(1)}, u32[]{:S(2)}, u32[]{:S(2)}) collective-permute-start(bf16[256,512]{1,0:T(8,128)(2,1)S(1)} %constant_dynamic-slice_fusion.c3.table), channel_id=1, source_target_pairs={{0,192},{64,0},{128,64},{192,128},{1,193},{65,1},{129,65},{193,129... | collective-permute-start | bytes 786440 | tf_op jit(solution)/shard_map/ppermute | solution.py:256
  8.8 16.5 %collective-permute-start.1 = (bf16[256,512]{1,0:T(8,128)(2,1)S(1)}, bf16[256,512]{1,0:T(8,128)(2,1)S(1)}, u32[]{:S(2)}, u32[]{:S(2)}) collective-permute-start(bf16[256,512]{1,0:T(8,128)(2,1)S(1)} %constant_dynamic-slice_fusion.c3.table), channel_id=1, source_target_pairs={{0,128},{64,192},{128,0},{192,64},{1,129},{65,193},{129,1},{193,65... | collective-permute-start | bytes 786440 | tf_op jit(solution)/shard_map/ppermute | solution.py:256
  9.8 18.3 %collective-permute-start.2 = (bf16[256,512]{1,0:T(8,128)(2,1)S(1)}, bf16[256,512]{1,0:T(8,128)(2,1)S(1)}, u32[]{:S(2)}, u32[]{:S(2)}) collective-permute-start(bf16[256,512]{1,0:T(8,128)(2,1)S(1)} %constant_dynamic-slice_fusion.c3.table), channel_id=1, source_target_pairs={{0,64},{64,128},{128,192},{192,0},{1,65},{65,129},{129,193},{193,1... | collective-permute-start | bytes 786440 | tf_op jit(solution)/shard_map/ppermute | solution.py:256
  13.9 1.6 copy-start.2
  17.9 3.2 copy-start.1
  28.1 15.0 %copy-start.5 = (s32[128,2]{0,1:T(2,128)S(1)}, s32[128,2]{0,1:T(2,128)}, u32[]{:S(2)}) copy-start(s32[128,2]{0,1:T(2,128)} %param.5) | copy-start | bytes 3076
  28.1 121.3 %all-to-all-start = ((bf16[64,128,512]{2,1,0:T(8,128)(2,1)}), bf16[64,128,512]{2,1,0:T(8,128)(2,1)}, u32[]{:S(2)}, u32[]{:S(2)}) async-start(bf16[64,128,512]{2,1,0:T(8,128)(2,1)} %bitcast.42), calls=%async_computation | async-start | bytes 16777216 | tf_op jit(solution)/shard_map/all_to_all | solution.py:264
  156.1 16.7 %all-to-all-start.1 = ((f32[64,1,128]{2,1,0:T(1,128)}), f32[64,1,128]{2,1,0:T(1,128)S(1)}, u32[]{:S(2)}, u32[]{:S(2)}) async-start(f32[64,1,128]{2,1,0:T(1,128)} %bitcast.7), calls=%async_computation.1 | async-start | bytes 65536 | tf_op jit(solution)/shard_map/all_to_all | solution.py:264
  172.8 0.6 copy-start.3
  196.9 16.8 %collective-permute-start.3 = (bf16[272,512]{1,0:T(8,128)(2,1)S(1)}, bf16[272,512]{1,0:T(8,128)(2,1)S(1)}, u32[]{:S(2)}, u32[]{:S(2)}) collective-permute-start(bf16[272,512]{1,0:T(8,128)(2,1)S(1)} %get-tuple-element.35), channel_id=1, source_target_pairs={{0,64},{64,128},{128,192},{192,0},{1,65},{65,129},{129,193},{193,1... | collective-permute-start | bytes 835592 | tf_op jit(solution)/shard_map/ppermute | solution.py:256
  199.1 24.4 %collective-permute-start.4 = (bf16[272,512]{1,0:T(8,128)(2,1)S(1)}, bf16[272,512]{1,0:T(8,128)(2,1)S(1)}, u32[]{:S(2)}, u32[]{:S(2)}) collective-permute-start(bf16[272,512]{1,0:T(8,128)(2,1)S(1)} %get-tuple-element.34), channel_id=1, source_target_pairs={{0,128},{64,192},{128,0},{192,64},{1,129},{65,193},{129,1},{193,65... | collective-permute-start | bytes 835592 | tf_op jit(solution)/shard_map/ppermute | solution.py:256
  203.1 25.0 %collective-permute-start.5 = (bf16[272,512]{1,0:T(8,128)(2,1)S(1)}, bf16[272,512]{1,0:T(8,128)(2,1)S(1)}, u32[]{:S(2)}, u32[]{:S(2)}) collective-permute-start(bf16[272,512]{1,0:T(8,128)(2,1)S(1)} %get-tuple-element.33), channel_id=1, source_target_pairs={{0,192},{64,0},{128,64},{192,128},{1,193},{65,1},{129,65},{193,129... | collective-permute-start | bytes 835592 | tf_op jit(solution)/shard_map/ppermute | solution.py:256
  228.4 21.9 %collective-permute-start.6 = (bf16[256,512]{1,0:T(8,128)(2,1)S(1)}, bf16[256,512]{1,0:T(8,128)(2,1)S(1)}, u32[]{:S(2)}, u32[]{:S(2)}) collective-permute-start(bf16[256,512]{1,0:T(8,128)(2,1)S(1)} %new_centres.2.c3.table), channel_id=1, source_target_pairs={{0,192},{64,0},{128,64},{192,128},{1,193},{65,1},{129,65},{193,129... | collective-permute-start | bytes 786440 | tf_op jit(solution)/shard_map/ppermute | solution.py:256
  231.8 20.0 %collective-permute-start.7 = (bf16[256,512]{1,0:T(8,128)(2,1)S(1)}, bf16[256,512]{1,0:T(8,128)(2,1)S(1)}, u32[]{:S(2)}, u32[]{:S(2)}) collective-permute-start(bf16[256,512]{1,0:T(8,128)(2,1)S(1)} %new_centres.2.c3.table), channel_id=1, source_target_pairs={{0,128},{64,192},{128,0},{192,64},{1,129},{65,193},{129,1},{193,65... | collective-permute-start | bytes 786440 | tf_op jit(solution)/shard_map/ppermute | solution.py:256
  233.4 21.1 %collective-permute-start.8 = (bf16[256,512]{1,0:T(8,128)(2,1)S(1)}, bf16[256,512]{1,0:T(8,128)(2,1)S(1)}, u32[]{:S(2)}, u32[]{:S(2)}) collective-permute-start(bf16[256,512]{1,0:T(8,128)(2,1)S(1)} %new_centres.2.c3.table), channel_id=1, source_target_pairs={{0,64},{64,128},{128,192},{192,0},{1,65},{65,129},{129,193},{193,1... | collective-permute-start | bytes 786440 | tf_op jit(solution)/shard_map/ppermute | solution.py:256
  277.4 54.7 %copy-start.4 = (f32[128,128]{1,0:T(8,128)S(1)}, f32[128,128]{1,0:T(8,128)}, u32[]{:S(2)}) copy-start(f32[128,128]{1,0:T(8,128)} %get-tuple-element.29) | copy-start | bytes 196612
  298.6 14.9 %collective-permute-start.10 = (bf16[272,512]{1,0:T(8,128)(2,1)S(1)}, bf16[272,512]{1,0:T(8,128)(2,1)S(1)}, u32[]{:S(2)}, u32[]{:S(2)}) collective-permute-start(bf16[272,512]{1,0:T(8,128)(2,1)S(1)} %get-tuple-element.31), channel_id=1, source_target_pairs={{0,128},{64,192},{128,0},{192,64},{1,129},{65,193},{129,1},{193,65... | collective-permute-start | bytes 835592 | tf_op jit(solution)/shard_map/ppermute | solution.py:256
  301.0 26.3 %collective-permute-start.11 = (bf16[272,512]{1,0:T(8,128)(2,1)S(1)}, bf16[272,512]{1,0:T(8,128)(2,1)S(1)}, u32[]{:S(2)}, u32[]{:S(2)}) collective-permute-start(bf16[272,512]{1,0:T(8,128)(2,1)S(1)} %get-tuple-element.30), channel_id=1, source_target_pairs={{0,192},{64,0},{128,64},{192,128},{1,193},{65,1},{129,65},{193,129... | collective-permute-start | bytes 835592 | tf_op jit(solution)/shard_map/ppermute | solution.py:256
  302.7 24.6 %collective-permute-start.9 = (bf16[272,512]{1,0:T(8,128)(2,1)S(1)}, bf16[272,512]{1,0:T(8,128)(2,1)S(1)}, u32[]{:S(2)}, u32[]{:S(2)}) collective-permute-start(bf16[272,512]{1,0:T(8,128)(2,1)S(1)} %get-tuple-element.32), channel_id=1, source_target_pairs={{0,64},{64,128},{128,192},{192,0},{1,65},{65,129},{129,193},{193,1... | collective-permute-start | bytes 835592 | tf_op jit(solution)/shard_map/ppermute | solution.py:256
  328.5 18.2 %all-to-all-start.5 = ((bf16[4,256,512]{2,1,0:T(8,128)(2,1)}), bf16[4,256,512]{2,1,0:T(8,128)(2,1)S(1)}, u32[]{:S(2)}, u32[]{:S(2)}) async-start(bf16[4,256,512]{2,1,0:T(8,128)(2,1)} %new_centres.3), calls=%async_computation.5 | async-start | bytes 2097152 | tf_op jit(solution)/shard_map/all_to_all | solution.py:299

commit v3 on v2

v3 whole, which is shorter than its diff:
```python
import functools
import math

import jax
import jax.numpy as jnp
from jax import lax
from jax.experimental import pallas as pl
from jax.experimental.pallas import tpu as pltpu
from jax.sharding import Mesh, PartitionSpec as P

D = 512
CB = 256
PB = 16
PBD = 128
NCB = 256
ITERS = 2
CAP = 2
COPIES = 4
PEERS = NCB // COPIES
LANES = COPIES * CAP * PB
SLOTS = PEERS * COPIES * CAP
ENTRIES = 2 * PBD
COLS = PEERS * CAP * PB
MSG = CB + 16
EMPTY = 1e30
GROUP = ("zl", "y", "core", "x")
BETA = 1.0 / math.sqrt(D)
LOG2E = 1.0 / math.log(2.0)
LN2 = math.log(2.0)
F32 = jnp.float32
BF16 = jnp.bfloat16


def picked_sum(chosen, values):
    total = None
    for _ in range(3):
        piece = values.astype(BF16)
        part = jnp.dot(chosen, piece, preferred_element_type=F32)
        total = part if total is None else total + part
        values = values - piece.astype(F32)
    return total


def iota(shape, dim):
    return lax.broadcasted_iota(jnp.int32, shape, dim)


def pack_kernel(src, points, out):
    base = pl.program_id(0) * out.shape[0]

    def body(i, carry):
        s = src[base + i]
        block = points[jnp.maximum(s, 0)]
        out[i] = jnp.where(s >= 0, block, jnp.zeros_like(block))
        return carry

    lax.fori_loop(0, out.shape[0], body, 0, unroll=8)


def pack(src, points):
    per = 128
    return pl.pallas_call(
        pack_kernel,
        grid_spec=pltpu.PrefetchScalarGridSpec(
            num_scalar_prefetch=1,
            grid=(SLOTS // per,),
            in_specs=[pl.BlockSpec((PBD, PB, D), lambda i, s: (0, 0, 0))],
            out_specs=pl.BlockSpec((per, PB, D), lambda i, s: (i, 0, 0)),
        ),
        out_shape=jax.ShapeDtypeStruct((SLOTS, PB, D), BF16),
        compiler_params=pltpu.CompilerParams(vmem_limit_bytes=20 << 20),
        name="pack_points",
    )(src, points)


def norms_of(table):
    wide = table[...].astype(F32)
    return (BETA * LOG2E) * jnp.sum(wide * wide, axis=1, keepdims=True)


def scores_of(table, block, norms):
    products = lax.dot_general(table[...], block, (((1,), (1,)), ((), ())), preferred_element_type=F32)
    return (2.0 * BETA * LOG2E) * products - norms


def turned_by(value, groups, per_row):
    row = iota(value.shape, 0) % COPIES
    turned = value
    for k in range(COPIES):
        turn = lax.rem(groups + per_row * k + 2 * COPIES, COPIES) * (CAP * PB)
        turned = jnp.where(row == k, pltpu.roll(value, turn, 1), turned)
    return turned


def label_of(me, s):
    return lax.rem(me + 1 + s, COPIES)


def each_label(which, body):
    for k in range(len(which)):
        pl.when(pl.program_id(0) == k)(functools.partial(body, k))


def call_by_label(kernel, me, rows, tables, which, extra, outs, out_specs, flops, name):
    first = which[0]
    by = which[1] - which[0] if len(which) > 1 else 0
    row_spec = pl.BlockSpec((PEERS, CAP * PB, D), lambda i, m: (0, label_of(m[0], first + by * i), 0))
    whole = lambda v: pl.BlockSpec(v.shape, lambda i, m: (0,) * v.ndim)
    chosen = [tables[s] for s in which]
    return pl.pallas_call(
        functools.partial(kernel, which),
        grid_spec=pltpu.PrefetchScalarGridSpec(
            num_scalar_prefetch=1,
            grid=(len(which),),
            in_specs=[row_spec, *map(whole, chosen), *map(whole, extra)],
            out_specs=out_specs,
        ),
        out_shape=outs,
        compiler_params=pltpu.CompilerParams(vmem_limit_bytes=40 << 20),
        cost_estimate=pl.CostEstimate(
            flops=len(which) * flops * COLS * CB * D,
            bytes_accessed=len(which) * COLS * D * 2,
            transcendentals=len(which) * COLS * CB,
        ),
        name=name,
    )(me, rows, *chosen, *extra)


def score_kernel(which, me, rows, *refs):
    tables, previous, out = refs[: len(which)], refs[len(which) : -1], refs[-1]

    @pl.when(pl.program_id(0) == 0)
    def _():
        out[...] = previous[0][...] if previous else jnp.zeros_like(out)

    def body(k):
        label = label_of(me[0], which[k])
        scores = scores_of(tables[k], rows[...].reshape(COLS, D), norms_of(tables[k]))
        highest = jnp.max(scores, axis=0, keepdims=True)
        partial = highest + jnp.log2(jnp.sum(jnp.exp2(scores - highest), axis=0, keepdims=True))
        partial = partial * LN2
        tiles = [jnp.broadcast_to(partial[:, c : c + LANES], (COPIES, LANES)) for c in range(0, COLS, LANES)]
        lanes = iota((PEERS, LANES), 1) // (CAP * PB)
        out[...] = jnp.where(lanes == label, turned_by(jnp.concatenate(tiles, axis=0), label, -1), out[...])

    each_label(which, body)


def score(me, rows, tables, which, previous):
    return call_by_label(
        score_kernel, me, rows, tables, which, previous,
        jax.ShapeDtypeStruct((PEERS, LANES), F32),
        pl.BlockSpec((PEERS, LANES), lambda i, m: (0, 0)),
        2, "score_blocks",
    )


def home_kernel(returned, peer_col, slot_col, peer_row, lse, outward):
    pick = (iota((ENTRIES, PEERS), 1) == peer_col[...]).astype(BF16)
    mask = (iota((ENTRIES, LANES), 1) // PB == slot_col[...]).astype(F32)
    mine = picked_sum(pick, returned[...]) * mask
    turn = LANES // 2
    while turn >= PB:
        mine = mine + pltpu.roll(mine, turn, 1)
        turn //= 2
    first, second = mine[:PBD], mine[PBD:]
    highest = jnp.maximum(first, second)
    total = highest + jnp.log(jnp.exp(first - highest) + jnp.exp(second - highest))
    lse[...] = total
    place = (iota((PEERS, ENTRIES), 0) == peer_row[...]).astype(BF16)
    filled = jnp.dot(place, mask.astype(BF16), preferred_element_type=F32)
    both = jnp.concatenate([total, total], axis=0)
    outward[...] = jnp.where(filled > 0.5, picked_sum(place, both * mask), EMPTY)


def home(returned, peer_col, slot_col, peer_row):
    return pl.pallas_call(
        home_kernel,
        out_shape=(
            jax.ShapeDtypeStruct((PBD, LANES), F32),
            jax.ShapeDtypeStruct((PEERS, LANES), F32),
        ),
        name="join_halves",
    )(returned, peer_col, slot_col, peer_row)


def weigh_kernel(which, me, rows, *refs):
    tables, inward, outs = refs[: len(which)], refs[len(which)], refs[len(which) + 1 :]
    mine = iota((PEERS, LANES), 1) // (CAP * PB) == iota((PEERS, LANES), 0) % COPIES

    def body(k):
        label = label_of(me[0], which[k])
        block = rows[...].reshape(COLS, D)
        turned = jnp.where(mine, turned_by(inward[...] * LOG2E, -label, 1), 0.0)
        tiles = [jnp.sum(turned[c : c + COPIES], axis=0, keepdims=True) for c in range(0, PEERS, COPIES)]
        point_lse = jnp.concatenate(tiles, axis=1)
        weights = jnp.exp2(scores_of(tables[k], block, norms_of(tables[k])) - point_lse)
        sums = jnp.dot(weights.astype(BF16), block, preferred_element_type=F32)
        mass = weights[:, :128]
        for c in range(128, COLS, 128):
            mass += weights[:, c : c + 128]
        mass = jnp.sum(mass.T, axis=0, keepdims=True)
        if which[k] == COPIES - 1:
            outs[0][...] = sums
            outs[1][...] = jnp.broadcast_to(mass, outs[1].shape)
        else:
            outs[0][0, :CB] = sums.astype(BF16)
            coarse = mass.astype(BF16)
            fine = (mass - coarse.astype(F32)).astype(BF16)
            pair = jnp.concatenate([coarse.astype(F32), fine.astype(F32)], axis=1)
            outs[0][0, CB:] = jnp.broadcast_to(pair, (MSG - CB, D)).astype(BF16)

    each_label(which, body)


def weigh(me, rows, tables, which, inward):
    if which[0] == COPIES - 1:
        outs = (jax.ShapeDtypeStruct((CB, D), F32), jax.ShapeDtypeStruct((8, CB), F32))
        specs = [pl.BlockSpec(o.shape, lambda i, m: (0, 0)) for o in outs]
    else:
        outs = (jax.ShapeDtypeStruct((len(which), MSG, D), BF16),)
        specs = [pl.BlockSpec((1, MSG, D), lambda i, m: (i, 0, 0))]
    return call_by_label(weigh_kernel, me, rows, tables, which, (inward,), outs, specs, 4, "weigh_points")


def finish_kernel(own_sum, own_mass, m0, m1, m2, table, out):
    total, mass = own_sum[...], own_mass[:1]
    for message in (m0, m1, m2):
        total += message[:CB].astype(F32)
        pair = message[CB:].astype(F32)[:1]
        mass += pair[:, :CB] + pair[:, CB:]
    column = jnp.broadcast_to(mass + 1.0, (128, CB)).T[:, :1]
    fresh = ((total + table[...].astype(F32)) / column).astype(BF16)
    out[...] = jnp.broadcast_to(fresh, out.shape)


def finish(own_sum, own_mass, arrived, table, copies):
    return pl.pallas_call(
        finish_kernel,
        out_shape=jax.ShapeDtypeStruct((*copies, CB, D), BF16),
        compiler_params=pltpu.CompilerParams(vmem_limit_bytes=16 << 20),
        name="new_centres",
    )(own_sum, own_mass, *arrived, table)


def shifted(value, by):
    return lax.ppermute(value, "zh", [(i, (i + by) % COPIES) for i in range(COPIES)])


def tables_of(own):
    return [shifted(own, COPIES - 1 - s) for s in range(COPIES - 1)] + [own]


def exchange(value):
    return lax.all_to_all(value, GROUP, split_axis=0, concat_axis=0, tiled=True)


def route(candidates):
    picked = candidates.T.reshape(-1)
    labels = jnp.arange(NCB, dtype=jnp.int32)
    member = (picked[:, None] == labels[None, :]).astype(BF16)
    index = jnp.arange(ENTRIES, dtype=jnp.int32)
    earlier = (index[None, :] < index[:, None]).astype(BF16)
    hits = jnp.dot(earlier, member, preferred_element_type=F32)
    arrival = jnp.sum(hits * member.astype(F32), axis=1).astype(jnp.int32)
    peer = picked % PEERS
    slot = picked // PEERS * CAP + arrival
    position = peer * (COPIES * CAP) + slot
    places = jnp.arange(SLOTS, dtype=jnp.int32)
    source = jnp.sum(jnp.where(position[:, None] == places[None, :], index[:, None] % PBD + 1, 0), axis=0) - 1
    return source, peer, slot


def on_device(points, centroids, candidates):
    me = lax.axis_index("zh").reshape(1)
    own = lax.dynamic_slice_in_dim(centroids, lax.axis_index("x") * CB, CB, 0)
    source, peer, slot = route(candidates)
    outgoing = pack(source, points.reshape(PBD, PB, D))
    outgoing, *tables = lax.optimization_barrier((outgoing, *tables_of(own)))
    rows = exchange(outgoing.reshape(PEERS, LANES, D))
    for iteration in range(ITERS):
        partial = score(me, rows, tables, (3,), ())
        returned = exchange(score(me, rows, tables, (0, 1, 2), (partial,)))
        lse, outward = home(returned, peer[:, None], slot[:, None], peer[None, :])
        inward = exchange(outward)
        far, inward = lax.optimization_barrier((*weigh(me, rows, tables, (1,), inward), inward))
        arrived = [shifted(far[0], 2)]
        near, inward = lax.optimization_barrier((*weigh(me, rows, tables, (0, 2), inward), inward))
        arrived += [shifted(near[0], 1), shifted(near[1], 3)]
        own_sum, own_mass = weigh(me, rows, tables, (3,), inward)
        last = iteration == ITERS - 1
        own = finish(own_sum, own_mass, arrived, own, (COPIES,) if last else ())
        if not last:
            tables = tables_of(own)
    gathered = lax.all_to_all(own, "x", split_axis=0, concat_axis=0, tiled=True)
    return gathered.reshape(COPIES * CB, D), lse[:, :PB].reshape(-1)


def solution(mesh):
    split = Mesh(mesh.devices.reshape(4, 2, 4, 2, 4), ("zh", "zl", "y", "core", "x"))
    pts = ("zh", "zl", "y", "core")
    return jax.shard_map(
        on_device,
        mesh=split,
        in_specs=(P((*pts, "x"), None), P(pts, None), P((*pts, "x"), None)),
        out_specs=(P(pts, None), P((*pts, "x"))),
        check_vma=False,
    )
```

time: 348 us -> 348 us (level)
  waiting for transfers between devices: 199 us -> 181 us
  Pallas kernels: 38 us -> 45.4 us
  starting transfers between devices: 57.9 us -> 63.3 us
  blocking collectives: 40 us -> 45.1 us
    ppermute x12, waiting for transfers between devices: 72.2 us -> 53.9 us  [shifted(): lax.ppermute(value, 'zh', [(i, (i + by) % COPIES) for i in range(COPIES)])]
    pallas_call x4 -> x10, Pallas kernels: 29.1 us -> 37 us  [call_by_label(): pl.pallas_call(functools.partial(kernel, which), grid_spec=pltpu.Prefetch...]
    ppermute x12, starting transfers between devices: 30.9 us -> 36.3 us  [shifted(): lax.ppermute(value, 'zh', [(i, (i + by) % COPIES) for i in range(COPIES)])]
    all_to_all x3, blocking collectives: 40 us -> 45.1 us  [exchange(): return lax.all_to_all(value, GROUP, split_axis=0, concat_axis=0, tiled=True)]
  transfers between devices with their start and end apart: 15 -> 15, of which waited for: 13 -> 13; matrix products, arithmetic and copies ran while one was open for 1% -> 1% of each run, Pallas kernels for 1% -> 3%
where the time goes in v3:
time: 348 us; the launch traced here: 347 us
  waiting for transfers between devices  181 us (52%)
  starting transfers between devices  63.3 us (18%)
  Pallas kernels  45.4 us (13%)
  blocking collectives  45.1 us (13%)
  local copies, waits for them, and re-layouts  8.65 us (2%)
    all_to_all x2, waiting for transfers between devices, exchange(): return lax.all_to_all(value, GROUP, split_axis=0, concat_axis=0, tiled=True)  113 us
    ppermute x12, waiting for transfers between devices, shifted(): lax.ppermute(value, 'zh', [(i, (i + by) % COPIES) for i in range(COPIES)])  53.9 us
    all_to_all x3, blocking collectives, exchange(): return lax.all_to_all(value, GROUP, split_axis=0, concat_axis=0, tiled=True)  45.1 us
    pallas_call x10, Pallas kernels, call_by_label(): pl.pallas_call(functools.partial(kernel, which), grid_spec=pltpu.Prefetch...  37 us
    ppermute x12, starting transfers between devices, shifted(): lax.ppermute(value, 'zh', [(i, (i + by) % COPIES) for i in range(COPIES)])  36.3 us
    all_to_all x2, starting transfers between devices, exchange(): return lax.all_to_all(value, GROUP, split_axis=0, concat_axis=0, tiled=True)  23.4 us
    all_to_all x1, waiting for transfers between devices, on_device(): gathered = lax.all_to_all(own, 'x', split_axis=0, concat_axis=0, tiled=True)  14 us
    unnamed x13, local copies, waits for them, and re-layouts  7.61 us
  transfers between devices with their start and end apart: 15, of which 13 were waited for; matrix products, arithmetic and copies ran while one was open for 1% of the time, Pallas kernels for 3%

profile of v3, /device:TPU:1, one launch (start us, length us, event | category | flops | bytes accessed | tf_op | source)
XLA Modules:
  0.0 347.3 jit_solution(9826772511964316706)
XLA Ops:
  0.6 1.2 copy-done
  1.9 6.9 %collective-permute-start = (bf16[256,512]{1,0:T(8,128)(2,1)S(1)}, bf16[256,512]{1,0:T(8,128)(2,1)S(1)}, u32[]{:S(2)}, u32[]{:S(2)}) collective-permute-start(bf16[256,512]{1,0:T(8,128)(2,1)S(1)} %constant_dynamic-slice_fusion.refs_0_.table), channel_id=1, source_target_pairs={{0,192},{64,0},{128,64},{192,128},{1,193},{65,1},{129,65},{193,129... | collective-permute-start | bytes 786440 | tf_op jit(solution)/shard_map/ppermute | solution.py:247
  8.8 1.0 collective-permute-start.1
  9.8 2.3 collective-permute-start.2
  12.1 1.0 fusion
  13.9 1.6 copy-done.2
  15.5 2.3 pack_points.1
  17.9 3.2 copy-done.1
  21.1 4.2 %collective-permute-done.1.refs_1_.refs_0_ = bf16[256,512]{1,0:T(8,128)(2,1)S(1)} collective-permute-done((bf16[256,512]{1,0:T(8,128)(2,1)S(1)}, bf16[256,512]{1,0:T(8,128)(2,1)S(1)}, u32[]{:S(2)}, u32[]{:S(2)}) %collective-permute-start.1) | collective-permute-done | bytes 262176 | tf_op jit(solution)/shard_map/ppermute | solution.py:247
  25.3 2.8 collective-permute-done.2.refs_2_.refs_1_
  28.1 14.8 %all-to-all-start = ((bf16[64,128,512]{2,1,0:T(8,128)(2,1)}), bf16[64,128,512]{2,1,0:T(8,128)(2,1)}, u32[]{:S(2)}, u32[]{:S(2)}) async-start(bf16[64,128,512]{2,1,0:T(8,128)(2,1)} %bitcast.40), calls=%async_computation | async-start | bytes 16777216 | tf_op jit(solution)/shard_map/all_to_all | solution.py:255
  43.2 0.8 fusion.3
  44.0 105.4 %all-to-all-done.rows = bf16[64,128,512]{2,1,0:T(8,128)(2,1)} async-done(((bf16[64,128,512]{2,1,0:T(8,128)(2,1)}), bf16[64,128,512]{2,1,0:T(8,128)(2,1)}, u32[]{:S(2)}, u32[]{:S(2)}) %all-to-all-start) | async-done | bytes 8388640 | tf_op jit(solution)/shard_map/all_to_all | solution.py:255
  149.4 2.6 score_blocks.4.refs_3_
  151.9 5.8 %score_blocks.5 = f32[64,128]{1,0:T(8,128)} custom-call(s32[1]{0:T(128)} %bitcast.me, bf16[64,128,512]{2,1,0:T(8,128)(2,1)} %all-to-all-done.rows, bf16[256,512]{1,0:T(8,128)(2,1)S(1)} %collective-permute-done.refs_0_, bf16[256,512]{1,0:T(8,128)(2,1)S(1)} %collective-permute-done.1.refs_1_.refs_0_, ...), custom_call_target="tpu_custom_call" | custom-call | flops 1610612736 | bytes 6291456 | tf_op jit(solution)/shard_map/score_blocks/pallas_call | solution.py:110
  157.8 8.6 %all-to-all-start.1 = ((f32[64,1,128]{2,1,0:T(1,128)}), f32[64,1,128]{2,1,0:T(1,128)S(1)}, u32[]{:S(2)}, u32[]{:S(2)}) async-start(f32[64,1,128]{2,1,0:T(1,128)} %bitcast.7), calls=%async_computation.1 | async-start | bytes 65536 | tf_op jit(solution)/shard_map/all_to_all | solution.py:255
  167.0 7.5 %all-to-all-done.1 = f32[64,1,128]{2,1,0:T(1,128)S(1)} async-done(((f32[64,1,128]{2,1,0:T(1,128)}), f32[64,1,128]{2,1,0:T(1,128)S(1)}, u32[]{:S(2)}, u32[]{:S(2)}) %all-to-all-start.1) | async-done | bytes 32800 | tf_op jit(solution)/shard_map/all_to_all | solution.py:255
  175.1 2.3 join_halves.2
  177.4 12.8 %all_to_all.54 = f32[64,1,128]{2,1,0:T(1,128)S(1)} all-to-all(f32[64,1,128]{2,1,0:T(1,128)} %bitcast.56), channel_id=1, replica_groups=mesh['zh'=4,'zl'=2,'y'=4,'core'=2,'x'=4] {'zl','y','core','x'}, dimensions={0} | all-to-all | bytes 65536 | tf_op jit(solution)/shard_map/all_to_all | solution.py:255
  190.1 3.0 weigh_points.6
  193.1 4.5 %weigh_points.7 = bf16[2,272,512]{2,1,0:T(8,128)(2,1)S(1)} custom-call(s32[1]{0:T(128)} %bitcast.me, bf16[64,128,512]{2,1,0:T(8,128)(2,1)} %all-to-all-done.rows, bf16[256,512]{1,0:T(8,128)(2,1)S(1)} %collective-permute-done.refs_0_, bf16[256,512]{1,0:T(8,128)(2,1)S(1)} %collective-permute-done.2.refs_2_.refs_1_, f32[64,128]{1,0:T(8,128)S(1)} %bitcast.46), custom_call_target="tpu_custom_call" | custom-call | flops 2147483648 | bytes 4194304 | tf_op jit(solution)/shard_map/weigh_points/pallas_call | solution.py:110
  197.6 2.3 collective-permute-start.4
  199.9 2.0 collective-permute-start.5
  201.9 4.6 %collective-permute-start.3 = (bf16[272,512]{1,0:T(8,128)(2,1)S(1)}, bf16[272,512]{1,0:T(8,128)(2,1)S(1)}, u32[]{:S(2)}, u32[]{:S(2)}) collective-permute-start(bf16[272,512]{1,0:T(8,128)(2,1)S(1)} %bitcast.49), channel_id=1, source_target_pairs={{0,128},{64,192},{128,0},{192,64},{1,129},{65,193},{129,1},{193,65... | collective-permute-start | bytes 835592 | tf_op jit(solution)/shard_map/ppermute | solution.py:247
  206.5 3.0 weigh_points.8
  209.5 5.0 %collective-permute-done.4.m1 = bf16[272,512]{1,0:T(8,128)(2,1)S(1)} collective-permute-done((bf16[272,512]{1,0:T(8,128)(2,1)S(1)}, bf16[272,512]{1,0:T(8,128)(2,1)S(1)}, u32[]{:S(2)}, u32[]{:S(2)}) %collective-permute-start.4) | collective-permute-done | bytes 278560 | tf_op jit(solution)/shard_map/ppermute | solution.py:247
  214.4 9.4 %collective-permute-done.5.m2 = bf16[272,512]{1,0:T(8,128)(2,1)S(1)} collective-permute-done((bf16[272,512]{1,0:T(8,128)(2,1)S(1)}, bf16[272,512]{1,0:T(8,128)(2,1)S(1)}, u32[]{:S(2)}, u32[]{:S(2)}) %collective-permute-start.5) | collective-permute-done | bytes 278560 | tf_op jit(solution)/shard_map/ppermute | solution.py:247
  224.5 5.5 %collective-permute-start.6 = (bf16[256,512]{1,0:T(8,128)(2,1)S(1)}, bf16[256,512]{1,0:T(8,128)(2,1)S(1)}, u32[]{:S(2)}, u32[]{:S(2)}) collective-permute-start(bf16[256,512]{1,0:T(8,128)(2,1)S(1)} %new_centres.2.refs_0_.table), channel_id=1, source_target_pairs={{0,192},{64,0},{128,64},{192,128},{1,193},{65,1},{129,65},{193,129... | collective-permute-start | bytes 786440 | tf_op jit(solution)/shard_map/ppermute | solution.py:247
  230.0 2.2 collective-permute-start.8
  232.2 2.6 score_blocks.6.refs_3_
  234.7 4.0 %collective-permute-done.6.refs_0_ = bf16[256,512]{1,0:T(8,128)(2,1)S(1)} collective-permute-done((bf16[256,512]{1,0:T(8,128)(2,1)S(1)}, bf16[256,512]{1,0:T(8,128)(2,1)S(1)}, u32[]{:S(2)}, u32[]{:S(2)}) %collective-permute-start.6) | collective-permute-done | bytes 262176 | tf_op jit(solution)/shard_map/ppermute | solution.py:247
  238.7 2.6 collective-permute-done.7.refs_2_.refs_1_
  241.3 4.7 %collective-permute-done.8.refs_1_.refs_0_ = bf16[256,512]{1,0:T(8,128)(2,1)S(1)} collective-permute-done((bf16[256,512]{1,0:T(8,128)(2,1)S(1)}, bf16[256,512]{1,0:T(8,128)(2,1)S(1)}, u32[]{:S(2)}, u32[]{:S(2)}) %collective-permute-start.8) | collective-permute-done | bytes 262176 | tf_op jit(solution)/shard_map/ppermute | solution.py:247
  246.1 5.2 %score_blocks.7 = f32[64,128]{1,0:T(8,128)S(1)} custom-call(s32[1]{0:T(128)} %bitcast.me, bf16[64,128,512]{2,1,0:T(8,128)(2,1)} %all-to-all-done.rows, bf16[256,512]{1,0:T(8,128)(2,1)S(1)} %collective-permute-done.6.refs_0_, bf16[256,512]{1,0:T(8,128)(2,1)S(1)} %collective-permute-done.8.refs_1_.refs_0_, ...), custom_call_target="tpu_custom_call" | custom-call | flops 1610612736 | bytes 6291456 | tf_op jit(solution)/shard_map/score_blocks/pallas_call | solution.py:110
  251.3 19.5 %all_to_all.55 = f32[64,1,128]{2,1,0:T(1,128)} all-to-all(f32[64,1,128]{2,1,0:T(1,128)S(1)} %bitcast.50), channel_id=1, replica_groups=mesh['zh'=4,'zl'=2,'y'=4,'core'=2,'x'=4] {'zl','y','core','x'}, dimensions={0} | all-to-all | bytes 65536 | tf_op jit(solution)/shard_map/all_to_all | solution.py:255
  270.8 2.3 join_halves.3
  273.1 12.8 %all_to_all.56 = f32[64,1,128]{2,1,0:T(1,128)S(1)} all-to-all(f32[64,1,128]{2,1,0:T(1,128)} %bitcast.55), channel_id=1, replica_groups=mesh['zh'=4,'zl'=2,'y'=4,'core'=2,'x'=4] {'zl','y','core','x'}, dimensions={0} | all-to-all | bytes 65536 | tf_op jit(solution)/shard_map/all_to_all | solution.py:255
  285.9 3.0 weigh_points.9
  288.9 4.5 %weigh_points.10 = bf16[2,272,512]{2,1,0:T(8,128)(2,1)S(1)} custom-call(s32[1]{0:T(128)} %bitcast.me, bf16[64,128,512]{2,1,0:T(8,128)(2,1)} %all-to-all-done.rows, bf16[256,512]{1,0:T(8,128)(2,1)S(1)} %collective-permute-done.6.refs_0_, bf16[256,512]{1,0:T(8,128)(2,1)S(1)} %collective-permute-done.7.refs_2_.refs_1_, f32[64,128]{1,0:T(8,128)S(1)} %bitcast.43), custom_call_target="tpu_custom_call" | custom-call | flops 2147483648 | bytes 4194304 | tf_op jit(solution)/shard_map/weigh_points/pallas_call | solution.py:110
  293.4 6.3 %collective-permute-start.10 = (bf16[272,512]{1,0:T(8,128)(2,1)S(1)}, bf16[272,512]{1,0:T(8,128)(2,1)S(1)}, u32[]{:S(2)}, u32[]{:S(2)}) collective-permute-start(bf16[272,512]{1,0:T(8,128)(2,1)S(1)} %get-tuple-element.43), channel_id=1, source_target_pairs={{0,64},{64,128},{128,192},{192,0},{1,65},{65,129},{129,193},{193,1... | collective-permute-start | bytes 835592 | tf_op jit(solution)/shard_map/ppermute | solution.py:247
  299.7 3.3 collective-permute-start.9
  303.1 3.0 weigh_points.11
  306.0 6.1 %collective-permute-done.10.m1 = bf16[272,512]{1,0:T(8,128)(2,1)S(1)} collective-permute-done((bf16[272,512]{1,0:T(8,128)(2,1)S(1)}, bf16[272,512]{1,0:T(8,128)(2,1)S(1)}, u32[]{:S(2)}, u32[]{:S(2)}) %collective-permute-start.10) | collective-permute-done | bytes 278560 | tf_op jit(solution)/shard_map/ppermute | solution.py:247
  312.2 14.7 %collective-permute-done.11.m2 = bf16[272,512]{1,0:T(8,128)(2,1)S(1)} collective-permute-done((bf16[272,512]{1,0:T(8,128)(2,1)S(1)}, bf16[272,512]{1,0:T(8,128)(2,1)S(1)}, u32[]{:S(2)}, u32[]{:S(2)}) %collective-permute-start.11) | collective-permute-done | bytes 278560 | tf_op jit(solution)/shard_map/ppermute | solution.py:247
  326.9 1.2 new_centres.3
  328.1 3.5 %all-to-all-start.5 = ((bf16[4,256,512]{2,1,0:T(8,128)(2,1)}), bf16[4,256,512]{2,1,0:T(8,128)(2,1)S(1)}, u32[]{:S(2)}, u32[]{:S(2)}) async-start(bf16[4,256,512]{2,1,0:T(8,128)(2,1)} %new_centres.3), calls=%async_computation.5 | async-start | bytes 2097152 | tf_op jit(solution)/shard_map/all_to_all | solution.py:295
  332.3 14.0 %all-to-all-done.5 = bf16[4,256,512]{2,1,0:T(8,128)(2,1)S(1)} async-done(((bf16[4,256,512]{2,1,0:T(8,128)(2,1)}), bf16[4,256,512]{2,1,0:T(8,128)(2,1)S(1)}, u32[]{:S(2)}, u32[]{:S(2)}) %all-to-all-start.5) | async-done | bytes 1048608 | tf_op jit(solution)/shard_map/all_to_all | solution.py:295
  346.3 1.0 copy.29
  (26 shorter events, 3.9 us)
Async XLA Ops:
  0.6 1.2 copy-start
  1.9 19.2 %collective-permute-start = (bf16[256,512]{1,0:T(8,128)(2,1)S(1)}, bf16[256,512]{1,0:T(8,128)(2,1)S(1)}, u32[]{:S(2)}, u32[]{:S(2)}) collective-permute-start(bf16[256,512]{1,0:T(8,128)(2,1)S(1)} %constant_dynamic-slice_fusion.refs_0_.table), channel_id=1, source_target_pairs={{0,192},{64,0},{128,64},{192,128},{1,193},{65,1},{129,65},{193,129... | collective-permute-start | bytes 786440 | tf_op jit(solution)/shard_map/ppermute | solution.py:247
  8.8 16.5 %collective-permute-start.1 = (bf16[256,512]{1,0:T(8,128)(2,1)S(1)}, bf16[256,512]{1,0:T(8,128)(2,1)S(1)}, u32[]{:S(2)}, u32[]{:S(2)}) collective-permute-start(bf16[256,512]{1,0:T(8,128)(2,1)S(1)} %constant_dynamic-slice_fusion.refs_0_.table), channel_id=1, source_target_pairs={{0,128},{64,192},{128,0},{192,64},{1,129},{65,193},{129,1},{193,65... | collective-permute-start | bytes 786440 | tf_op jit(solution)/shard_map/ppermute | solution.py:247
  9.8 18.3 %collective-permute-start.2 = (bf16[256,512]{1,0:T(8,128)(2,1)S(1)}, bf16[256,512]{1,0:T(8,128)(2,1)S(1)}, u32[]{:S(2)}, u32[]{:S(2)}) collective-permute-start(bf16[256,512]{1,0:T(8,128)(2,1)S(1)} %constant_dynamic-slice_fusion.refs_0_.table), channel_id=1, source_target_pairs={{0,64},{64,128},{128,192},{192,0},{1,65},{65,129},{129,193},{193,1... | collective-permute-start | bytes 786440 | tf_op jit(solution)/shard_map/ppermute | solution.py:247
  13.9 1.6 copy-start.2
  17.9 3.2 copy-start.1
  28.1 15.0 %copy-start.5 = (s32[128,2]{0,1:T(2,128)S(1)}, s32[128,2]{0,1:T(2,128)}, u32[]{:S(2)}) copy-start(s32[128,2]{0,1:T(2,128)} %param.5) | copy-start | bytes 3076
  28.1 121.3 %all-to-all-start = ((bf16[64,128,512]{2,1,0:T(8,128)(2,1)}), bf16[64,128,512]{2,1,0:T(8,128)(2,1)}, u32[]{:S(2)}, u32[]{:S(2)}) async-start(bf16[64,128,512]{2,1,0:T(8,128)(2,1)} %bitcast.40), calls=%async_computation | async-start | bytes 16777216 | tf_op jit(solution)/shard_map/all_to_all | solution.py:255
  157.8 16.7 %all-to-all-start.1 = ((f32[64,1,128]{2,1,0:T(1,128)}), f32[64,1,128]{2,1,0:T(1,128)S(1)}, u32[]{:S(2)}, u32[]{:S(2)}) async-start(f32[64,1,128]{2,1,0:T(1,128)} %bitcast.7), calls=%async_computation.1 | async-start | bytes 65536 | tf_op jit(solution)/shard_map/all_to_all | solution.py:255
  174.5 0.6 copy-start.3
  197.6 16.8 %collective-permute-start.4 = (bf16[272,512]{1,0:T(8,128)(2,1)S(1)}, bf16[272,512]{1,0:T(8,128)(2,1)S(1)}, u32[]{:S(2)}, u32[]{:S(2)}) collective-permute-start(bf16[272,512]{1,0:T(8,128)(2,1)S(1)} %get-tuple-element.45), channel_id=1, source_target_pairs={{0,64},{64,128},{128,192},{192,0},{1,65},{65,129},{129,193},{193,1... | collective-permute-start | bytes 835592 | tf_op jit(solution)/shard_map/ppermute | solution.py:247
  199.9 24.0 %collective-permute-start.5 = (bf16[272,512]{1,0:T(8,128)(2,1)S(1)}, bf16[272,512]{1,0:T(8,128)(2,1)S(1)}, u32[]{:S(2)}, u32[]{:S(2)}) collective-permute-start(bf16[272,512]{1,0:T(8,128)(2,1)S(1)} %get-tuple-element.44), channel_id=1, source_target_pairs={{0,192},{64,0},{128,64},{192,128},{1,193},{65,1},{129,65},{193,129... | collective-permute-start | bytes 835592 | tf_op jit(solution)/shard_map/ppermute | solution.py:247
  201.9 22.4 %collective-permute-start.3 = (bf16[272,512]{1,0:T(8,128)(2,1)S(1)}, bf16[272,512]{1,0:T(8,128)(2,1)S(1)}, u32[]{:S(2)}, u32[]{:S(2)}) collective-permute-start(bf16[272,512]{1,0:T(8,128)(2,1)S(1)} %bitcast.49), channel_id=1, source_target_pairs={{0,128},{64,192},{128,0},{192,64},{1,129},{65,193},{129,1},{193,65... | collective-permute-start | bytes 835592 | tf_op jit(solution)/shard_map/ppermute | solution.py:247
  224.5 14.2 %collective-permute-start.6 = (bf16[256,512]{1,0:T(8,128)(2,1)S(1)}, bf16[256,512]{1,0:T(8,128)(2,1)S(1)}, u32[]{:S(2)}, u32[]{:S(2)}) collective-permute-start(bf16[256,512]{1,0:T(8,128)(2,1)S(1)} %new_centres.2.refs_0_.table), channel_id=1, source_target_pairs={{0,192},{64,0},{128,64},{192,128},{1,193},{65,1},{129,65},{193,129... | collective-permute-start | bytes 786440 | tf_op jit(solution)/shard_map/ppermute | solution.py:247
  230.0 11.4 %collective-permute-start.7 = (bf16[256,512]{1,0:T(8,128)(2,1)S(1)}, bf16[256,512]{1,0:T(8,128)(2,1)S(1)}, u32[]{:S(2)}, u32[]{:S(2)}) collective-permute-start(bf16[256,512]{1,0:T(8,128)(2,1)S(1)} %new_centres.2.refs_0_.table), channel_id=1, source_target_pairs={{0,64},{64,128},{128,192},{192,0},{1,65},{65,129},{129,193},{193,1... | collective-permute-start | bytes 786440 | tf_op jit(solution)/shard_map/ppermute | solution.py:247
  230.0 16.1 %collective-permute-start.8 = (bf16[256,512]{1,0:T(8,128)(2,1)S(1)}, bf16[256,512]{1,0:T(8,128)(2,1)S(1)}, u32[]{:S(2)}, u32[]{:S(2)}) collective-permute-start(bf16[256,512]{1,0:T(8,128)(2,1)S(1)} %new_centres.2.refs_0_.table), channel_id=1, source_target_pairs={{0,128},{64,192},{128,0},{192,64},{1,129},{65,193},{129,1},{193,65... | collective-permute-start | bytes 786440 | tf_op jit(solution)/shard_map/ppermute | solution.py:247
  293.4 38.2 %copy-start.4 = (f32[128,128]{1,0:T(8,128)S(1)}, f32[128,128]{1,0:T(8,128)}, u32[]{:S(2)}) copy-start(f32[128,128]{1,0:T(8,128)} %get-tuple-element.41) | copy-start | bytes 196612
  293.4 18.7 %collective-permute-start.10 = (bf16[272,512]{1,0:T(8,128)(2,1)S(1)}, bf16[272,512]{1,0:T(8,128)(2,1)S(1)}, u32[]{:S(2)}, u32[]{:S(2)}) collective-permute-start(bf16[272,512]{1,0:T(8,128)(2,1)S(1)} %get-tuple-element.43), channel_id=1, source_target_pairs={{0,64},{64,128},{128,192},{192,0},{1,65},{65,129},{129,193},{193,1... | collective-permute-start | bytes 835592 | tf_op jit(solution)/shard_map/ppermute | solution.py:247
  299.7 27.2 %collective-permute-start.11 = (bf16[272,512]{1,0:T(8,128)(2,1)S(1)}, bf16[272,512]{1,0:T(8,128)(2,1)S(1)}, u32[]{:S(2)}, u32[]{:S(2)}) collective-permute-start(bf16[272,512]{1,0:T(8,128)(2,1)S(1)} %get-tuple-element.42), channel_id=1, source_target_pairs={{0,192},{64,0},{128,64},{192,128},{1,193},{65,1},{129,65},{193,129... | collective-permute-start | bytes 835592 | tf_op jit(solution)/shard_map/ppermute | solution.py:247
  299.7 27.1 %collective-permute-start.9 = (bf16[272,512]{1,0:T(8,128)(2,1)S(1)}, bf16[272,512]{1,0:T(8,128)(2,1)S(1)}, u32[]{:S(2)}, u32[]{:S(2)}) collective-permute-start(bf16[272,512]{1,0:T(8,128)(2,1)S(1)} %bitcast.48), channel_id=1, source_target_pairs={{0,128},{64,192},{128,0},{192,64},{1,129},{65,193},{129,1},{193,65... | collective-permute-start | bytes 835592 | tf_op jit(solution)/shard_map/ppermute | solution.py:247
  328.1 18.2 %all-to-all-start.5 = ((bf16[4,256,512]{2,1,0:T(8,128)(2,1)}), bf16[4,256,512]{2,1,0:T(8,128)(2,1)S(1)}, u32[]{:S(2)}, u32[]{:S(2)}) async-start(bf16[4,256,512]{2,1,0:T(8,128)(2,1)} %new_centres.3), calls=%async_computation.5 | async-start | bytes 2097152 | tf_op jit(solution)/shard_map/all_to_all | solution.py:295

commit v4 on v3

--- a/solution.py
+++ b/solution.py
@@ -22,6 +22,8 @@
 ENTRIES = 2 * PBD
 COLS = PEERS * CAP * PB
 MSG = CB + 16
+ORDER = (2, 1, 3)
+LIMIT = 28
 EMPTY = 1e30
 GROUP = ("zl", "y", "core", "x")
 BETA = 1.0 / math.sqrt(D)
@@ -96,63 +98,63 @@
     return lax.rem(me + 1 + s, COPIES)
 
 
-def each_label(which, body):
-    for k in range(len(which)):
-        pl.when(pl.program_id(0) == k)(functools.partial(body, k))
-
-
-def call_by_label(kernel, me, rows, tables, which, extra, outs, out_specs, flops, name):
-    first = which[0]
-    by = which[1] - which[0] if len(which) > 1 else 0
-    row_spec = pl.BlockSpec((PEERS, CAP * PB, D), lambda i, m: (0, label_of(m[0], first + by * i), 0))
-    whole = lambda v: pl.BlockSpec(v.shape, lambda i, m: (0,) * v.ndim)
-    chosen = [tables[s] for s in which]
+def call_whole(kernel, me, rows, tables, which, extra, outs, flops, name):
     return pl.pallas_call(
         functools.partial(kernel, which),
-        grid_spec=pltpu.PrefetchScalarGridSpec(
-            num_scalar_prefetch=1,
-            grid=(len(which),),
-            in_specs=[row_spec, *map(whole, chosen), *map(whole, extra)],
-            out_specs=out_specs,
-        ),
+        in_specs=[pl.BlockSpec(memory_space=pltpu.SMEM)]
+        + [pl.BlockSpec(memory_space=pltpu.VMEM)] * (1 + len(which) + len(extra)),
         out_shape=outs,
-        compiler_params=pltpu.CompilerParams(vmem_limit_bytes=40 << 20),
+        compiler_params=pltpu.CompilerParams(vmem_limit_bytes=LIMIT << 20),
         cost_estimate=pl.CostEstimate(
             flops=len(which) * flops * COLS * CB * D,
             bytes_accessed=len(which) * COLS * D * 2,
             transcendentals=len(which) * COLS * CB,
         ),
         name=name,
-    )(me, rows, *chosen, *extra)
+    )(me, rows, *[tables[s] for s in which], *extra)
+
+
+def keep_kernel(source, kept, done):
+    copy = pltpu.make_async_copy(source, kept, done)
+    copy.start()
+    copy.wait()
+
+
+def keep(rows):
+    return pl.pallas_call(
+        keep_kernel,
+        in_specs=[pl.BlockSpec(memory_space=pl.ANY)],
+        out_specs=pl.BlockSpec(memory_space=pltpu.VMEM),
+        out_shape=jax.ShapeDtypeStruct(rows.shape, rows.dtype),
+        scratch_shapes=[pltpu.SemaphoreType.DMA],
+        compiler_params=pltpu.CompilerParams(vmem_limit_bytes=LIMIT << 20),
+        name="keep_points",
+    )(rows)
+
+
+def rows_of(rows, label):
+    part = rows[:, pl.ds(pl.multiple_of(label * (CAP * PB), CAP * PB), CAP * PB), :]
+    return part.reshape(COLS, D)
 
 
 def score_kernel(which, me, rows, *refs):
-    tables, previous, out = refs[: len(which)], refs[len(which) : -1], refs[-1]
-
-    @pl.when(pl.program_id(0) == 0)
-    def _():
-        out[...] = previous[0][...] if previous else jnp.zeros_like(out)
-
-    def body(k):
-        label = label_of(me[0], which[k])
-        scores = scores_of(tables[k], rows[...].reshape(COLS, D), norms_of(tables[k]))
+    tables, out = refs[:-1], refs[-1]
+    lanes = iota((PEERS, LANES), 1) // (CAP * PB)
+    total = jnp.zeros((PEERS, LANES), F32)
+    for k, s in enumerate(which):
+        label = label_of(me[0], s)
+        scores = scores_of(tables[k], rows_of(rows, label), norms_of(tables[k]))
         highest = jnp.max(scores, axis=0, keepdims=True)
         partial = highest + jnp.log2(jnp.sum(jnp.exp2(scores - highest), axis=0, keepdims=True))
         partial = partial * LN2
         tiles = [jnp.broadcast_to(partial[:, c : c + LANES], (COPIES, LANES)) for c in range(0, COLS, LANES)]
-        lanes = iota((PEERS, LANES), 1) // (CAP * PB)
-        out[...] = jnp.where(lanes == label, turned_by(jnp.concatenate(tiles, axis=0), label, -1), out[...])
-
-    each_label(which, body)
-
-
-def score(me, rows, tables, which, previous):
-    return call_by_label(
-        score_kernel, me, rows, tables, which, previous,
-        jax.ShapeDtypeStruct((PEERS, LANES), F32),
-        pl.BlockSpec((PEERS, LANES), lambda i, m: (0, 0)),
-        2, "score_blocks",
-    )
+        total = jnp.where(lanes == label, turned_by(jnp.concatenate(tiles, axis=0), label, -1), total)
+    out[...] = total
+
+
+def score(me, rows, tables):
+    out = jax.ShapeDtypeStruct((PEERS, LANES), F32)
+    return call_whole(score_kernel, me, rows, tables, (0, 1, 2, 3), (), out, 2, "score_blocks")
 
 
 def home_kernel(returned, peer_col, slot_col, peer_row, lse, outward):
@@ -180,6 +182,7 @@
             jax.ShapeDtypeStruct((PBD, LANES), F32),
             jax.ShapeDtypeStruct((PEERS, LANES), F32),
         ),
+        compiler_params=pltpu.CompilerParams(vmem_limit_bytes=8 << 20),
         name="join_halves",
     )(returned, peer_col, slot_col, peer_row)
 
@@ -187,11 +190,11 @@
 def weigh_kernel(which, me, rows, *refs):
     tables, inward, outs = refs[: len(which)], refs[len(which)], refs[len(which) + 1 :]
     mine = iota((PEERS, LANES), 1) // (CAP * PB) == iota((PEERS, LANES), 0) % COPIES
-
-    def body(k):
-        label = label_of(me[0], which[k])
-        block = rows[...].reshape(COLS, D)
-        turned = jnp.where(mine, turned_by(inward[...] * LOG2E, -label, 1), 0.0)
+    incoming = inward[...] * LOG2E
+    for k, s in enumerate(which):
+        label = label_of(me[0], s)
+        block = rows_of(rows, label)
+        turned = jnp.where(mine, turned_by(incoming, -label, 1), 0.0)
         tiles = [jnp.sum(turned[c : c + COPIES], axis=0, keepdims=True) for c in range(0, PEERS, COPIES)]
         point_lse = jnp.concatenate(tiles, axis=1)
         weights = jnp.exp2(scores_of(tables[k], block, norms_of(tables[k])) - point_lse)
@@ -200,27 +203,25 @@
         for c in range(128, COLS, 128):
             mass += weights[:, c : c + 128]
         mass = jnp.sum(mass.T, axis=0, keepdims=True)
-        if which[k] == COPIES - 1:
+        if s == COPIES - 1:
             outs[0][...] = sums
             outs[1][...] = jnp.broadcast_to(mass, outs[1].shape)
-        else:
-            outs[0][0, :CB] = sums.astype(BF16)
-            coarse = mass.astype(BF16)
-            fine = (mass - coarse.astype(F32)).astype(BF16)
-            pair = jnp.concatenate([coarse.astype(F32), fine.astype(F32)], axis=1)
-            outs[0][0, CB:] = jnp.broadcast_to(pair, (MSG - CB, D)).astype(BF16)
-
-    each_label(which, body)
-
-
-def weigh(me, rows, tables, which, inward):
-    if which[0] == COPIES - 1:
-        outs = (jax.ShapeDtypeStruct((CB, D), F32), jax.ShapeDtypeStruct((8, CB), F32))
-        specs = [pl.BlockSpec(o.shape, lambda i, m: (0, 0)) for o in outs]
-    else:
-        outs = (jax.ShapeDtypeStruct((len(which), MSG, D), BF16),)
-        specs = [pl.BlockSpec((1, MSG, D), lambda i, m: (i, 0, 0))]
-    return call_by_label(weigh_kernel, me, rows, tables, which, (inward,), outs, specs, 4, "weigh_points")
+            continue
+        coarse = mass.astype(BF16).astype(F32)
+        fine = mass - coarse
+        outs[0][k, :CB] = sums.astype(BF16)
+        pair = jnp.concatenate([coarse, fine], axis=1)
+        outs[0][k, CB:] = jnp.broadcast_to(pair, (MSG - CB, D)).astype(BF16)
+
+
+def weigh_own(me, rows, tables, inward):
+    outs = (jax.ShapeDtypeStruct((CB, D), F32), jax.ShapeDtypeStruct((8, CB), F32))
+    return call_whole(weigh_kernel, me, rows, tables, (3,), (inward,), outs, 4, "weigh_own")
+
+
+def weigh_others(me, rows, tables, inward):
+    out = jax.ShapeDtypeStruct((COPIES - 1, MSG, D), BF16)
+    return call_whole(weigh_kernel, me, rows, tables, (0, 1, 2), (inward,), out, 4, "weigh_others")
 
 
 def finish_kernel(own_sum, own_mass, m0, m1, m2, table, out):
@@ -276,19 +277,18 @@
     own = lax.dynamic_slice_in_dim(centroids, lax.axis_index("x") * CB, CB, 0)
     source, peer, slot = route(candidates)
     outgoing = pack(source, points.reshape(PBD, PB, D))
-    outgoing, *tables = lax.optimization_barrier((outgoing, *tables_of(own)))
-    rows = exchange(outgoing.reshape(PEERS, LANES, D))
+    where = (peer[:, None], slot[:, None], peer[None, :])
+    outgoing, where, tables = lax.optimization_barrier((outgoing, where, tables_of(own)))
+    rows = keep(exchange(outgoing.reshape(PEERS, LANES, D)))
     for iteration in range(ITERS):
-        partial = score(me, rows, tables, (3,), ())
-        returned = exchange(score(me, rows, tables, (0, 1, 2), (partial,)))
-        lse, outward = home(returned, peer[:, None], slot[:, None], peer[None, :])
+        returned = exchange(score(me, rows, tables))
+        lse, outward = home(returned, *where)
         inward = exchange(outward)
-        far, inward = lax.optimization_barrier((*weigh(me, rows, tables, (1,), inward), inward))
-        arrived = [shifted(far[0], 2)]
-        near, inward = lax.optimization_barrier((*weigh(me, rows, tables, (0, 2), inward), inward))
-        arrived += [shifted(near[0], 1), shifted(near[1], 3)]
-        own_sum, own_mass = weigh(me, rows, tables, (3,), inward)
         last = iteration == ITERS - 1
+        messages = weigh_others(me, rows, tables, inward)
+        arrived = [shifted(messages[n - 1], n) for n in ORDER]
+        messages, inward = lax.optimization_barrier((messages, inward))
+        own_sum, own_mass = weigh_own(me, rows, tables, inward)
         own = finish(own_sum, own_mass, arrived, own, (COPIES,) if last else ())
         if not last:
             tables = tables_of(own)

time: 348 us -> 331 us (0.951)
  Pallas kernels: 45.4 us -> 25.8 us
  starting transfers between devices: 63.3 us -> 43.9 us
  waiting for transfers between devices: 181 us -> 195 us
  blocking collectives: 45.1 us -> 53.3 us
    ppermute x12, waiting for transfers between devices: 53.9 us -> 75.2 us  [shifted(): lax.ppermute(value, 'zh', [(i, (i + by) % COPIES) for i in range(COPIES)])]
    pallas_call x10 -> x7, Pallas kernels: 37 us -> 20.2 us  [the longest x6 16.8 us: call_whole(): pl.pallas_call(functools.partial(kernel, which), in_specs=[pl.BlockSpec(m...]
    all_to_all x2 -> x1, starting transfers between devices: 23.4 us -> 8.17 us  [exchange(): return lax.all_to_all(value, GROUP, split_axis=0, concat_axis=0, tiled=True)]
    all_to_all x3 -> x4, blocking collectives: 45.1 us -> 53.3 us  [exchange(): return lax.all_to_all(value, GROUP, split_axis=0, concat_axis=0, tiled=True)]
    all_to_all x2 -> x1, waiting for transfers between devices: 113 us -> 107 us  [exchange(): return lax.all_to_all(value, GROUP, split_axis=0, concat_axis=0, tiled=True)]
    ppermute x12, starting transfers between devices: 36.3 us -> 32.3 us  [shifted(): lax.ppermute(value, 'zh', [(i, (i + by) % COPIES) for i in range(COPIES)])]
    unnamed x13 -> x7, local copies, waits for them, and re-layouts: 7.61 us -> 7 us
  transfers between devices with their start and end apart: 15 -> 14, of which waited for: 13 -> 11; matrix products, arithmetic and copies ran while one was open for 1% -> 1% of each run, Pallas kernels for 3% -> 2%
where the time goes in v4:
time: 331 us; the launch traced here: 330 us
  waiting for transfers between devices  195 us (59%)
  blocking collectives  53.3 us (16%)
  starting transfers between devices  43.9 us (13%)
  Pallas kernels  25.8 us (8%)
  local copies, waits for them, and re-layouts  8.75 us (3%)
    all_to_all x1, waiting for transfers between devices, exchange(): return lax.all_to_all(value, GROUP, split_axis=0, concat_axis=0, tiled=True)  107 us
    ppermute x12, waiting for transfers between devices, shifted(): lax.ppermute(value, 'zh', [(i, (i + by) % COPIES) for i in range(COPIES)])  75.2 us
    all_to_all x4, blocking collectives, exchange(): return lax.all_to_all(value, GROUP, split_axis=0, concat_axis=0, tiled=True)  53.3 us
    ppermute x12, starting transfers between devices, shifted(): lax.ppermute(value, 'zh', [(i, (i + by) % COPIES) for i in range(COPIES)])  32.3 us
    pallas_call x6, Pallas kernels, call_whole(): pl.pallas_call(functools.partial(kernel, which), in_specs=[pl.BlockSpec(m...  16.8 us
    all_to_all x1, waiting for transfers between devices, on_device(): gathered = lax.all_to_all(own, 'x', split_axis=0, concat_axis=0, tiled=True)  13.4 us
    all_to_all x1, starting transfers between devices, exchange(): return lax.all_to_all(value, GROUP, split_axis=0, concat_axis=0, tiled=True)  8.17 us
    unnamed x7, local copies, waits for them, and re-layouts  7 us
  transfers between devices with their start and end apart: 14, of which 11 were waited for; matrix products, arithmetic and copies ran while one was open for 1% of the time, Pallas kernels for 2%

profile of v4, /device:TPU:1, one launch (start us, length us, event | category | flops | bytes accessed | tf_op | source)
XLA Modules:
  0.0 330.4 jit_solution(16700210086354557020)
XLA Ops:
  0.6 1.2 copy-done
  1.9 3.9 %collective-permute-start.2 = (bf16[256,512]{1,0:T(8,128)(2,1)S(1)}, bf16[256,512]{1,0:T(8,128)(2,1)S(1)}, u32[]{:S(2)}, u32[]{:S(2)}) collective-permute-start(bf16[256,512]{1,0:T(8,128)(2,1)S(1)} %constant_dynamic-slice_fusion.refs_3_.refs_0_.table), channel_id=1, source_target_pairs={{0,64},{64,128},{128,192},{192,0},{1,65},{65,129},{129,193},{193,1... | collective-permute-start | bytes 786440 | tf_op jit(solution)/shard_map/ppermute | solution.py:248
  5.8 5.1 %collective-permute-start.1 = (bf16[256,512]{1,0:T(8,128)(2,1)S(1)}, bf16[256,512]{1,0:T(8,128)(2,1)S(1)}, u32[]{:S(2)}, u32[]{:S(2)}) collective-permute-start(bf16[256,512]{1,0:T(8,128)(2,1)S(1)} %constant_dynamic-slice_fusion.refs_3_.refs_0_.table), channel_id=1, source_target_pairs={{0,128},{64,192},{128,0},{192,64},{1,129},{65,193},{129,1},{193,65... | collective-permute-start | bytes 786440 | tf_op jit(solution)/shard_map/ppermute | solution.py:248
  10.9 2.4 collective-permute-start
  13.3 1.0 fusion
  14.3 0.7 fusion.8
  15.1 0.7 and_select_fusion.peer_row
  16.0 0.8 copy.19
  16.8 1.6 copy-done.2
  18.4 2.3 pack_points.1
  20.8 3.2 copy-done.1
  24.1 2.1 collective-permute-done.1.refs_1_
  26.2 8.9 %collective-permute-done.refs_0_ = bf16[256,512]{1,0:T(8,128)(2,1)S(1)} collective-permute-done((bf16[256,512]{1,0:T(8,128)(2,1)S(1)}, bf16[256,512]{1,0:T(8,128)(2,1)S(1)}, u32[]{:S(2)}, u32[]{:S(2)}) %collective-permute-start) | collective-permute-done | bytes 262176 | tf_op jit(solution)/shard_map/ppermute | solution.py:248
  35.1 8.2 %all-to-all-start = ((bf16[64,128,512]{2,1,0:T(8,128)(2,1)}), bf16[64,128,512]{2,1,0:T(8,128)(2,1)}, u32[]{:S(2)}, u32[]{:S(2)}) async-start(bf16[64,128,512]{2,1,0:T(8,128)(2,1)} %bitcast.42), calls=%async_computation | async-start | bytes 16777216 | tf_op jit(solution)/shard_map/all_to_all | solution.py:256
  43.3 106.5 %all-to-all-done.source = bf16[64,128,512]{2,1,0:T(8,128)(2,1)} async-done(((bf16[64,128,512]{2,1,0:T(8,128)(2,1)}), bf16[64,128,512]{2,1,0:T(8,128)(2,1)}, u32[]{:S(2)}, u32[]{:S(2)}) %all-to-all-start) | async-done | bytes 8388640 | tf_op jit(solution)/shard_map/all_to_all | solution.py:256
  149.8 3.4 %keep_points.1.rows = bf16[64,128,512]{2,1,0:T(8,128)(2,1)S(1)} custom-call(bf16[64,128,512]{2,1,0:T(8,128)(2,1)} %all-to-all-done.source), custom_call_target="tpu_custom_call" | custom-call | tf_op jit(solution)/shard_map/keep_points/pallas_call | solution.py:124
  153.2 3.0 score_blocks.2
  156.3 16.5 %all_to_all.54 = f32[64,1,128]{2,1,0:T(1,128)S(1)} all-to-all(f32[64,1,128]{2,1,0:T(1,128)S(1)} %bitcast.48), channel_id=1, replica_groups=mesh['zh'=4,'zl'=2,'y'=4,'core'=2,'x'=4] {'zl','y','core','x'}, dimensions={0} | all-to-all | bytes 65536 | tf_op jit(solution)/shard_map/all_to_all | solution.py:256
  172.8 1.1 join_halves.2
  173.9 12.1 %all_to_all.55 = f32[64,1,128]{2,1,0:T(1,128)S(1)} all-to-all(f32[64,1,128]{2,1,0:T(1,128)S(1)} %bitcast.54), channel_id=1, replica_groups=mesh['zh'=4,'zl'=2,'y'=4,'core'=2,'x'=4] {'zl','y','core','x'}, dimensions={0} | all-to-all | bytes 65536 | tf_op jit(solution)/shard_map/all_to_all | solution.py:256
  186.0 3.9 %weigh_others.2 = bf16[3,272,512]{2,1,0:T(8,128)(2,1)S(1)} custom-call(s32[1]{0:T(128)} %bitcast.me, bf16[64,128,512]{2,1,0:T(8,128)(2,1)S(1)} %keep_points.1.rows, bf16[256,512]{1,0:T(8,128)(2,1)S(1)} %collective-permute-done.refs_0_, bf16[256,512]{1,0:T(8,128)(2,1)S(1)} %collective-permute-done.1.refs_1_, ...), custom_call_target="tpu_custom_call" | custom-call | flops 3221225472 | bytes 6291456 | tf_op jit(solution)/shard_map/weigh_others/pallas_call | solution.py:102
  190.1 3.3 %collective-permute-start.5 = (bf16[272,512]{1,0:T(8,128)(2,1)S(1)}, bf16[272,512]{1,0:T(8,128)(2,1)S(1)}, u32[]{:S(2)}, u32[]{:S(2)}) collective-permute-start(bf16[272,512]{1,0:T(8,128)(2,1)S(1)} %get-tuple-element.39), channel_id=1, source_target_pairs={{0,192},{64,0},{128,64},{192,128},{1,193},{65,1},{129,65},{193,129... | collective-permute-start | bytes 835592 | tf_op jit(solution)/shard_map/ppermute | solution.py:248
  193.4 3.1 collective-permute-start.3
  196.4 1.4 weigh_own.2
  197.8 16.2 %collective-permute-done.5.m2 = bf16[272,512]{1,0:T(8,128)(2,1)S(1)} collective-permute-done((bf16[272,512]{1,0:T(8,128)(2,1)S(1)}, bf16[272,512]{1,0:T(8,128)(2,1)S(1)}, u32[]{:S(2)}, u32[]{:S(2)}) %collective-permute-start.5) | collective-permute-done | bytes 278560 | tf_op jit(solution)/shard_map/ppermute | solution.py:248
  214.0 3.9 %collective-permute-done.3.m0 = bf16[272,512]{1,0:T(8,128)(2,1)S(1)} collective-permute-done((bf16[272,512]{1,0:T(8,128)(2,1)S(1)}, bf16[272,512]{1,0:T(8,128)(2,1)S(1)}, u32[]{:S(2)}, u32[]{:S(2)}) %collective-permute-start.3) | collective-permute-done | bytes 278560 | tf_op jit(solution)/shard_map/ppermute | solution.py:248
  218.2 5.0 %collective-permute-start.8 = (bf16[256,512]{1,0:T(8,128)(2,1)S(1)}, bf16[256,512]{1,0:T(8,128)(2,1)S(1)}, u32[]{:S(2)}, u32[]{:S(2)}) collective-permute-start(bf16[256,512]{1,0:T(8,128)(2,1)S(1)} %new_centres.2.refs_3_.refs_0_.table), channel_id=1, source_target_pairs={{0,64},{64,128},{128,192},{192,0},{1,65},{65,129},{129,193},{193,1... | collective-permute-start | bytes 786440 | tf_op jit(solution)/shard_map/ppermute | solution.py:248
  223.1 1.3 collective-permute-start.7
  224.5 2.0 collective-permute-start.6
  226.5 7.8 %collective-permute-done.8.refs_2_ = bf16[256,512]{1,0:T(8,128)(2,1)S(1)} collective-permute-done((bf16[256,512]{1,0:T(8,128)(2,1)S(1)}, bf16[256,512]{1,0:T(8,128)(2,1)S(1)}, u32[]{:S(2)}, u32[]{:S(2)}) %collective-permute-start.8) | collective-permute-done | bytes 262176 | tf_op jit(solution)/shard_map/ppermute | solution.py:248
  234.4 12.9 %collective-permute-done.7.refs_1_ = bf16[256,512]{1,0:T(8,128)(2,1)S(1)} collective-permute-done((bf16[256,512]{1,0:T(8,128)(2,1)S(1)}, bf16[256,512]{1,0:T(8,128)(2,1)S(1)}, u32[]{:S(2)}, u32[]{:S(2)}) %collective-permute-start.7) | collective-permute-done | bytes 262176 | tf_op jit(solution)/shard_map/ppermute | solution.py:248
  247.3 0.8 collective-permute-done.6.refs_0_
  248.0 3.1 score_blocks.3
  251.1 12.5 %all_to_all.56 = f32[64,1,128]{2,1,0:T(1,128)S(1)} all-to-all(f32[64,1,128]{2,1,0:T(1,128)S(1)} %bitcast.49), channel_id=1, replica_groups=mesh['zh'=4,'zl'=2,'y'=4,'core'=2,'x'=4] {'zl','y','core','x'}, dimensions={0} | all-to-all | bytes 65536 | tf_op jit(solution)/shard_map/all_to_all | solution.py:256
  263.6 0.7 join_halves.3
  264.3 12.2 %all_to_all.57 = f32[64,1,128]{2,1,0:T(1,128)S(1)} all-to-all(f32[64,1,128]{2,1,0:T(1,128)S(1)} %bitcast.53), channel_id=1, replica_groups=mesh['zh'=4,'zl'=2,'y'=4,'core'=2,'x'=4] {'zl','y','core','x'}, dimensions={0} | all-to-all | bytes 65536 | tf_op jit(solution)/shard_map/all_to_all | solution.py:256
  276.4 4.0 %weigh_others.3 = bf16[3,272,512]{2,1,0:T(8,128)(2,1)S(1)} custom-call(s32[1]{0:T(128)} %bitcast.me, bf16[64,128,512]{2,1,0:T(8,128)(2,1)S(1)} %keep_points.1.rows, bf16[256,512]{1,0:T(8,128)(2,1)S(1)} %collective-permute-done.6.refs_0_, bf16[256,512]{1,0:T(8,128)(2,1)S(1)} %collective-permute-done.7.refs_1_, ...), custom_call_target="tpu_custom_call" | custom-call | flops 3221225472 | bytes 6291456 | tf_op jit(solution)/shard_map/weigh_others/pallas_call | solution.py:102
  280.5 2.0 collective-permute-start.11
  282.4 0.5 collective-permute-start.10
  282.9 3.7 %collective-permute-start.9 = (bf16[272,512]{1,0:T(8,128)(2,1)S(1)}, bf16[272,512]{1,0:T(8,128)(2,1)S(1)}, u32[]{:S(2)}, u32[]{:S(2)}) collective-permute-start(bf16[272,512]{1,0:T(8,128)(2,1)S(1)} %get-tuple-element.38), channel_id=1, source_target_pairs={{0,128},{64,192},{128,0},{192,64},{1,129},{65,193},{129,1},{193,65... | collective-permute-start | bytes 835592 | tf_op jit(solution)/shard_map/ppermute | solution.py:248
  286.6 1.4 weigh_own.3
  288.0 19.7 %collective-permute-done.11.m2 = bf16[272,512]{1,0:T(8,128)(2,1)S(1)} collective-permute-done((bf16[272,512]{1,0:T(8,128)(2,1)S(1)}, bf16[272,512]{1,0:T(8,128)(2,1)S(1)}, u32[]{:S(2)}, u32[]{:S(2)}) %collective-permute-start.11) | collective-permute-done | bytes 278560 | tf_op jit(solution)/shard_map/ppermute | solution.py:248
  307.7 2.9 collective-permute-done.9.m0
  310.6 1.2 new_centres.3
  311.8 3.5 %all-to-all-start.5 = ((bf16[4,256,512]{2,1,0:T(8,128)(2,1)}), bf16[4,256,512]{2,1,0:T(8,128)(2,1)S(1)}, u32[]{:S(2)}, u32[]{:S(2)}) async-start(bf16[4,256,512]{2,1,0:T(8,128)(2,1)} %new_centres.3), calls=%async_computation.5 | async-start | bytes 2097152 | tf_op jit(solution)/shard_map/all_to_all | solution.py:295
  315.4 0.7 reshape.246
  316.0 13.4 %all-to-all-done.5 = bf16[4,256,512]{2,1,0:T(8,128)(2,1)S(1)} async-done(((bf16[4,256,512]{2,1,0:T(8,128)(2,1)}), bf16[4,256,512]{2,1,0:T(8,128)(2,1)S(1)}, u32[]{:S(2)}, u32[]{:S(2)}) %all-to-all-start.5) | async-done | bytes 1048608 | tf_op jit(solution)/shard_map/all_to_all | solution.py:295
  329.4 1.0 copy.29
  (16 shorter events, 0.8 us)
Async XLA Ops:
  0.6 1.2 copy-start
  1.9 22.2 %collective-permute-start.2 = (bf16[256,512]{1,0:T(8,128)(2,1)S(1)}, bf16[256,512]{1,0:T(8,128)(2,1)S(1)}, u32[]{:S(2)}, u32[]{:S(2)}) collective-permute-start(bf16[256,512]{1,0:T(8,128)(2,1)S(1)} %constant_dynamic-slice_fusion.refs_3_.refs_0_.table), channel_id=1, source_target_pairs={{0,64},{64,128},{128,192},{192,0},{1,65},{65,129},{129,193},{193,1... | collective-permute-start | bytes 786440 | tf_op jit(solution)/shard_map/ppermute | solution.py:248
  5.8 20.4 %collective-permute-start.1 = (bf16[256,512]{1,0:T(8,128)(2,1)S(1)}, bf16[256,512]{1,0:T(8,128)(2,1)S(1)}, u32[]{:S(2)}, u32[]{:S(2)}) collective-permute-start(bf16[256,512]{1,0:T(8,128)(2,1)S(1)} %constant_dynamic-slice_fusion.refs_3_.refs_0_.table), channel_id=1, source_target_pairs={{0,128},{64,192},{128,0},{192,64},{1,129},{65,193},{129,1},{193,65... | collective-permute-start | bytes 786440 | tf_op jit(solution)/shard_map/ppermute | solution.py:248
  10.9 24.3 %collective-permute-start = (bf16[256,512]{1,0:T(8,128)(2,1)S(1)}, bf16[256,512]{1,0:T(8,128)(2,1)S(1)}, u32[]{:S(2)}, u32[]{:S(2)}) collective-permute-start(bf16[256,512]{1,0:T(8,128)(2,1)S(1)} %constant_dynamic-slice_fusion.refs_3_.refs_0_.table), channel_id=1, source_target_pairs={{0,192},{64,0},{128,64},{192,128},{1,193},{65,1},{129,65},{193,129... | collective-permute-start | bytes 786440 | tf_op jit(solution)/shard_map/ppermute | solution.py:248
  16.8 1.6 copy-start.2
  20.8 3.2 copy-start.1
  35.1 114.7 %all-to-all-start = ((bf16[64,128,512]{2,1,0:T(8,128)(2,1)}), bf16[64,128,512]{2,1,0:T(8,128)(2,1)}, u32[]{:S(2)}, u32[]{:S(2)}) async-start(bf16[64,128,512]{2,1,0:T(8,128)(2,1)} %bitcast.42), calls=%async_computation | async-start | bytes 16777216 | tf_op jit(solution)/shard_map/all_to_all | solution.py:256
  190.1 24.0 %collective-permute-start.5 = (bf16[272,512]{1,0:T(8,128)(2,1)S(1)}, bf16[272,512]{1,0:T(8,128)(2,1)S(1)}, u32[]{:S(2)}, u32[]{:S(2)}) collective-permute-start(bf16[272,512]{1,0:T(8,128)(2,1)S(1)} %get-tuple-element.39), channel_id=1, source_target_pairs={{0,192},{64,0},{128,64},{192,128},{1,193},{65,1},{129,65},{193,129... | collective-permute-start | bytes 835592 | tf_op jit(solution)/shard_map/ppermute | solution.py:248
  193.4 20.7 %collective-permute-start.4 = (bf16[272,512]{1,0:T(8,128)(2,1)S(1)}, bf16[272,512]{1,0:T(8,128)(2,1)S(1)}, u32[]{:S(2)}, u32[]{:S(2)}) collective-permute-start(bf16[272,512]{1,0:T(8,128)(2,1)S(1)} %get-tuple-element.40), channel_id=1, source_target_pairs={{0,64},{64,128},{128,192},{192,0},{1,65},{65,129},{129,193},{193,1... | collective-permute-start | bytes 835592 | tf_op jit(solution)/shard_map/ppermute | solution.py:248
  193.4 24.5 %collective-permute-start.3 = (bf16[272,512]{1,0:T(8,128)(2,1)S(1)}, bf16[272,512]{1,0:T(8,128)(2,1)S(1)}, u32[]{:S(2)}, u32[]{:S(2)}) collective-permute-start(bf16[272,512]{1,0:T(8,128)(2,1)S(1)} %get-tuple-element.41), channel_id=1, source_target_pairs={{0,128},{64,192},{128,0},{192,64},{1,129},{65,193},{129,1},{193,65... | collective-permute-start | bytes 835592 | tf_op jit(solution)/shard_map/ppermute | solution.py:248
  218.2 16.2 %collective-permute-start.8 = (bf16[256,512]{1,0:T(8,128)(2,1)S(1)}, bf16[256,512]{1,0:T(8,128)(2,1)S(1)}, u32[]{:S(2)}, u32[]{:S(2)}) collective-permute-start(bf16[256,512]{1,0:T(8,128)(2,1)S(1)} %new_centres.2.refs_3_.refs_0_.table), channel_id=1, source_target_pairs={{0,64},{64,128},{128,192},{192,0},{1,65},{65,129},{129,193},{193,1... | collective-permute-start | bytes 786440 | tf_op jit(solution)/shard_map/ppermute | solution.py:248
  223.1 24.1 %collective-permute-start.7 = (bf16[256,512]{1,0:T(8,128)(2,1)S(1)}, bf16[256,512]{1,0:T(8,128)(2,1)S(1)}, u32[]{:S(2)}, u32[]{:S(2)}) collective-permute-start(bf16[256,512]{1,0:T(8,128)(2,1)S(1)} %new_centres.2.refs_3_.refs_0_.table), channel_id=1, source_target_pairs={{0,128},{64,192},{128,0},{192,64},{1,129},{65,193},{129,1},{193,65... | collective-permute-start | bytes 786440 | tf_op jit(solution)/shard_map/ppermute | solution.py:248
  224.5 23.5 %collective-permute-start.6 = (bf16[256,512]{1,0:T(8,128)(2,1)S(1)}, bf16[256,512]{1,0:T(8,128)(2,1)S(1)}, u32[]{:S(2)}, u32[]{:S(2)}) collective-permute-start(bf16[256,512]{1,0:T(8,128)(2,1)S(1)} %new_centres.2.refs_3_.refs_0_.table), channel_id=1, source_target_pairs={{0,192},{64,0},{128,64},{192,128},{1,193},{65,1},{129,65},{193,129... | collective-permute-start | bytes 786440 | tf_op jit(solution)/shard_map/ppermute | solution.py:248
  280.5 27.3 %collective-permute-start.11 = (bf16[272,512]{1,0:T(8,128)(2,1)S(1)}, bf16[272,512]{1,0:T(8,128)(2,1)S(1)}, u32[]{:S(2)}, u32[]{:S(2)}) collective-permute-start(bf16[272,512]{1,0:T(8,128)(2,1)S(1)} %get-tuple-element.36), channel_id=1, source_target_pairs={{0,192},{64,0},{128,64},{192,128},{1,193},{65,1},{129,65},{193,129... | collective-permute-start | bytes 835592 | tf_op jit(solution)/shard_map/ppermute | solution.py:248
  282.4 25.3 %collective-permute-start.10 = (bf16[272,512]{1,0:T(8,128)(2,1)S(1)}, bf16[272,512]{1,0:T(8,128)(2,1)S(1)}, u32[]{:S(2)}, u32[]{:S(2)}) collective-permute-start(bf16[272,512]{1,0:T(8,128)(2,1)S(1)} %get-tuple-element.37), channel_id=1, source_target_pairs={{0,64},{64,128},{128,192},{192,0},{1,65},{65,129},{129,193},{193,1... | collective-permute-start | bytes 835592 | tf_op jit(solution)/shard_map/ppermute | solution.py:248
  282.9 27.7 %collective-permute-start.9 = (bf16[272,512]{1,0:T(8,128)(2,1)S(1)}, bf16[272,512]{1,0:T(8,128)(2,1)S(1)}, u32[]{:S(2)}, u32[]{:S(2)}) collective-permute-start(bf16[272,512]{1,0:T(8,128)(2,1)S(1)} %get-tuple-element.38), channel_id=1, source_target_pairs={{0,128},{64,192},{128,0},{192,64},{1,129},{65,193},{129,1},{193,65... | collective-permute-start | bytes 835592 | tf_op jit(solution)/shard_map/ppermute | solution.py:248
  311.8 17.6 %all-to-all-start.5 = ((bf16[4,256,512]{2,1,0:T(8,128)(2,1)}), bf16[4,256,512]{2,1,0:T(8,128)(2,1)S(1)}, u32[]{:S(2)}, u32[]{:S(2)}) async-start(bf16[4,256,512]{2,1,0:T(8,128)(2,1)} %new_centres.3), calls=%async_computation.5 | async-start | bytes 2097152 | tf_op jit(solution)/shard_map/all_to_all | solution.py:295

commit v5 on v4

--- a/solution.py
+++ b/solution.py
@@ -70,7 +70,7 @@
             out_specs=pl.BlockSpec((per, PB, D), lambda i, s: (i, 0, 0)),
         ),
         out_shape=jax.ShapeDtypeStruct((SLOTS, PB, D), BF16),
-        compiler_params=pltpu.CompilerParams(vmem_limit_bytes=20 << 20),
+        compiler_params=pltpu.CompilerParams(vmem_limit_bytes=58 << 20),
         name="pack_points",
     )(src, points)
 
@@ -138,9 +138,9 @@
 
 
 def score_kernel(which, me, rows, *refs):
-    tables, out = refs[:-1], refs[-1]
+    tables, previous, out = refs[: len(which)], refs[len(which) : -1], refs[-1]
     lanes = iota((PEERS, LANES), 1) // (CAP * PB)
-    total = jnp.zeros((PEERS, LANES), F32)
+    total = previous[0][...] if previous else jnp.zeros((PEERS, LANES), F32)
     for k, s in enumerate(which):
         label = label_of(me[0], s)
         scores = scores_of(tables[k], rows_of(rows, label), norms_of(tables[k]))
@@ -154,7 +154,8 @@
 
 def score(me, rows, tables):
     out = jax.ShapeDtypeStruct((PEERS, LANES), F32)
-    return call_whole(score_kernel, me, rows, tables, (0, 1, 2, 3), (), out, 2, "score_blocks")
+    partial = call_whole(score_kernel, me, rows, tables, (0, 2, 3), (), out, 2, "score_near")
+    return call_whole(score_kernel, me, rows, tables, (1,), (partial,), out, 2, "score_far")
 
 
 def home_kernel(returned, peer_col, slot_col, peer_row, lse, outward):
@@ -278,8 +279,10 @@
     source, peer, slot = route(candidates)
     outgoing = pack(source, points.reshape(PBD, PB, D))
     where = (peer[:, None], slot[:, None], peer[None, :])
-    outgoing, where, tables = lax.optimization_barrier((outgoing, where, tables_of(own)))
-    rows = keep(exchange(outgoing.reshape(PEERS, LANES, D)))
+    tables = tables_of(own)
+    outgoing, tables[0], tables[2] = lax.optimization_barrier((outgoing, tables[0], tables[2]))
+    rows, where = lax.optimization_barrier((exchange(outgoing.reshape(PEERS, LANES, D)), where))
+    rows = keep(rows)
     for iteration in range(ITERS):
         returned = exchange(score(me, rows, tables))
         lse, outward = home(returned, *where)

time: 331 us -> 321 us (0.970)
  the two profiles are of different devices: /device:TPU:1 before, /device:TPU:32 now
where the time goes in v5:
time: 321 us; the launch traced here: 320 us
  waiting for transfers between devices  186 us (58%)
  blocking collectives  55.5 us (17%)
  starting transfers between devices  41.9 us (13%)
  Pallas kernels  30.6 us (10%)
  local copies, waits for them, and re-layouts  3.28 us (1%)
    all_to_all x1, waiting for transfers between devices, exchange(): return lax.all_to_all(value, GROUP, split_axis=0, concat_axis=0, tiled=True)  106 us
    ppermute x12, waiting for transfers between devices, shifted(): lax.ppermute(value, 'zh', [(i, (i + by) % COPIES) for i in range(COPIES)])  66 us
    all_to_all x4, blocking collectives, exchange(): return lax.all_to_all(value, GROUP, split_axis=0, concat_axis=0, tiled=True)  55.5 us
    ppermute x12, starting transfers between devices, shifted(): lax.ppermute(value, 'zh', [(i, (i + by) % COPIES) for i in range(COPIES)])  29.1 us
    pallas_call x8, Pallas kernels, call_whole(): pl.pallas_call(functools.partial(kernel, which), in_specs=[pl.BlockSpec(m...  17.4 us
    all_to_all x1, waiting for transfers between devices, on_device(): gathered = lax.all_to_all(own, 'x', split_axis=0, concat_axis=0, tiled=True)  13.5 us
    all_to_all x1, starting transfers between devices, exchange(): return lax.all_to_all(value, GROUP, split_axis=0, concat_axis=0, tiled=True)  9.26 us
    pallas_call x1, Pallas kernels, pack(): pl.pallas_call(pack_kernel, grid_spec=pltpu.PrefetchScalarGridSpec(num_sc...  6.5 us
  transfers between devices with their start and end apart: 14, of which 12 were waited for; matrix products, arithmetic and copies ran while one was open for 1% of the time, Pallas kernels for 5%

profile of v5, /device:TPU:32, one launch (start us, length us, event | category | flops | bytes accessed | tf_op | source)
XLA Modules:
  0.0 320.5 jit_solution(6393474454938063236)
XLA Ops:
  0.6 1.2 copy-done
  1.9 5.5 %collective-permute-start = (bf16[256,512]{1,0:T(8,128)(2,1)S(1)}, bf16[256,512]{1,0:T(8,128)(2,1)S(1)}, u32[]{:S(2)}, u32[]{:S(2)}) collective-permute-start(bf16[256,512]{1,0:T(8,128)(2,1)S(1)} %constant_dynamic-slice_fusion.refs_2_.refs_0_.table), channel_id=1, source_target_pairs={{0,192},{64,0},{128,64},{192,128},{1,193},{65,1},{129,65},{193,129... | collective-permute-start | bytes 786440 | tf_op jit(solution)/shard_map/ppermute | solution.py:249
  7.4 1.0 fusion
  8.4 0.7 fusion.8
  9.1 0.1 select_reduce_fusion
  9.2 0.6 broadcast_add_fusion.src
  9.8 6.5 %pack_points.1 = bf16[512,16,512]{2,1,0:T(8,128)(2,1)} custom-call(s32[512]{0:T(512)} %broadcast_add_fusion.src, bf16[128,16,512]{2,1,0:T(8,128)(2,1)} %bitcast.55), custom_call_target="tpu_custom_call" | custom-call | tf_op jit(solution)/shard_map/pack_points/pallas_call | solution.py:64
  16.3 0.8 collective-permute-done.refs_0_
  17.1 5.7 %collective-permute-done.1.refs_1_.refs_2_ = bf16[256,512]{1,0:T(8,128)(2,1)S(1)} collective-permute-done((bf16[256,512]{1,0:T(8,128)(2,1)S(1)}, bf16[256,512]{1,0:T(8,128)(2,1)S(1)}, u32[]{:S(2)}, u32[]{:S(2)}) %collective-permute-start.1) | collective-permute-done | bytes 262176 | tf_op jit(solution)/shard_map/ppermute | solution.py:249
  22.9 9.3 %all-to-all-start = ((bf16[64,128,512]{2,1,0:T(8,128)(2,1)}), bf16[64,128,512]{2,1,0:T(8,128)(2,1)}, u32[]{:S(2)}, u32[]{:S(2)}) async-start(bf16[64,128,512]{2,1,0:T(8,128)(2,1)} %bitcast.53), calls=%async_computation | async-start | bytes 16777216 | tf_op jit(solution)/shard_map/all_to_all | solution.py:257
  32.1 1.6 collective-permute-start.2
  34.2 106.3 %all-to-all-done.source = bf16[64,128,512]{2,1,0:T(8,128)(2,1)} async-done(((bf16[64,128,512]{2,1,0:T(8,128)(2,1)}), bf16[64,128,512]{2,1,0:T(8,128)(2,1)}, u32[]{:S(2)}, u32[]{:S(2)}) %all-to-all-start) | async-done | bytes 8388640 | tf_op jit(solution)/shard_map/all_to_all | solution.py:257
  140.5 3.4 %keep_points.1.rows = bf16[64,128,512]{2,1,0:T(8,128)(2,1)S(1)} custom-call(bf16[64,128,512]{2,1,0:T(8,128)(2,1)} %all-to-all-done.source), custom_call_target="tpu_custom_call" | custom-call | tf_op jit(solution)/shard_map/keep_points/pallas_call | solution.py:124
  143.9 2.4 score_near.2.refs_1_
  146.3 1.2 collective-permute-done.2.refs_0_.refs_1_
  147.5 1.0 score_far.2
  148.5 15.5 %all_to_all.54 = f32[64,1,128]{2,1,0:T(1,128)S(1)} all-to-all(f32[64,1,128]{2,1,0:T(1,128)S(1)} %bitcast.46), channel_id=1, replica_groups=mesh['zh'=4,'zl'=2,'y'=4,'core'=2,'x'=4] {'zl','y','core','x'}, dimensions={0} | all-to-all | bytes 65536 | tf_op jit(solution)/shard_map/all_to_all | solution.py:257
  164.0 1.1 join_halves.2
  165.2 12.1 %all_to_all.55 = f32[64,1,128]{2,1,0:T(1,128)S(1)} all-to-all(f32[64,1,128]{2,1,0:T(1,128)S(1)} %bitcast.52), channel_id=1, replica_groups=mesh['zh'=4,'zl'=2,'y'=4,'core'=2,'x'=4] {'zl','y','core','x'}, dimensions={0} | all-to-all | bytes 65536 | tf_op jit(solution)/shard_map/all_to_all | solution.py:257
  177.3 4.0 %weigh_others.2 = bf16[3,272,512]{2,1,0:T(8,128)(2,1)S(1)} custom-call(s32[1]{0:T(128)} %bitcast.me, bf16[64,128,512]{2,1,0:T(8,128)(2,1)S(1)} %keep_points.1.rows, bf16[256,512]{1,0:T(8,128)(2,1)S(1)} %collective-permute-done.refs_0_, bf16[256,512]{1,0:T(8,128)(2,1)S(1)} %collective-permute-done.2.refs_0_.refs_1_, ...), custom_call_target="tpu_custom_call" | custom-call | flops 3221225472 | bytes 6291456 | tf_op jit(solution)/shard_map/weigh_others/pallas_call | solution.py:102
  181.4 4.5 %collective-permute-start.3 = (bf16[272,512]{1,0:T(8,128)(2,1)S(1)}, bf16[272,512]{1,0:T(8,128)(2,1)S(1)}, u32[]{:S(2)}, u32[]{:S(2)}) collective-permute-start(bf16[272,512]{1,0:T(8,128)(2,1)S(1)} %get-tuple-element.39), channel_id=1, source_target_pairs={{0,128},{64,192},{128,0},{192,64},{1,129},{65,193},{129,1},{193,65... | collective-permute-start | bytes 835592 | tf_op jit(solution)/shard_map/ppermute | solution.py:249
  185.8 4.1 %collective-permute-start.5 = (bf16[272,512]{1,0:T(8,128)(2,1)S(1)}, bf16[272,512]{1,0:T(8,128)(2,1)S(1)}, u32[]{:S(2)}, u32[]{:S(2)}) collective-permute-start(bf16[272,512]{1,0:T(8,128)(2,1)S(1)} %get-tuple-element.37), channel_id=1, source_target_pairs={{0,192},{64,0},{128,64},{192,128},{1,193},{65,1},{129,65},{193,129... | collective-permute-start | bytes 835592 | tf_op jit(solution)/shard_map/ppermute | solution.py:249
  190.0 1.4 weigh_own.2
  191.3 5.0 %collective-permute-done.3.m0 = bf16[272,512]{1,0:T(8,128)(2,1)S(1)} collective-permute-done((bf16[272,512]{1,0:T(8,128)(2,1)S(1)}, bf16[272,512]{1,0:T(8,128)(2,1)S(1)}, u32[]{:S(2)}, u32[]{:S(2)}) %collective-permute-start.3) | collective-permute-done | bytes 278560 | tf_op jit(solution)/shard_map/ppermute | solution.py:249
  196.3 9.9 %collective-permute-done.4.m1 = bf16[272,512]{1,0:T(8,128)(2,1)S(1)} collective-permute-done((bf16[272,512]{1,0:T(8,128)(2,1)S(1)}, bf16[272,512]{1,0:T(8,128)(2,1)S(1)}, u32[]{:S(2)}, u32[]{:S(2)}) %collective-permute-start.4) | collective-permute-done | bytes 278560 | tf_op jit(solution)/shard_map/ppermute | solution.py:249
  206.2 0.2 new_centres.2.refs_2_.refs_0_.table
  206.5 2.4 collective-permute-start.6
  208.8 0.6 collective-permute-start.8
  209.5 2.9 collective-permute-start.7
  212.4 14.2 %collective-permute-done.6.refs_0_ = bf16[256,512]{1,0:T(8,128)(2,1)S(1)} collective-permute-done((bf16[256,512]{1,0:T(8,128)(2,1)S(1)}, bf16[256,512]{1,0:T(8,128)(2,1)S(1)}, u32[]{:S(2)}, u32[]{:S(2)}) %collective-permute-start.6) | collective-permute-done | bytes 262176 | tf_op jit(solution)/shard_map/ppermute | solution.py:249
  226.6 2.4 score_near.3.refs_1_
  229.0 6.5 %collective-permute-done.7.refs_0_.refs_1_ = bf16[256,512]{1,0:T(8,128)(2,1)S(1)} collective-permute-done((bf16[256,512]{1,0:T(8,128)(2,1)S(1)}, bf16[256,512]{1,0:T(8,128)(2,1)S(1)}, u32[]{:S(2)}, u32[]{:S(2)}) %collective-permute-start.7) | collective-permute-done | bytes 262176 | tf_op jit(solution)/shard_map/ppermute | solution.py:249
  235.5 1.0 score_far.3
  236.4 15.8 %all_to_all.56 = f32[64,1,128]{2,1,0:T(1,128)S(1)} all-to-all(f32[64,1,128]{2,1,0:T(1,128)S(1)} %bitcast.47), channel_id=1, replica_groups=mesh['zh'=4,'zl'=2,'y'=4,'core'=2,'x'=4] {'zl','y','core','x'}, dimensions={0} | all-to-all | bytes 65536 | tf_op jit(solution)/shard_map/all_to_all | solution.py:257
  252.2 0.7 join_halves.3
  252.9 12.2 %all_to_all.57 = f32[64,1,128]{2,1,0:T(1,128)S(1)} all-to-all(f32[64,1,128]{2,1,0:T(1,128)S(1)} %bitcast.51), channel_id=1, replica_groups=mesh['zh'=4,'zl'=2,'y'=4,'core'=2,'x'=4] {'zl','y','core','x'}, dimensions={0} | all-to-all | bytes 65536 | tf_op jit(solution)/shard_map/all_to_all | solution.py:257
  265.0 3.9 %weigh_others.3 = bf16[3,272,512]{2,1,0:T(8,128)(2,1)S(1)} custom-call(s32[1]{0:T(128)} %bitcast.me, bf16[64,128,512]{2,1,0:T(8,128)(2,1)S(1)} %keep_points.1.rows, bf16[256,512]{1,0:T(8,128)(2,1)S(1)} %collective-permute-done.6.refs_0_, bf16[256,512]{1,0:T(8,128)(2,1)S(1)} %collective-permute-done.7.refs_0_.refs_1_, ...), custom_call_target="tpu_custom_call" | custom-call | flops 3221225472 | bytes 6291456 | tf_op jit(solution)/shard_map/weigh_others/pallas_call | solution.py:102
  269.2 4.1 %collective-permute-start.11 = (bf16[272,512]{1,0:T(8,128)(2,1)S(1)}, bf16[272,512]{1,0:T(8,128)(2,1)S(1)}, u32[]{:S(2)}, u32[]{:S(2)}) collective-permute-start(bf16[272,512]{1,0:T(8,128)(2,1)S(1)} %get-tuple-element.34), channel_id=1, source_target_pairs={{0,192},{64,0},{128,64},{192,128},{1,193},{65,1},{129,65},{193,129... | collective-permute-start | bytes 835592 | tf_op jit(solution)/shard_map/ppermute | solution.py:249
  273.3 3.2 %collective-permute-start.9 = (bf16[272,512]{1,0:T(8,128)(2,1)S(1)}, bf16[272,512]{1,0:T(8,128)(2,1)S(1)}, u32[]{:S(2)}, u32[]{:S(2)}) collective-permute-start(bf16[272,512]{1,0:T(8,128)(2,1)S(1)} %get-tuple-element.36), channel_id=1, source_target_pairs={{0,128},{64,192},{128,0},{192,64},{1,129},{65,193},{129,1},{193,65... | collective-permute-start | bytes 835592 | tf_op jit(solution)/shard_map/ppermute | solution.py:249
  276.5 1.4 weigh_own.3
  277.9 7.6 %collective-permute-done.10.m1 = bf16[272,512]{1,0:T(8,128)(2,1)S(1)} collective-permute-done((bf16[272,512]{1,0:T(8,128)(2,1)S(1)}, bf16[272,512]{1,0:T(8,128)(2,1)S(1)}, u32[]{:S(2)}, u32[]{:S(2)}) %collective-permute-start.10) | collective-permute-done | bytes 278560 | tf_op jit(solution)/shard_map/ppermute | solution.py:249
  285.5 6.7 %collective-permute-done.11.m2 = bf16[272,512]{1,0:T(8,128)(2,1)S(1)} collective-permute-done((bf16[272,512]{1,0:T(8,128)(2,1)S(1)}, bf16[272,512]{1,0:T(8,128)(2,1)S(1)}, u32[]{:S(2)}, u32[]{:S(2)}) %collective-permute-start.11) | collective-permute-done | bytes 278560 | tf_op jit(solution)/shard_map/ppermute | solution.py:249
  292.2 8.4 %collective-permute-done.9.m0 = bf16[272,512]{1,0:T(8,128)(2,1)S(1)} collective-permute-done((bf16[272,512]{1,0:T(8,128)(2,1)S(1)}, bf16[272,512]{1,0:T(8,128)(2,1)S(1)}, u32[]{:S(2)}, u32[]{:S(2)}) %collective-permute-start.9) | collective-permute-done | bytes 278560 | tf_op jit(solution)/shard_map/ppermute | solution.py:249
  300.6 1.2 new_centres.3
  301.8 3.5 %all-to-all-start.5 = ((bf16[4,256,512]{2,1,0:T(8,128)(2,1)}), bf16[4,256,512]{2,1,0:T(8,128)(2,1)S(1)}, u32[]{:S(2)}, u32[]{:S(2)}) async-start(bf16[4,256,512]{2,1,0:T(8,128)(2,1)} %new_centres.3), calls=%async_computation.5 | async-start | bytes 2097152 | tf_op jit(solution)/shard_map/all_to_all | solution.py:298
  305.3 0.7 reshape.246
  306.0 13.5 %all-to-all-done.5 = bf16[4,256,512]{2,1,0:T(8,128)(2,1)S(1)} async-done(((bf16[4,256,512]{2,1,0:T(8,128)(2,1)}), bf16[4,256,512]{2,1,0:T(8,128)(2,1)S(1)}, u32[]{:S(2)}, u32[]{:S(2)}) %all-to-all-start.5) | async-done | bytes 1048608 | tf_op jit(solution)/shard_map/all_to_all | solution.py:298
  319.5 1.0 copy.29
  (16 shorter events, 0.6 us)
Async XLA Ops:
  0.6 1.2 copy-start
  1.9 15.3 %collective-permute-start = (bf16[256,512]{1,0:T(8,128)(2,1)S(1)}, bf16[256,512]{1,0:T(8,128)(2,1)S(1)}, u32[]{:S(2)}, u32[]{:S(2)}) collective-permute-start(bf16[256,512]{1,0:T(8,128)(2,1)S(1)} %constant_dynamic-slice_fusion.refs_2_.refs_0_.table), channel_id=1, source_target_pairs={{0,192},{64,0},{128,64},{192,128},{1,193},{65,1},{129,65},{193,129... | collective-permute-start | bytes 786440 | tf_op jit(solution)/shard_map/ppermute | solution.py:249
  7.4 15.5 %collective-permute-start.1 = (bf16[256,512]{1,0:T(8,128)(2,1)S(1)}, bf16[256,512]{1,0:T(8,128)(2,1)S(1)}, u32[]{:S(2)}, u32[]{:S(2)}) collective-permute-start(bf16[256,512]{1,0:T(8,128)(2,1)S(1)} %constant_dynamic-slice_fusion.refs_2_.refs_0_.table), channel_id=1, source_target_pairs={{0,64},{64,128},{128,192},{192,0},{1,65},{65,129},{129,193},{193,1... | collective-permute-start | bytes 786440 | tf_op jit(solution)/shard_map/ppermute | solution.py:249
  22.9 11.1 %copy-start.1 = (s32[128,2]{0,1:T(2,128)S(1)}, s32[128,2]{0,1:T(2,128)}, u32[]{:S(2)}) copy-start(s32[128,2]{0,1:T(2,128)} %param.5) | copy-start | bytes 3076
  22.9 117.6 %all-to-all-start = ((bf16[64,128,512]{2,1,0:T(8,128)(2,1)}), bf16[64,128,512]{2,1,0:T(8,128)(2,1)}, u32[]{:S(2)}, u32[]{:S(2)}) async-start(bf16[64,128,512]{2,1,0:T(8,128)(2,1)} %bitcast.53), calls=%async_computation | async-start | bytes 16777216 | tf_op jit(solution)/shard_map/all_to_all | solution.py:257
  32.1 115.4 %collective-permute-start.2 = (bf16[256,512]{1,0:T(8,128)(2,1)S(1)}, bf16[256,512]{1,0:T(8,128)(2,1)S(1)}, u32[]{:S(2)}, u32[]{:S(2)}) collective-permute-start(bf16[256,512]{1,0:T(8,128)(2,1)S(1)} %constant_dynamic-slice_fusion.refs_2_.refs_0_.table), channel_id=1, source_target_pairs={{0,128},{64,192},{128,0},{192,64},{1,129},{65,193},{129,1},{193,65... | collective-permute-start | bytes 786440 | tf_op jit(solution)/shard_map/ppermute | solution.py:249
  181.4 14.9 %collective-permute-start.3 = (bf16[272,512]{1,0:T(8,128)(2,1)S(1)}, bf16[272,512]{1,0:T(8,128)(2,1)S(1)}, u32[]{:S(2)}, u32[]{:S(2)}) collective-permute-start(bf16[272,512]{1,0:T(8,128)(2,1)S(1)} %get-tuple-element.39), channel_id=1, source_target_pairs={{0,128},{64,192},{128,0},{192,64},{1,129},{65,193},{129,1},{193,65... | collective-permute-start | bytes 835592 | tf_op jit(solution)/shard_map/ppermute | solution.py:249
  185.8 20.4 %collective-permute-start.4 = (bf16[272,512]{1,0:T(8,128)(2,1)S(1)}, bf16[272,512]{1,0:T(8,128)(2,1)S(1)}, u32[]{:S(2)}, u32[]{:S(2)}) collective-permute-start(bf16[272,512]{1,0:T(8,128)(2,1)S(1)} %get-tuple-element.38), channel_id=1, source_target_pairs={{0,64},{64,128},{128,192},{192,0},{1,65},{65,129},{129,193},{193,1... | collective-permute-start | bytes 835592 | tf_op jit(solution)/shard_map/ppermute | solution.py:249
  185.8 20.4 %collective-permute-start.5 = (bf16[272,512]{1,0:T(8,128)(2,1)S(1)}, bf16[272,512]{1,0:T(8,128)(2,1)S(1)}, u32[]{:S(2)}, u32[]{:S(2)}) collective-permute-start(bf16[272,512]{1,0:T(8,128)(2,1)S(1)} %get-tuple-element.37), channel_id=1, source_target_pairs={{0,192},{64,0},{128,64},{192,128},{1,193},{65,1},{129,65},{193,129... | collective-permute-start | bytes 835592 | tf_op jit(solution)/shard_map/ppermute | solution.py:249
  206.5 20.1 %collective-permute-start.6 = (bf16[256,512]{1,0:T(8,128)(2,1)S(1)}, bf16[256,512]{1,0:T(8,128)(2,1)S(1)}, u32[]{:S(2)}, u32[]{:S(2)}) collective-permute-start(bf16[256,512]{1,0:T(8,128)(2,1)S(1)} %new_centres.2.refs_2_.refs_0_.table), channel_id=1, source_target_pairs={{0,192},{64,0},{128,64},{192,128},{1,193},{65,1},{129,65},{193,129... | collective-permute-start | bytes 786440 | tf_op jit(solution)/shard_map/ppermute | solution.py:249
  208.8 17.8 %collective-permute-start.8 = (bf16[256,512]{1,0:T(8,128)(2,1)S(1)}, bf16[256,512]{1,0:T(8,128)(2,1)S(1)}, u32[]{:S(2)}, u32[]{:S(2)}) collective-permute-start(bf16[256,512]{1,0:T(8,128)(2,1)S(1)} %new_centres.2.refs_2_.refs_0_.table), channel_id=1, source_target_pairs={{0,64},{64,128},{128,192},{192,0},{1,65},{65,129},{129,193},{193,1... | collective-permute-start | bytes 786440 | tf_op jit(solution)/shard_map/ppermute | solution.py:249
  209.5 26.0 %collective-permute-start.7 = (bf16[256,512]{1,0:T(8,128)(2,1)S(1)}, bf16[256,512]{1,0:T(8,128)(2,1)S(1)}, u32[]{:S(2)}, u32[]{:S(2)}) collective-permute-start(bf16[256,512]{1,0:T(8,128)(2,1)S(1)} %new_centres.2.refs_2_.refs_0_.table), channel_id=1, source_target_pairs={{0,128},{64,192},{128,0},{192,64},{1,129},{65,193},{129,1},{193,65... | collective-permute-start | bytes 786440 | tf_op jit(solution)/shard_map/ppermute | solution.py:249
  269.1 16.4 %collective-permute-start.10 = (bf16[272,512]{1,0:T(8,128)(2,1)S(1)}, bf16[272,512]{1,0:T(8,128)(2,1)S(1)}, u32[]{:S(2)}, u32[]{:S(2)}) collective-permute-start(bf16[272,512]{1,0:T(8,128)(2,1)S(1)} %get-tuple-element.35), channel_id=1, source_target_pairs={{0,64},{64,128},{128,192},{192,0},{1,65},{65,129},{129,193},{193,1... | collective-permute-start | bytes 835592 | tf_op jit(solution)/shard_map/ppermute | solution.py:249
  269.2 23.1 %collective-permute-start.11 = (bf16[272,512]{1,0:T(8,128)(2,1)S(1)}, bf16[272,512]{1,0:T(8,128)(2,1)S(1)}, u32[]{:S(2)}, u32[]{:S(2)}) collective-permute-start(bf16[272,512]{1,0:T(8,128)(2,1)S(1)} %get-tuple-element.34), channel_id=1, source_target_pairs={{0,192},{64,0},{128,64},{192,128},{1,193},{65,1},{129,65},{193,129... | collective-permute-start | bytes 835592 | tf_op jit(solution)/shard_map/ppermute | solution.py:249
  273.3 27.3 %collective-permute-start.9 = (bf16[272,512]{1,0:T(8,128)(2,1)S(1)}, bf16[272,512]{1,0:T(8,128)(2,1)S(1)}, u32[]{:S(2)}, u32[]{:S(2)}) collective-permute-start(bf16[272,512]{1,0:T(8,128)(2,1)S(1)} %get-tuple-element.36), channel_id=1, source_target_pairs={{0,128},{64,192},{128,0},{192,64},{1,129},{65,193},{129,1},{193,65... | collective-permute-start | bytes 835592 | tf_op jit(solution)/shard_map/ppermute | solution.py:249
  301.8 17.7 %all-to-all-start.5 = ((bf16[4,256,512]{2,1,0:T(8,128)(2,1)}), bf16[4,256,512]{2,1,0:T(8,128)(2,1)S(1)}, u32[]{:S(2)}, u32[]{:S(2)}) async-start(bf16[4,256,512]{2,1,0:T(8,128)(2,1)} %new_centres.3), calls=%async_computation.5 | async-start | bytes 2097152 | tf_op jit(solution)/shard_map/all_to_all | solution.py:298

commit v6 on v5

--- a/solution.py
+++ b/solution.py
@@ -22,8 +22,8 @@
 ENTRIES = 2 * PBD
 COLS = PEERS * CAP * PB
 MSG = CB + 16
-ORDER = (2, 1, 3)
 LIMIT = 28
+QUARTERS = 4
 EMPTY = 1e30
 GROUP = ("zl", "y", "core", "x")
 BETA = 1.0 / math.sqrt(D)
@@ -105,31 +105,8 @@
         + [pl.BlockSpec(memory_space=pltpu.VMEM)] * (1 + len(which) + len(extra)),
         out_shape=outs,
         compiler_params=pltpu.CompilerParams(vmem_limit_bytes=LIMIT << 20),
-        cost_estimate=pl.CostEstimate(
-            flops=len(which) * flops * COLS * CB * D,
-            bytes_accessed=len(which) * COLS * D * 2,
-            transcendentals=len(which) * COLS * CB,
-        ),
         name=name,
     )(me, rows, *[tables[s] for s in which], *extra)
-
-
-def keep_kernel(source, kept, done):
-    copy = pltpu.make_async_copy(source, kept, done)
-    copy.start()
-    copy.wait()
-
-
-def keep(rows):
-    return pl.pallas_call(
-        keep_kernel,
-        in_specs=[pl.BlockSpec(memory_space=pl.ANY)],
-        out_specs=pl.BlockSpec(memory_space=pltpu.VMEM),
-        out_shape=jax.ShapeDtypeStruct(rows.shape, rows.dtype),
-        scratch_shapes=[pltpu.SemaphoreType.DMA],
-        compiler_params=pltpu.CompilerParams(vmem_limit_bytes=LIMIT << 20),
-        name="keep_points",
-    )(rows)
 
 
 def rows_of(rows, label):
@@ -137,24 +114,68 @@
     return part.reshape(COLS, D)
 
 
+def scored(total, table, norms, block, label):
+    scores = scores_of(table, block, norms)
+    highest = jnp.max(scores, axis=0, keepdims=True)
+    partial = highest + jnp.log2(jnp.sum(jnp.exp2(scores - highest), axis=0, keepdims=True))
+    partial = partial * LN2
+    tiles = [jnp.broadcast_to(partial[:, c : c + LANES], (COPIES, LANES)) for c in range(0, block.shape[0], LANES)]
+    lanes = iota(total.shape, 1) // (CAP * PB)
+    return jnp.where(lanes == label, turned_by(jnp.concatenate(tiles, axis=0), label, -1), total)
+
+
 def score_kernel(which, me, rows, *refs):
     tables, previous, out = refs[: len(which)], refs[len(which) : -1], refs[-1]
-    lanes = iota((PEERS, LANES), 1) // (CAP * PB)
     total = previous[0][...] if previous else jnp.zeros((PEERS, LANES), F32)
     for k, s in enumerate(which):
         label = label_of(me[0], s)
-        scores = scores_of(tables[k], rows_of(rows, label), norms_of(tables[k]))
-        highest = jnp.max(scores, axis=0, keepdims=True)
-        partial = highest + jnp.log2(jnp.sum(jnp.exp2(scores - highest), axis=0, keepdims=True))
-        partial = partial * LN2
-        tiles = [jnp.broadcast_to(partial[:, c : c + LANES], (COPIES, LANES)) for c in range(0, COLS, LANES)]
-        total = jnp.where(lanes == label, turned_by(jnp.concatenate(tiles, axis=0), label, -1), total)
+        total = scored(total, tables[k], norms_of(tables[k]), rows_of(rows, label), label)
     out[...] = total
 
 
-def score(me, rows, tables):
+def keep_kernel(which, me, source, *refs):
+    tables, (kept, out, done) = refs[: len(which)], refs[len(which) :]
+    per = PEERS // QUARTERS
+    parts = [pl.ds(i * per, per) for i in range(QUARTERS)]
+    copies = [pltpu.make_async_copy(source.at[p], kept.at[p], done.at[i]) for i, p in enumerate(parts)]
+    for copy in copies:
+        copy.start()
+    norms = [norms_of(table) for table in tables]
+    for copy, part in zip(copies, parts):
+        copy.wait()
+        total = jnp.zeros((per, LANES), F32)
+        for k, s in enumerate(which):
+            label = label_of(me[0], s)
+            width = CAP * PB
+            block = kept[part, pl.ds(pl.multiple_of(label * width, width), width), :]
+            total = scored(total, tables[k], norms[k], block.reshape(per * width, D), label)
+        out[part, :] = total
+
+
+def score_kept(me, received, tables):
+    which = (0, 2, 3)
+    vmem = pl.BlockSpec(memory_space=pltpu.VMEM)
+    return pl.pallas_call(
+        functools.partial(keep_kernel, which),
+        in_specs=[pl.BlockSpec(memory_space=pltpu.SMEM), pl.BlockSpec(memory_space=pl.ANY)] + [vmem] * len(which),
+        out_specs=(vmem, vmem),
+        out_shape=(
+            jax.ShapeDtypeStruct(received.shape, received.dtype),
+            jax.ShapeDtypeStruct((PEERS, LANES), F32),
+        ),
+        scratch_shapes=[pltpu.SemaphoreType.DMA((QUARTERS,))],
+        compiler_params=pltpu.CompilerParams(vmem_limit_bytes=LIMIT << 20),
+        name="keep_and_score",
+    )(me, received, *[tables[s] for s in which])
+
+
+def score_near(me, rows, tables):
     out = jax.ShapeDtypeStruct((PEERS, LANES), F32)
-    partial = call_whole(score_kernel, me, rows, tables, (0, 2, 3), (), out, 2, "score_near")
+    return call_whole(score_kernel, me, rows, tables, (0, 2, 3), (), out, 2, "score_near")
+
+
+def score_far(me, rows, tables, partial):
+    out = jax.ShapeDtypeStruct((PEERS, LANES), F32)
     return call_whole(score_kernel, me, rows, tables, (1,), (partial,), out, 2, "score_far")
 
 
@@ -220,14 +241,29 @@
     return call_whole(weigh_kernel, me, rows, tables, (3,), (inward,), outs, 4, "weigh_own")
 
 
-def weigh_others(me, rows, tables, inward):
-    out = jax.ShapeDtypeStruct((COPIES - 1, MSG, D), BF16)
-    return call_whole(weigh_kernel, me, rows, tables, (0, 1, 2), (inward,), out, 4, "weigh_others")
-
-
-def finish_kernel(own_sum, own_mass, m0, m1, m2, table, out):
+def weigh_others(me, rows, tables, which, inward):
+    out = jax.ShapeDtypeStruct((len(which), MSG, D), BF16)
+    return call_whole(weigh_kernel, me, rows, tables, which, (inward,), out, 4, "weigh_others")
+
+
+def merge_kernel(own_sum, own_mass, message, total, mass):
+    total[...] = own_sum[...] + message[:CB].astype(F32)
+    pair = message[CB:].astype(F32)[:1]
+    mass[...] = own_mass[...] + pair[:, :CB] + pair[:, CB:]
+
+
+def merge(own_sum, own_mass, message):
+    return pl.pallas_call(
+        merge_kernel,
+        out_shape=(jax.ShapeDtypeStruct((CB, D), F32), jax.ShapeDtypeStruct((8, CB), F32)),
+        compiler_params=pltpu.CompilerParams(vmem_limit_bytes=16 << 20),
+        name="merge_far",
+    )(own_sum, own_mass, message)
+
+
+def finish_kernel(own_sum, own_mass, m1, m2, table, out):
     total, mass = own_sum[...], own_mass[:1]
-    for message in (m0, m1, m2):
+    for message in (m1, m2):
         total += message[:CB].astype(F32)
         pair = message[CB:].astype(F32)[:1]
         mass += pair[:, :CB] + pair[:, CB:]
@@ -282,19 +318,27 @@
     tables = tables_of(own)
     outgoing, tables[0], tables[2] = lax.optimization_barrier((outgoing, tables[0], tables[2]))
     rows, where = lax.optimization_barrier((exchange(outgoing.reshape(PEERS, LANES, D)), where))
-    rows = keep(rows)
+    rows, partial = score_kept(me, rows, tables)
     for iteration in range(ITERS):
-        returned = exchange(score(me, rows, tables))
+        returned = exchange(score_far(me, rows, tables, partial))
         lse, outward = home(returned, *where)
         inward = exchange(outward)
         last = iteration == ITERS - 1
-        messages = weigh_others(me, rows, tables, inward)
-        arrived = [shifted(messages[n - 1], n) for n in ORDER]
-        messages, inward = lax.optimization_barrier((messages, inward))
-        own_sum, own_mass = weigh_own(me, rows, tables, inward)
-        own = finish(own_sum, own_mass, arrived, own, (COPIES,) if last else ())
+        if last:
+            far = weigh_others(me, rows, tables, (1,), inward)
+            arrived = shifted(far[0], 2)
+            far, inward = lax.optimization_barrier((far, inward))
+            near = weigh_others(me, rows, tables, (0, 2), inward)
+        else:
+            near = weigh_others(me, rows, tables, (0, 1, 2), inward)
+            arrived = shifted(near[1], 2)
+        near_arrived = [shifted(near[0], 1), shifted(near[-1], 3)]
+        near, inward = lax.optimization_barrier((near, inward))
+        own_sum, own_mass = merge(*weigh_own(me, rows, tables, inward), arrived)
+        own = finish(own_sum, own_mass, near_arrived, own, (COPIES,) if last else ())
         if not last:
             tables = tables_of(own)
+            partial = score_near(me, rows, tables)
     gathered = lax.all_to_all(own, "x", split_axis=0, concat_axis=0, tiled=True)
     return gathered.reshape(COPIES * CB, D), lse[:, :PB].reshape(-1)
 

time: 321 us -> 317 us (0.988)
  the two profiles are of different devices: /device:TPU:32 before, /device:TPU:1 now
where the time goes in v6:
time: 317 us; the launch traced here: 316 us
  waiting for transfers between devices  177 us (56%)
  blocking collectives  58.5 us (18%)
  starting transfers between devices  43.8 us (14%)
  Pallas kernels  30.1 us (9%)
  local copies, waits for them, and re-layouts  3.26 us (1%)
    all_to_all x1, waiting for transfers between devices, exchange(): return lax.all_to_all(value, GROUP, split_axis=0, concat_axis=0, tiled=True)  108 us
    all_to_all x4, blocking collectives, exchange(): return lax.all_to_all(value, GROUP, split_axis=0, concat_axis=0, tiled=True)  58.5 us
    ppermute x12, waiting for transfers between devices, shifted(): lax.ppermute(value, 'zh', [(i, (i + by) % COPIES) for i in range(COPIES)])  55.2 us
    ppermute x12, starting transfers between devices, shifted(): lax.ppermute(value, 'zh', [(i, (i + by) % COPIES) for i in range(COPIES)])  26.5 us
    pallas_call x8, Pallas kernels, call_whole(): pl.pallas_call(functools.partial(kernel, which), in_specs=[pl.BlockSpec(m...  15.1 us
    all_to_all x1, waiting for transfers between devices, on_device(): gathered = lax.all_to_all(own, 'x', split_axis=0, concat_axis=0, tiled=True)  14 us
    all_to_all x1, starting transfers between devices, exchange(): return lax.all_to_all(value, GROUP, split_axis=0, concat_axis=0, tiled=True)  13.8 us
    pallas_call x1, Pallas kernels, pack(): pl.pallas_call(pack_kernel, grid_spec=pltpu.PrefetchScalarGridSpec(num_sc...  6.53 us
  transfers between devices with their start and end apart: 14, of which 10 were waited for; matrix products, arithmetic and copies ran while one was open for 1% of the time, Pallas kernels for 6%

profile of v6, /device:TPU:1, one launch (start us, length us, event | category | flops | bytes accessed | tf_op | source)
XLA Modules:
  0.0 316.0 jit_solution(1783717505909988900)
XLA Ops:
  0.6 1.2 copy-done
  1.9 6.9 %collective-permute-start = (bf16[256,512]{1,0:T(8,128)(2,1)S(1)}, bf16[256,512]{1,0:T(8,128)(2,1)S(1)}, u32[]{:S(2)}, u32[]{:S(2)}) collective-permute-start(bf16[256,512]{1,0:T(8,128)(2,1)S(1)} %constant_dynamic-slice_fusion.refs_2_.refs_0_.table), channel_id=1, source_target_pairs={{0,192},{64,0},{128,64},{192,128},{1,193},{65,1},{129,65},{193,129... | collective-permute-start | bytes 786440 | tf_op jit(solution)/shard_map/ppermute | solution.py:285
  8.8 1.0 fusion
  9.8 0.7 fusion.8
  10.5 0.1 select_reduce_fusion
  10.7 0.6 broadcast_add_fusion.src
  11.3 6.5 %pack_points.1 = bf16[512,16,512]{2,1,0:T(8,128)(2,1)} custom-call(s32[512]{0:T(512)} %broadcast_add_fusion.src, bf16[128,16,512]{2,1,0:T(8,128)(2,1)} %bitcast.56), custom_call_target="tpu_custom_call" | custom-call | tf_op jit(solution)/shard_map/pack_points/pallas_call | solution.py:64
  17.8 1.8 collective-permute-done.1.refs_1_.refs_2_
  19.6 13.8 %all-to-all-start = ((bf16[64,128,512]{2,1,0:T(8,128)(2,1)}), bf16[64,128,512]{2,1,0:T(8,128)(2,1)}, u32[]{:S(2)}, u32[]{:S(2)}) async-start(bf16[64,128,512]{2,1,0:T(8,128)(2,1)} %bitcast.54), calls=%async_computation | async-start | bytes 16777216 | tf_op jit(solution)/shard_map/all_to_all | solution.py:293
  33.4 1.4 collective-permute-start.2
  34.9 0.1 copy.19
  35.2 107.8 %all-to-all-done.source = bf16[64,128,512]{2,1,0:T(8,128)(2,1)} async-done(((bf16[64,128,512]{2,1,0:T(8,128)(2,1)}), bf16[64,128,512]{2,1,0:T(8,128)(2,1)}, u32[]{:S(2)}, u32[]{:S(2)}) %all-to-all-start) | async-done | bytes 8388640 | tf_op jit(solution)/shard_map/all_to_all | solution.py:293
  143.0 5.1 %keep_and_score.1 = (bf16[64,128,512]{2,1,0:T(8,128)(2,1)S(1)}, f32[64,128]{1,0:T(8,128)S(1)}) custom-call(s32[1]{0:T(128)} %bitcast.me, bf16[64,128,512]{2,1,0:T(8,128)(2,1)} %all-to-all-done.source, bf16[256,512]{1,0:T(8,128)(2,1)S(1)} %collective-permute-done.refs_0_, bf16[256,512]{1,0:T(8,128)(2,1)S(1)} %collective-permute-done.1.refs_1_.refs_2_, ...), custom_call_target="tpu_custom_call" | custom-call | tf_op jit(solution)/shard_map/keep_and_score/pallas_call | solution.py:158
  148.2 1.0 score_far.2
  149.2 17.3 %all_to_all.54 = f32[64,1,128]{2,1,0:T(1,128)S(1)} all-to-all(f32[64,1,128]{2,1,0:T(1,128)S(1)} %bitcast.47), channel_id=1, replica_groups=mesh['zh'=4,'zl'=2,'y'=4,'core'=2,'x'=4] {'zl','y','core','x'}, dimensions={0} | all-to-all | bytes 65536 | tf_op jit(solution)/shard_map/all_to_all | solution.py:293
  166.5 1.1 join_halves.2
  167.6 12.1 %all_to_all.55 = f32[64,1,128]{2,1,0:T(1,128)S(1)} all-to-all(f32[64,1,128]{2,1,0:T(1,128)S(1)} %bitcast.53), channel_id=1, replica_groups=mesh['zh'=4,'zl'=2,'y'=4,'core'=2,'x'=4] {'zl','y','core','x'}, dimensions={0} | all-to-all | bytes 65536 | tf_op jit(solution)/shard_map/all_to_all | solution.py:293
  179.8 4.0 %weigh_others.3 = bf16[3,272,512]{2,1,0:T(8,128)(2,1)S(1)} custom-call(s32[1]{0:T(128)} %bitcast.me, bf16[64,128,512]{2,1,0:T(8,128)(2,1)S(1)} %get-tuple-element.29.rows, bf16[256,512]{1,0:T(8,128)(2,1)S(1)} %collective-permute-done.refs_0_, bf16[256,512]{1,0:T(8,128)(2,1)S(1)} %collective-permute-done.2.refs_0_.refs_1_, ...), custom_call_target="tpu_custom_call" | custom-call | tf_op jit(solution)/shard_map/weigh_others/pallas_call | solution.py:102
  183.8 4.2 %collective-permute-start.3 = (bf16[272,512]{1,0:T(8,128)(2,1)S(1)}, bf16[272,512]{1,0:T(8,128)(2,1)S(1)}, u32[]{:S(2)}, u32[]{:S(2)}) collective-permute-start(bf16[272,512]{1,0:T(8,128)(2,1)S(1)} %get-tuple-element.50), channel_id=1, source_target_pairs={{0,128},{64,192},{128,0},{192,64},{1,129},{65,193},{129,1},{193,65... | collective-permute-start | bytes 835592 | tf_op jit(solution)/shard_map/ppermute | solution.py:285
  188.0 3.6 %collective-permute-start.5 = (bf16[272,512]{1,0:T(8,128)(2,1)S(1)}, bf16[272,512]{1,0:T(8,128)(2,1)S(1)}, u32[]{:S(2)}, u32[]{:S(2)}) collective-permute-start(bf16[272,512]{1,0:T(8,128)(2,1)S(1)} %get-tuple-element.48), channel_id=1, source_target_pairs={{0,192},{64,0},{128,64},{192,128},{1,193},{65,1},{129,65},{193,129... | collective-permute-start | bytes 835592 | tf_op jit(solution)/shard_map/ppermute | solution.py:285
  191.6 1.4 weigh_own.2
  193.0 8.5 %collective-permute-done.3.message = bf16[272,512]{1,0:T(8,128)(2,1)S(1)} collective-permute-done((bf16[272,512]{1,0:T(8,128)(2,1)S(1)}, bf16[272,512]{1,0:T(8,128)(2,1)S(1)}, u32[]{:S(2)}, u32[]{:S(2)}) %collective-permute-start.3) | collective-permute-done | bytes 278560 | tf_op jit(solution)/shard_map/ppermute | solution.py:285
  201.5 8.8 %collective-permute-done.4.m1 = bf16[272,512]{1,0:T(8,128)(2,1)S(1)} collective-permute-done((bf16[272,512]{1,0:T(8,128)(2,1)S(1)}, bf16[272,512]{1,0:T(8,128)(2,1)S(1)}, u32[]{:S(2)}, u32[]{:S(2)}) %collective-permute-start.4) | collective-permute-done | bytes 278560 | tf_op jit(solution)/shard_map/ppermute | solution.py:285
  210.3 0.2 new_centres.2.refs_2_.refs_0_.table
  210.5 0.4 collective-permute-start.6
  210.9 2.1 collective-permute-start.7
  212.9 1.9 collective-permute-start.8
  214.9 13.8 %collective-permute-done.6.refs_0_ = bf16[256,512]{1,0:T(8,128)(2,1)S(1)} collective-permute-done((bf16[256,512]{1,0:T(8,128)(2,1)S(1)}, bf16[256,512]{1,0:T(8,128)(2,1)S(1)}, u32[]{:S(2)}, u32[]{:S(2)}) %collective-permute-start.6) | collective-permute-done | bytes 262176 | tf_op jit(solution)/shard_map/ppermute | solution.py:285
  228.7 2.4 score_near.1.refs_1_
  231.1 5.2 %collective-permute-done.8.refs_0_ = bf16[256,512]{1,0:T(8,128)(2,1)S(1)} collective-permute-done((bf16[256,512]{1,0:T(8,128)(2,1)S(1)}, bf16[256,512]{1,0:T(8,128)(2,1)S(1)}, u32[]{:S(2)}, u32[]{:S(2)}) %collective-permute-start.8) | collective-permute-done | bytes 262176 | tf_op jit(solution)/shard_map/ppermute | solution.py:285
  236.3 1.0 score_far.3
  237.2 16.9 %all_to_all.56 = f32[64,1,128]{2,1,0:T(1,128)S(1)} all-to-all(f32[64,1,128]{2,1,0:T(1,128)S(1)} %bitcast.48), channel_id=1, replica_groups=mesh['zh'=4,'zl'=2,'y'=4,'core'=2,'x'=4] {'zl','y','core','x'}, dimensions={0} | all-to-all | bytes 65536 | tf_op jit(solution)/shard_map/all_to_all | solution.py:293
  254.1 0.7 join_halves.3
  254.8 12.2 %all_to_all.57 = f32[64,1,128]{2,1,0:T(1,128)S(1)} all-to-all(f32[64,1,128]{2,1,0:T(1,128)S(1)} %bitcast.52), channel_id=1, replica_groups=mesh['zh'=4,'zl'=2,'y'=4,'core'=2,'x'=4] {'zl','y','core','x'}, dimensions={0} | all-to-all | bytes 65536 | tf_op jit(solution)/shard_map/all_to_all | solution.py:293
  267.0 1.4 weigh_others.4
  268.3 2.4 collective-permute-start.9
  270.7 2.6 weigh_others.5
  273.4 0.2 collective-permute-start.10
  273.6 3.5 %collective-permute-start.11 = (bf16[272,512]{1,0:T(8,128)(2,1)S(1)}, bf16[272,512]{1,0:T(8,128)(2,1)S(1)}, u32[]{:S(2)}, u32[]{:S(2)}) collective-permute-start(bf16[272,512]{1,0:T(8,128)(2,1)S(1)} %get-tuple-element.51), channel_id=1, source_target_pairs={{0,192},{64,0},{128,64},{192,128},{1,193},{65,1},{129,65},{193,129... | collective-permute-start | bytes 835592 | tf_op jit(solution)/shard_map/ppermute | solution.py:285
  277.0 1.4 weigh_own.3
  278.4 8.9 %collective-permute-done.9.message = bf16[272,512]{1,0:T(8,128)(2,1)S(1)} collective-permute-done((bf16[272,512]{1,0:T(8,128)(2,1)S(1)}, bf16[272,512]{1,0:T(8,128)(2,1)S(1)}, u32[]{:S(2)}, u32[]{:S(2)}) %collective-permute-start.9) | collective-permute-done | bytes 278560 | tf_op jit(solution)/shard_map/ppermute | solution.py:285
  287.3 2.1 collective-permute-done.10.m1
  289.5 6.2 %collective-permute-done.11.m2 = bf16[272,512]{1,0:T(8,128)(2,1)S(1)} collective-permute-done((bf16[272,512]{1,0:T(8,128)(2,1)S(1)}, bf16[272,512]{1,0:T(8,128)(2,1)S(1)}, u32[]{:S(2)}, u32[]{:S(2)}) %collective-permute-start.11) | collective-permute-done | bytes 278560 | tf_op jit(solution)/shard_map/ppermute | solution.py:285
  295.6 1.2 new_centres.3
  296.8 3.5 %all-to-all-start.5 = ((bf16[4,256,512]{2,1,0:T(8,128)(2,1)}), bf16[4,256,512]{2,1,0:T(8,128)(2,1)S(1)}, u32[]{:S(2)}, u32[]{:S(2)}) async-start(bf16[4,256,512]{2,1,0:T(8,128)(2,1)} %new_centres.3), calls=%async_computation.5 | async-start | bytes 2097152 | tf_op jit(solution)/shard_map/all_to_all | solution.py:342
  300.4 0.7 reshape.246
  301.0 14.0 %all-to-all-done.5 = bf16[4,256,512]{2,1,0:T(8,128)(2,1)S(1)} async-done(((bf16[4,256,512]{2,1,0:T(8,128)(2,1)}), bf16[4,256,512]{2,1,0:T(8,128)(2,1)S(1)}, u32[]{:S(2)}, u32[]{:S(2)}) %all-to-all-start.5) | async-done | bytes 1048608 | tf_op jit(solution)/shard_map/all_to_all | solution.py:342
  315.0 1.0 copy.29
  (18 shorter events, 0.5 us)
Async XLA Ops:
  0.6 1.2 copy-start
  1.9 15.9 %collective-permute-start = (bf16[256,512]{1,0:T(8,128)(2,1)S(1)}, bf16[256,512]{1,0:T(8,128)(2,1)S(1)}, u32[]{:S(2)}, u32[]{:S(2)}) collective-permute-start(bf16[256,512]{1,0:T(8,128)(2,1)S(1)} %constant_dynamic-slice_fusion.refs_2_.refs_0_.table), channel_id=1, source_target_pairs={{0,192},{64,0},{128,64},{192,128},{1,193},{65,1},{129,65},{193,129... | collective-permute-start | bytes 786440 | tf_op jit(solution)/shard_map/ppermute | solution.py:285
  8.8 10.8 %collective-permute-start.1 = (bf16[256,512]{1,0:T(8,128)(2,1)S(1)}, bf16[256,512]{1,0:T(8,128)(2,1)S(1)}, u32[]{:S(2)}, u32[]{:S(2)}) collective-permute-start(bf16[256,512]{1,0:T(8,128)(2,1)S(1)} %constant_dynamic-slice_fusion.refs_2_.refs_0_.table), channel_id=1, source_target_pairs={{0,64},{64,128},{128,192},{192,0},{1,65},{65,129},{129,193},{193,1... | collective-permute-start | bytes 786440 | tf_op jit(solution)/shard_map/ppermute | solution.py:285
  19.6 15.2 %copy-start.1 = (s32[128,2]{0,1:T(2,128)S(1)}, s32[128,2]{0,1:T(2,128)}, u32[]{:S(2)}) copy-start(s32[128,2]{0,1:T(2,128)} %param.5) | copy-start | bytes 3076
  19.6 123.5 %all-to-all-start = ((bf16[64,128,512]{2,1,0:T(8,128)(2,1)}), bf16[64,128,512]{2,1,0:T(8,128)(2,1)}, u32[]{:S(2)}, u32[]{:S(2)}) async-start(bf16[64,128,512]{2,1,0:T(8,128)(2,1)} %bitcast.54), calls=%async_computation | async-start | bytes 16777216 | tf_op jit(solution)/shard_map/all_to_all | solution.py:293
  33.4 114.8 %collective-permute-start.2 = (bf16[256,512]{1,0:T(8,128)(2,1)S(1)}, bf16[256,512]{1,0:T(8,128)(2,1)S(1)}, u32[]{:S(2)}, u32[]{:S(2)}) collective-permute-start(bf16[256,512]{1,0:T(8,128)(2,1)S(1)} %constant_dynamic-slice_fusion.refs_2_.refs_0_.table), channel_id=1, source_target_pairs={{0,128},{64,192},{128,0},{192,64},{1,129},{65,193},{129,1},{193,65... | collective-permute-start | bytes 786440 | tf_op jit(solution)/shard_map/ppermute | solution.py:285
  183.8 17.6 %collective-permute-start.3 = (bf16[272,512]{1,0:T(8,128)(2,1)S(1)}, bf16[272,512]{1,0:T(8,128)(2,1)S(1)}, u32[]{:S(2)}, u32[]{:S(2)}) collective-permute-start(bf16[272,512]{1,0:T(8,128)(2,1)S(1)} %get-tuple-element.50), channel_id=1, source_target_pairs={{0,128},{64,192},{128,0},{192,64},{1,129},{65,193},{129,1},{193,65... | collective-permute-start | bytes 835592 | tf_op jit(solution)/shard_map/ppermute | solution.py:285
  188.0 22.3 %collective-permute-start.4 = (bf16[272,512]{1,0:T(8,128)(2,1)S(1)}, bf16[272,512]{1,0:T(8,128)(2,1)S(1)}, u32[]{:S(2)}, u32[]{:S(2)}) collective-permute-start(bf16[272,512]{1,0:T(8,128)(2,1)S(1)} %get-tuple-element.49), channel_id=1, source_target_pairs={{0,64},{64,128},{128,192},{192,0},{1,65},{65,129},{129,193},{193,1... | collective-permute-start | bytes 835592 | tf_op jit(solution)/shard_map/ppermute | solution.py:285
  188.0 22.3 %collective-permute-start.5 = (bf16[272,512]{1,0:T(8,128)(2,1)S(1)}, bf16[272,512]{1,0:T(8,128)(2,1)S(1)}, u32[]{:S(2)}, u32[]{:S(2)}) collective-permute-start(bf16[272,512]{1,0:T(8,128)(2,1)S(1)} %get-tuple-element.48), channel_id=1, source_target_pairs={{0,192},{64,0},{128,64},{192,128},{1,193},{65,1},{129,65},{193,129... | collective-permute-start | bytes 835592 | tf_op jit(solution)/shard_map/ppermute | solution.py:285
  210.5 18.2 %collective-permute-start.6 = (bf16[256,512]{1,0:T(8,128)(2,1)S(1)}, bf16[256,512]{1,0:T(8,128)(2,1)S(1)}, u32[]{:S(2)}, u32[]{:S(2)}) collective-permute-start(bf16[256,512]{1,0:T(8,128)(2,1)S(1)} %new_centres.2.refs_2_.refs_0_.table), channel_id=1, source_target_pairs={{0,192},{64,0},{128,64},{192,128},{1,193},{65,1},{129,65},{193,129... | collective-permute-start | bytes 786440 | tf_op jit(solution)/shard_map/ppermute | solution.py:285
  210.9 17.8 %collective-permute-start.7 = (bf16[256,512]{1,0:T(8,128)(2,1)S(1)}, bf16[256,512]{1,0:T(8,128)(2,1)S(1)}, u32[]{:S(2)}, u32[]{:S(2)}) collective-permute-start(bf16[256,512]{1,0:T(8,128)(2,1)S(1)} %new_centres.2.refs_2_.refs_0_.table), channel_id=1, source_target_pairs={{0,64},{64,128},{128,192},{192,0},{1,65},{65,129},{129,193},{193,1... | collective-permute-start | bytes 786440 | tf_op jit(solution)/shard_map/ppermute | solution.py:285
  212.9 23.3 %collective-permute-start.8 = (bf16[256,512]{1,0:T(8,128)(2,1)S(1)}, bf16[256,512]{1,0:T(8,128)(2,1)S(1)}, u32[]{:S(2)}, u32[]{:S(2)}) collective-permute-start(bf16[256,512]{1,0:T(8,128)(2,1)S(1)} %new_centres.2.refs_2_.refs_0_.table), channel_id=1, source_target_pairs={{0,128},{64,192},{128,0},{192,64},{1,129},{65,193},{129,1},{193,65... | collective-permute-start | bytes 786440 | tf_op jit(solution)/shard_map/ppermute | solution.py:285
  268.3 19.0 %collective-permute-start.9 = (bf16[272,512]{1,0:T(8,128)(2,1)S(1)}, bf16[272,512]{1,0:T(8,128)(2,1)S(1)}, u32[]{:S(2)}, u32[]{:S(2)}) collective-permute-start(bf16[272,512]{1,0:T(8,128)(2,1)S(1)} %bitcast.46), channel_id=1, source_target_pairs={{0,128},{64,192},{128,0},{192,64},{1,129},{65,193},{129,1},{193,65... | collective-permute-start | bytes 835592 | tf_op jit(solution)/shard_map/ppermute | solution.py:285
  273.4 16.1 %collective-permute-start.10 = (bf16[272,512]{1,0:T(8,128)(2,1)S(1)}, bf16[272,512]{1,0:T(8,128)(2,1)S(1)}, u32[]{:S(2)}, u32[]{:S(2)}) collective-permute-start(bf16[272,512]{1,0:T(8,128)(2,1)S(1)} %get-tuple-element.52), channel_id=1, source_target_pairs={{0,64},{64,128},{128,192},{192,0},{1,65},{65,129},{129,193},{193,1... | collective-permute-start | bytes 835592 | tf_op jit(solution)/shard_map/ppermute | solution.py:285
  273.6 22.1 %collective-permute-start.11 = (bf16[272,512]{1,0:T(8,128)(2,1)S(1)}, bf16[272,512]{1,0:T(8,128)(2,1)S(1)}, u32[]{:S(2)}, u32[]{:S(2)}) collective-permute-start(bf16[272,512]{1,0:T(8,128)(2,1)S(1)} %get-tuple-element.51), channel_id=1, source_target_pairs={{0,192},{64,0},{128,64},{192,128},{1,193},{65,1},{129,65},{193,129... | collective-permute-start | bytes 835592 | tf_op jit(solution)/shard_map/ppermute | solution.py:285
  296.8 18.2 %all-to-all-start.5 = ((bf16[4,256,512]{2,1,0:T(8,128)(2,1)}), bf16[4,256,512]{2,1,0:T(8,128)(2,1)S(1)}, u32[]{:S(2)}, u32[]{:S(2)}) async-start(bf16[4,256,512]{2,1,0:T(8,128)(2,1)} %new_centres.3), calls=%async_computation.5 | async-start | bytes 2097152 | tf_op jit(solution)/shard_map/all_to_all | solution.py:342

commit v7 on v6

--- a/solution.py
+++ b/solution.py
@@ -268,21 +268,36 @@
         pair = message[CB:].astype(F32)[:1]
         mass += pair[:, :CB] + pair[:, CB:]
     column = jnp.broadcast_to(mass + 1.0, (128, CB)).T[:, :1]
-    fresh = ((total + table[...].astype(F32)) / column).astype(BF16)
-    out[...] = jnp.broadcast_to(fresh, out.shape)
-
-
-def finish(own_sum, own_mass, arrived, table, copies):
+    out[...] = ((total + table[...].astype(F32)) / column).astype(BF16)
+
+
+def finish(own_sum, own_mass, arrived, table):
     return pl.pallas_call(
         finish_kernel,
-        out_shape=jax.ShapeDtypeStruct((*copies, CB, D), BF16),
+        out_shape=jax.ShapeDtypeStruct((CB, D), BF16),
         compiler_params=pltpu.CompilerParams(vmem_limit_bytes=16 << 20),
         name="new_centres",
     )(own_sum, own_mass, *arrived, table)
 
 
-def shifted(value, by):
-    return lax.ppermute(value, "zh", [(i, (i + by) % COPIES) for i in range(COPIES)])
+def place_kernel(x, *refs):
+    pieces, out = refs[:-1], refs[-1]
+    for n in range(COPIES):
+        out[lax.rem(x[0] + COPIES - n, COPIES)] = pieces[n][...]
+
+
+def place(x, pieces):
+    return pl.pallas_call(
+        place_kernel,
+        in_specs=[pl.BlockSpec(memory_space=pltpu.SMEM)] + [pl.BlockSpec(memory_space=pltpu.VMEM)] * COPIES,
+        out_shape=jax.ShapeDtypeStruct((COPIES, CB, D), BF16),
+        compiler_params=pltpu.CompilerParams(vmem_limit_bytes=16 << 20),
+        name="place_blocks",
+    )(x, *pieces)
+
+
+def shifted(value, by, axis="zh"):
+    return lax.ppermute(value, axis, [(i, (i + by) % COPIES) for i in range(COPIES)])
 
 
 def tables_of(own):
@@ -335,11 +350,12 @@
         near_arrived = [shifted(near[0], 1), shifted(near[-1], 3)]
         near, inward = lax.optimization_barrier((near, inward))
         own_sum, own_mass = merge(*weigh_own(me, rows, tables, inward), arrived)
-        own = finish(own_sum, own_mass, near_arrived, own, (COPIES,) if last else ())
+        own = finish(own_sum, own_mass, near_arrived, own)
         if not last:
             tables = tables_of(own)
             partial = score_near(me, rows, tables)
-    gathered = lax.all_to_all(own, "x", split_axis=0, concat_axis=0, tiled=True)
+    pieces = [own] + [shifted(own, n, "x") for n in (1, 2, 3)]
+    gathered = place(lax.axis_index("x").reshape(1), pieces)
     return gathered.reshape(COPIES * CB, D), lse[:, :PB].reshape(-1)
 
 

time: 317 us -> 312 us (0.984)
    all_to_all x1 -> x0, waiting for transfers between devices: 14 us -> none  [on_device(): gathered = lax.all_to_all(own, 'x', split_axis=0, concat_axis=0, tiled=True)]
    ppermute x12 -> x15, waiting for transfers between devices: 55.2 us -> 66 us  [shifted(): lax.ppermute(value, axis, [(i, (i + by) % COPIES) for i in range(COPIES)])]
    ppermute x12 -> x15, starting transfers between devices: 26.5 us -> 30.2 us  [shifted(): lax.ppermute(value, axis, [(i, (i + by) % COPIES) for i in range(COPIES)])]
    all_to_all x1 -> x0, starting transfers between devices: 3.52 us -> none  [on_device(): gathered = lax.all_to_all(own, 'x', split_axis=0, concat_axis=0, tiled=True)]
  transfers between devices with their start and end apart: 14 -> 16, of which waited for: 10 -> 12; matrix products, arithmetic and copies ran while one was open for 1% -> 1% of each run, Pallas kernels for 6% -> 6%
where the time goes in v7:
time: 312 us
  waiting for transfers between devices  174 us (56%)
  blocking collectives  57.9 us (19%)
  starting transfers between devices  44.1 us (14%)
  Pallas kernels  30.1 us (10%)
    all_to_all x1, waiting for transfers between devices, exchange(): return lax.all_to_all(value, GROUP, split_axis=0, concat_axis=0, tiled=True)  108 us
    ppermute x15, waiting for transfers between devices, shifted(): lax.ppermute(value, axis, [(i, (i + by) % COPIES) for i in range(COPIES)])  66 us
    all_to_all x4, blocking collectives, exchange(): return lax.all_to_all(value, GROUP, split_axis=0, concat_axis=0, tiled=True)  57.9 us
    ppermute x15, starting transfers between devices, shifted(): lax.ppermute(value, axis, [(i, (i + by) % COPIES) for i in range(COPIES)])  30.2 us
    pallas_call x8, Pallas kernels, call_whole(): pl.pallas_call(functools.partial(kernel, which), in_specs=[pl.BlockSpec(m...  15.1 us
    all_to_all x1, starting transfers between devices, exchange(): return lax.all_to_all(value, GROUP, split_axis=0, concat_axis=0, tiled=True)  13.8 us
    pallas_call x1, Pallas kernels, pack(): pl.pallas_call(pack_kernel, grid_spec=pltpu.PrefetchScalarGridSpec(num_sc...  6.52 us
  transfers between devices with their start and end apart: 16, of which 12 were waited for; matrix products, arithmetic and copies ran while one was open for 1% of the time, Pallas kernels for 6%

profile of v7, /device:TPU:1, one launch (start us, length us, event | category | flops | bytes accessed | tf_op | source)
XLA Modules:
  0.0 311.6 jit_solution(5612398277267684062)
XLA Ops:
  0.6 1.2 copy-done
  1.9 6.9 %collective-permute-start = (bf16[256,512]{1,0:T(8,128)(2,1)S(1)}, bf16[256,512]{1,0:T(8,128)(2,1)S(1)}, u32[]{:S(2)}, u32[]{:S(2)}) collective-permute-start(bf16[256,512]{1,0:T(8,128)(2,1)S(1)} %constant_dynamic-slice_fusion.refs_2_.refs_0_.table), channel_id=1, source_target_pairs={{0,192},{64,0},{128,64},{192,128},{1,193},{65,1},{129,65},{193,129... | collective-permute-start | bytes 786440 | tf_op jit(solution)/shard_map/ppermute | solution.py:300
  8.8 1.0 fusion
  9.8 0.7 fusion.8
  10.7 0.6 broadcast_add_fusion.src
  11.3 6.5 %pack_points.1 = bf16[512,16,512]{2,1,0:T(8,128)(2,1)} custom-call(s32[512]{0:T(512)} %broadcast_add_fusion.src, bf16[128,16,512]{2,1,0:T(8,128)(2,1)} %bitcast.56), custom_call_target="tpu_custom_call" | custom-call | tf_op jit(solution)/shard_map/pack_points/pallas_call | solution.py:64
  17.8 1.8 collective-permute-done.1.refs_1_.refs_2_
  19.6 13.8 %all-to-all-start = ((bf16[64,128,512]{2,1,0:T(8,128)(2,1)}), bf16[64,128,512]{2,1,0:T(8,128)(2,1)}, u32[]{:S(2)}, u32[]{:S(2)}) async-start(bf16[64,128,512]{2,1,0:T(8,128)(2,1)} %bitcast.55), calls=%async_computation | async-start | bytes 16777216 | tf_op jit(solution)/shard_map/all_to_all | solution.py:308
  33.4 1.4 collective-permute-start.2
  35.2 107.8 %all-to-all-done.source = bf16[64,128,512]{2,1,0:T(8,128)(2,1)} async-done(((bf16[64,128,512]{2,1,0:T(8,128)(2,1)}), bf16[64,128,512]{2,1,0:T(8,128)(2,1)}, u32[]{:S(2)}, u32[]{:S(2)}) %all-to-all-start) | async-done | bytes 8388640 | tf_op jit(solution)/shard_map/all_to_all | solution.py:308
  143.0 5.1 %keep_and_score.1 = (bf16[64,128,512]{2,1,0:T(8,128)(2,1)S(1)}, f32[64,128]{1,0:T(8,128)S(1)}) custom-call(s32[1]{0:T(128)} %bitcast.1.me, bf16[64,128,512]{2,1,0:T(8,128)(2,1)} %all-to-all-done.source, bf16[256,512]{1,0:T(8,128)(2,1)S(1)} %collective-permute-done.refs_0_, bf16[256,512]{1,0:T(8,128)(2,1)S(1)} %collective-permute-done.1.refs_1_.refs_2_, ...), custom_call_target="tpu_custom_call" | custom-call | tf_op jit(solution)/shard_map/keep_and_score/pallas_call | solution.py:158
  148.2 1.0 score_far.2
  149.2 17.3 %all_to_all.49 = f32[64,1,128]{2,1,0:T(1,128)S(1)} all-to-all(f32[64,1,128]{2,1,0:T(1,128)S(1)} %bitcast.48), channel_id=1, replica_groups=mesh['zh'=4,'zl'=2,'y'=4,'core'=2,'x'=4] {'zl','y','core','x'}, dimensions={0} | all-to-all | bytes 65536 | tf_op jit(solution)/shard_map/all_to_all | solution.py:308
  166.5 1.1 join_halves.2
  167.6 12.1 %all_to_all.50 = f32[64,1,128]{2,1,0:T(1,128)S(1)} all-to-all(f32[64,1,128]{2,1,0:T(1,128)S(1)} %bitcast.54), channel_id=1, replica_groups=mesh['zh'=4,'zl'=2,'y'=4,'core'=2,'x'=4] {'zl','y','core','x'}, dimensions={0} | all-to-all | bytes 65536 | tf_op jit(solution)/shard_map/all_to_all | solution.py:308
  179.8 4.0 %weigh_others.3 = bf16[3,272,512]{2,1,0:T(8,128)(2,1)S(1)} custom-call(s32[1]{0:T(128)} %bitcast.1.me, bf16[64,128,512]{2,1,0:T(8,128)(2,1)S(1)} %get-tuple-element.29.rows, bf16[256,512]{1,0:T(8,128)(2,1)S(1)} %collective-permute-done.refs_0_, bf16[256,512]{1,0:T(8,128)(2,1)S(1)} %collective-permute-done.2.refs_0_.refs_1_, ...), custom_call_target="tpu_custom_call" | custom-call | tf_op jit(solution)/shard_map/weigh_others/pallas_call | solution.py:102
  183.8 4.2 %collective-permute-start.3 = (bf16[272,512]{1,0:T(8,128)(2,1)S(1)}, bf16[272,512]{1,0:T(8,128)(2,1)S(1)}, u32[]{:S(2)}, u32[]{:S(2)}) collective-permute-start(bf16[272,512]{1,0:T(8,128)(2,1)S(1)} %get-tuple-element.50), channel_id=1, source_target_pairs={{0,128},{64,192},{128,0},{192,64},{1,129},{65,193},{129,1},{193,65... | collective-permute-start | bytes 835592 | tf_op jit(solution)/shard_map/ppermute | solution.py:300
  188.0 3.6 %collective-permute-start.5 = (bf16[272,512]{1,0:T(8,128)(2,1)S(1)}, bf16[272,512]{1,0:T(8,128)(2,1)S(1)}, u32[]{:S(2)}, u32[]{:S(2)}) collective-permute-start(bf16[272,512]{1,0:T(8,128)(2,1)S(1)} %get-tuple-element.48), channel_id=1, source_target_pairs={{0,192},{64,0},{128,64},{192,128},{1,193},{65,1},{129,65},{193,129... | collective-permute-start | bytes 835592 | tf_op jit(solution)/shard_map/ppermute | solution.py:300
  191.6 1.4 weigh_own.2
  193.0 8.4 %collective-permute-done.3.message = bf16[272,512]{1,0:T(8,128)(2,1)S(1)} collective-permute-done((bf16[272,512]{1,0:T(8,128)(2,1)S(1)}, bf16[272,512]{1,0:T(8,128)(2,1)S(1)}, u32[]{:S(2)}, u32[]{:S(2)}) %collective-permute-start.3) | collective-permute-done | bytes 278560 | tf_op jit(solution)/shard_map/ppermute | solution.py:300
  201.5 8.8 %collective-permute-done.4.m1 = bf16[272,512]{1,0:T(8,128)(2,1)S(1)} collective-permute-done((bf16[272,512]{1,0:T(8,128)(2,1)S(1)}, bf16[272,512]{1,0:T(8,128)(2,1)S(1)}, u32[]{:S(2)}, u32[]{:S(2)}) %collective-permute-start.4) | collective-permute-done | bytes 278560 | tf_op jit(solution)/shard_map/ppermute | solution.py:300
  210.3 0.2 new_centres.2.refs_2_.refs_0_.table
  210.5 0.4 collective-permute-start.6
  210.8 2.1 collective-permute-start.7
  212.9 2.0 collective-permute-start.8
  214.9 13.4 %collective-permute-done.6.refs_0_ = bf16[256,512]{1,0:T(8,128)(2,1)S(1)} collective-permute-done((bf16[256,512]{1,0:T(8,128)(2,1)S(1)}, bf16[256,512]{1,0:T(8,128)(2,1)S(1)}, u32[]{:S(2)}, u32[]{:S(2)}) %collective-permute-start.6) | collective-permute-done | bytes 262176 | tf_op jit(solution)/shard_map/ppermute | solution.py:300
  228.3 2.4 score_near.1.refs_1_
  230.8 5.6 %collective-permute-done.8.refs_0_ = bf16[256,512]{1,0:T(8,128)(2,1)S(1)} collective-permute-done((bf16[256,512]{1,0:T(8,128)(2,1)S(1)}, bf16[256,512]{1,0:T(8,128)(2,1)S(1)}, u32[]{:S(2)}, u32[]{:S(2)}) %collective-permute-start.8) | collective-permute-done | bytes 262176 | tf_op jit(solution)/shard_map/ppermute | solution.py:300
  236.3 1.0 score_far.3
  237.3 16.3 %all_to_all.51 = f32[64,1,128]{2,1,0:T(1,128)S(1)} all-to-all(f32[64,1,128]{2,1,0:T(1,128)S(1)} %bitcast.49), channel_id=1, replica_groups=mesh['zh'=4,'zl'=2,'y'=4,'core'=2,'x'=4] {'zl','y','core','x'}, dimensions={0} | all-to-all | bytes 65536 | tf_op jit(solution)/shard_map/all_to_all | solution.py:308
  253.6 0.7 join_halves.3
  254.3 12.2 %all_to_all.52 = f32[64,1,128]{2,1,0:T(1,128)S(1)} all-to-all(f32[64,1,128]{2,1,0:T(1,128)S(1)} %bitcast.53), channel_id=1, replica_groups=mesh['zh'=4,'zl'=2,'y'=4,'core'=2,'x'=4] {'zl','y','core','x'}, dimensions={0} | all-to-all | bytes 65536 | tf_op jit(solution)/shard_map/all_to_all | solution.py:308
  266.4 1.4 weigh_others.4
  267.8 3.1 collective-permute-start.9
  270.9 2.6 weigh_others.5
  273.6 3.6 %collective-permute-start.11 = (bf16[272,512]{1,0:T(8,128)(2,1)S(1)}, bf16[272,512]{1,0:T(8,128)(2,1)S(1)}, u32[]{:S(2)}, u32[]{:S(2)}) collective-permute-start(bf16[272,512]{1,0:T(8,128)(2,1)S(1)} %get-tuple-element.51), channel_id=1, source_target_pairs={{0,192},{64,0},{128,64},{192,128},{1,193},{65,1},{129,65},{193,129... | collective-permute-start | bytes 835592 | tf_op jit(solution)/shard_map/ppermute | solution.py:300
  277.2 1.4 weigh_own.3
  278.6 7.3 %collective-permute-done.9.message = bf16[272,512]{1,0:T(8,128)(2,1)S(1)} collective-permute-done((bf16[272,512]{1,0:T(8,128)(2,1)S(1)}, bf16[272,512]{1,0:T(8,128)(2,1)S(1)}, u32[]{:S(2)}, u32[]{:S(2)}) %collective-permute-start.9) | collective-permute-done | bytes 278560 | tf_op jit(solution)/shard_map/ppermute | solution.py:300
  286.0 2.7 collective-permute-done.10.m1
  288.6 7.0 %collective-permute-done.11.m2 = bf16[272,512]{1,0:T(8,128)(2,1)S(1)} collective-permute-done((bf16[272,512]{1,0:T(8,128)(2,1)S(1)}, bf16[272,512]{1,0:T(8,128)(2,1)S(1)}, u32[]{:S(2)}, u32[]{:S(2)}) %collective-permute-start.11) | collective-permute-done | bytes 278560 | tf_op jit(solution)/shard_map/ppermute | solution.py:300
  295.9 0.4 collective-permute-start.12
  296.2 1.9 collective-permute-start.13
  298.1 0.8 collective-permute-start.14
  298.9 0.7 reshape.250
  299.6 5.4 %collective-permute-done.12.refs_1_ = bf16[256,512]{1,0:T(8,128)(2,1)S(1)} collective-permute-done((bf16[256,512]{1,0:T(8,128)(2,1)S(1)}, bf16[256,512]{1,0:T(8,128)(2,1)S(1)}, u32[]{:S(2)}, u32[]{:S(2)}) %collective-permute-start.12) | collective-permute-done | bytes 262176 | tf_op jit(solution)/shard_map/ppermute | solution.py:300
  305.0 4.7 %collective-permute-done.13.refs_2_ = bf16[256,512]{1,0:T(8,128)(2,1)S(1)} collective-permute-done((bf16[256,512]{1,0:T(8,128)(2,1)S(1)}, bf16[256,512]{1,0:T(8,128)(2,1)S(1)}, u32[]{:S(2)}, u32[]{:S(2)}) %collective-permute-start.13) | collective-permute-done | bytes 262176 | tf_op jit(solution)/shard_map/ppermute | solution.py:300
  309.7 0.8 collective-permute-done.14.refs_3_
  310.6 1.0 place_blocks.1
  (22 shorter events, 1.1 us)
Async XLA Ops:
  0.6 1.2 copy-start
  1.9 15.9 %collective-permute-start = (bf16[256,512]{1,0:T(8,128)(2,1)S(1)}, bf16[256,512]{1,0:T(8,128)(2,1)S(1)}, u32[]{:S(2)}, u32[]{:S(2)}) collective-permute-start(bf16[256,512]{1,0:T(8,128)(2,1)S(1)} %constant_dynamic-slice_fusion.refs_2_.refs_0_.table), channel_id=1, source_target_pairs={{0,192},{64,0},{128,64},{192,128},{1,193},{65,1},{129,65},{193,129... | collective-permute-start | bytes 786440 | tf_op jit(solution)/shard_map/ppermute | solution.py:300
  8.8 10.8 %collective-permute-start.1 = (bf16[256,512]{1,0:T(8,128)(2,1)S(1)}, bf16[256,512]{1,0:T(8,128)(2,1)S(1)}, u32[]{:S(2)}, u32[]{:S(2)}) collective-permute-start(bf16[256,512]{1,0:T(8,128)(2,1)S(1)} %constant_dynamic-slice_fusion.refs_2_.refs_0_.table), channel_id=1, source_target_pairs={{0,64},{64,128},{128,192},{192,0},{1,65},{65,129},{129,193},{193,1... | collective-permute-start | bytes 786440 | tf_op jit(solution)/shard_map/ppermute | solution.py:300
  19.6 15.2 %copy-start.1 = (s32[128,2]{0,1:T(2,128)S(1)}, s32[128,2]{0,1:T(2,128)}, u32[]{:S(2)}) copy-start(s32[128,2]{0,1:T(2,128)} %param.5) | copy-start | bytes 3076
  19.6 123.5 %all-to-all-start = ((bf16[64,128,512]{2,1,0:T(8,128)(2,1)}), bf16[64,128,512]{2,1,0:T(8,128)(2,1)}, u32[]{:S(2)}, u32[]{:S(2)}) async-start(bf16[64,128,512]{2,1,0:T(8,128)(2,1)} %bitcast.55), calls=%async_computation | async-start | bytes 16777216 | tf_op jit(solution)/shard_map/all_to_all | solution.py:308
  33.4 114.8 %collective-permute-start.2 = (bf16[256,512]{1,0:T(8,128)(2,1)S(1)}, bf16[256,512]{1,0:T(8,128)(2,1)S(1)}, u32[]{:S(2)}, u32[]{:S(2)}) collective-permute-start(bf16[256,512]{1,0:T(8,128)(2,1)S(1)} %constant_dynamic-slice_fusion.refs_2_.refs_0_.table), channel_id=1, source_target_pairs={{0,128},{64,192},{128,0},{192,64},{1,129},{65,193},{129,1},{193,65... | collective-permute-start | bytes 786440 | tf_op jit(solution)/shard_map/ppermute | solution.py:300
  183.8 17.6 %collective-permute-start.3 = (bf16[272,512]{1,0:T(8,128)(2,1)S(1)}, bf16[272,512]{1,0:T(8,128)(2,1)S(1)}, u32[]{:S(2)}, u32[]{:S(2)}) collective-permute-start(bf16[272,512]{1,0:T(8,128)(2,1)S(1)} %get-tuple-element.50), channel_id=1, source_target_pairs={{0,128},{64,192},{128,0},{192,64},{1,129},{65,193},{129,1},{193,65... | collective-permute-start | bytes 835592 | tf_op jit(solution)/shard_map/ppermute | solution.py:300
  188.0 22.2 %collective-permute-start.4 = (bf16[272,512]{1,0:T(8,128)(2,1)S(1)}, bf16[272,512]{1,0:T(8,128)(2,1)S(1)}, u32[]{:S(2)}, u32[]{:S(2)}) collective-permute-start(bf16[272,512]{1,0:T(8,128)(2,1)S(1)} %get-tuple-element.49), channel_id=1, source_target_pairs={{0,64},{64,128},{128,192},{192,0},{1,65},{65,129},{129,193},{193,1... | collective-permute-start | bytes 835592 | tf_op jit(solution)/shard_map/ppermute | solution.py:300
  188.0 22.2 %collective-permute-start.5 = (bf16[272,512]{1,0:T(8,128)(2,1)S(1)}, bf16[272,512]{1,0:T(8,128)(2,1)S(1)}, u32[]{:S(2)}, u32[]{:S(2)}) collective-permute-start(bf16[272,512]{1,0:T(8,128)(2,1)S(1)} %get-tuple-element.48), channel_id=1, source_target_pairs={{0,192},{64,0},{128,64},{192,128},{1,193},{65,1},{129,65},{193,129... | collective-permute-start | bytes 835592 | tf_op jit(solution)/shard_map/ppermute | solution.py:300
  210.5 17.9 %collective-permute-start.6 = (bf16[256,512]{1,0:T(8,128)(2,1)S(1)}, bf16[256,512]{1,0:T(8,128)(2,1)S(1)}, u32[]{:S(2)}, u32[]{:S(2)}) collective-permute-start(bf16[256,512]{1,0:T(8,128)(2,1)S(1)} %new_centres.2.refs_2_.refs_0_.table), channel_id=1, source_target_pairs={{0,192},{64,0},{128,64},{192,128},{1,193},{65,1},{129,65},{193,129... | collective-permute-start | bytes 786440 | tf_op jit(solution)/shard_map/ppermute | solution.py:300
  210.8 17.5 %collective-permute-start.7 = (bf16[256,512]{1,0:T(8,128)(2,1)S(1)}, bf16[256,512]{1,0:T(8,128)(2,1)S(1)}, u32[]{:S(2)}, u32[]{:S(2)}) collective-permute-start(bf16[256,512]{1,0:T(8,128)(2,1)S(1)} %new_centres.2.refs_2_.refs_0_.table), channel_id=1, source_target_pairs={{0,64},{64,128},{128,192},{192,0},{1,65},{65,129},{129,193},{193,1... | collective-permute-start | bytes 786440 | tf_op jit(solution)/shard_map/ppermute | solution.py:300
  212.9 23.4 %collective-permute-start.8 = (bf16[256,512]{1,0:T(8,128)(2,1)S(1)}, bf16[256,512]{1,0:T(8,128)(2,1)S(1)}, u32[]{:S(2)}, u32[]{:S(2)}) collective-permute-start(bf16[256,512]{1,0:T(8,128)(2,1)S(1)} %new_centres.2.refs_2_.refs_0_.table), channel_id=1, source_target_pairs={{0,128},{64,192},{128,0},{192,64},{1,129},{65,193},{129,1},{193,65... | collective-permute-start | bytes 786440 | tf_op jit(solution)/shard_map/ppermute | solution.py:300
  267.8 18.1 %collective-permute-start.9 = (bf16[272,512]{1,0:T(8,128)(2,1)S(1)}, bf16[272,512]{1,0:T(8,128)(2,1)S(1)}, u32[]{:S(2)}, u32[]{:S(2)}) collective-permute-start(bf16[272,512]{1,0:T(8,128)(2,1)S(1)} %bitcast.47), channel_id=1, source_target_pairs={{0,128},{64,192},{128,0},{192,64},{1,129},{65,193},{129,1},{193,65... | collective-permute-start | bytes 835592 | tf_op jit(solution)/shard_map/ppermute | solution.py:300
  273.5 15.1 %collective-permute-start.10 = (bf16[272,512]{1,0:T(8,128)(2,1)S(1)}, bf16[272,512]{1,0:T(8,128)(2,1)S(1)}, u32[]{:S(2)}, u32[]{:S(2)}) collective-permute-start(bf16[272,512]{1,0:T(8,128)(2,1)S(1)} %get-tuple-element.52), channel_id=1, source_target_pairs={{0,64},{64,128},{128,192},{192,0},{1,65},{65,129},{129,193},{193,1... | collective-permute-start | bytes 835592 | tf_op jit(solution)/shard_map/ppermute | solution.py:300
  273.6 22.0 %collective-permute-start.11 = (bf16[272,512]{1,0:T(8,128)(2,1)S(1)}, bf16[272,512]{1,0:T(8,128)(2,1)S(1)}, u32[]{:S(2)}, u32[]{:S(2)}) collective-permute-start(bf16[272,512]{1,0:T(8,128)(2,1)S(1)} %get-tuple-element.51), channel_id=1, source_target_pairs={{0,192},{64,0},{128,64},{192,128},{1,193},{65,1},{129,65},{193,129... | collective-permute-start | bytes 835592 | tf_op jit(solution)/shard_map/ppermute | solution.py:300
  295.9 9.1 %collective-permute-start.12 = (bf16[256,512]{1,0:T(8,128)(2,1)S(1)}, bf16[256,512]{1,0:T(8,128)(2,1)S(1)}, u32[]{:S(2)}, u32[]{:S(2)}) collective-permute-start(bf16[256,512]{1,0:T(8,128)(2,1)S(1)} %new_centres.3.refs_0_), channel_id=1, source_target_pairs={{0,1},{1,2},{2,3},{3,0},{4,5},{5,6},{6,7},{7,4},{8,9},{9,10},{10,1... | collective-permute-start | bytes 786440 | tf_op jit(solution)/shard_map/ppermute | solution.py:300
  296.2 13.5 %collective-permute-start.13 = (bf16[256,512]{1,0:T(8,128)(2,1)S(1)}, bf16[256,512]{1,0:T(8,128)(2,1)S(1)}, u32[]{:S(2)}, u32[]{:S(2)}) collective-permute-start(bf16[256,512]{1,0:T(8,128)(2,1)S(1)} %new_centres.3.refs_0_), channel_id=1, source_target_pairs={{0,2},{1,3},{2,0},{3,1},{4,6},{5,7},{6,4},{7,5},{8,10},{9,11},{10,... | collective-permute-start | bytes 786440 | tf_op jit(solution)/shard_map/ppermute | solution.py:300
  298.1 12.4 %collective-permute-start.14 = (bf16[256,512]{1,0:T(8,128)(2,1)S(1)}, bf16[256,512]{1,0:T(8,128)(2,1)S(1)}, u32[]{:S(2)}, u32[]{:S(2)}) collective-permute-start(bf16[256,512]{1,0:T(8,128)(2,1)S(1)} %new_centres.3.refs_0_), channel_id=1, source_target_pairs={{0,3},{1,0},{2,1},{3,2},{4,7},{5,4},{6,5},{7,6},{8,11},{9,8},{10,9... | collective-permute-start | bytes 786440 | tf_op jit(solution)/shard_map/ppermute | solution.py:300

commit v8 on v7

--- a/solution.py
+++ b/solution.py
@@ -45,6 +45,25 @@
 
 def iota(shape, dim):
     return lax.broadcasted_iota(jnp.int32, shape, dim)
+
+
+def fetch_kernel(x, source, out, done):
+    start = pl.multiple_of(x[0] * CB, CB)
+    copy = pltpu.make_async_copy(source.at[pl.ds(start, CB)], out, done)
+    copy.start()
+    copy.wait()
+
+
+def fetch(x, centroids):
+    return pl.pallas_call(
+        fetch_kernel,
+        in_specs=[pl.BlockSpec(memory_space=pltpu.SMEM), pl.BlockSpec(memory_space=pl.ANY)],
+        out_specs=pl.BlockSpec(memory_space=pltpu.VMEM),
+        out_shape=jax.ShapeDtypeStruct((CB, D), BF16),
+        scratch_shapes=[pltpu.SemaphoreType.DMA],
+        compiler_params=pltpu.CompilerParams(vmem_limit_bytes=58 << 20),
+        name="fetch_own",
+    )(x, centroids)
 
 
 def pack_kernel(src, points, out):
@@ -326,7 +345,7 @@
 
 def on_device(points, centroids, candidates):
     me = lax.axis_index("zh").reshape(1)
-    own = lax.dynamic_slice_in_dim(centroids, lax.axis_index("x") * CB, CB, 0)
+    own = fetch(lax.axis_index("x").reshape(1), centroids)
     source, peer, slot = route(candidates)
     outgoing = pack(source, points.reshape(PBD, PB, D))
     where = (peer[:, None], slot[:, None], peer[None, :])

time: 312 us -> 313 us (level)
  no operation moved by 1% of the time
where the time goes in v8:
time: 313 us; the launch traced here: 312 us
  waiting for transfers between devices  172 us (55%)
  blocking collectives  60.4 us (19%)
  starting transfers between devices  43.9 us (14%)
  Pallas kernels  31.8 us (10%)
    all_to_all x1, waiting for transfers between devices, exchange(): return lax.all_to_all(value, GROUP, split_axis=0, concat_axis=0, tiled=True)  105 us
    ppermute x15, waiting for transfers between devices, shifted(): lax.ppermute(value, axis, [(i, (i + by) % COPIES) for i in range(COPIES)])  66.4 us
    all_to_all x4, blocking collectives, exchange(): return lax.all_to_all(value, GROUP, split_axis=0, concat_axis=0, tiled=True)  60.4 us
    ppermute x15, starting transfers between devices, shifted(): lax.ppermute(value, axis, [(i, (i + by) % COPIES) for i in range(COPIES)])  30 us
    pallas_call x8, Pallas kernels, call_whole(): pl.pallas_call(functools.partial(kernel, which), in_specs=[pl.BlockSpec(m...  15.1 us
    all_to_all x1, starting transfers between devices, exchange(): return lax.all_to_all(value, GROUP, split_axis=0, concat_axis=0, tiled=True)  13.9 us
    pallas_call x1, Pallas kernels, pack(): pl.pallas_call(pack_kernel, grid_spec=pltpu.PrefetchScalarGridSpec(num_sc...  6.52 us
  transfers between devices with their start and end apart: 16, of which 12 were waited for; matrix products, arithmetic and copies ran while one was open for 1% of the time, Pallas kernels for 6%

profile of v8, /device:TPU:1, one launch (start us, length us, event | category | flops | bytes accessed | tf_op | source)
XLA Modules:
  0.0 312.3 jit_solution(70808513370236560)
XLA Ops:
  0.6 1.7 fetch_own.1.refs_2_.refs_0_.table
  2.3 6.9 %collective-permute-start = (bf16[256,512]{1,0:T(8,128)(2,1)}, bf16[256,512]{1,0:T(8,128)(2,1)S(1)}, u32[]{:S(2)}, u32[]{:S(2)}) collective-permute-start(bf16[256,512]{1,0:T(8,128)(2,1)} %fetch_own.1.refs_2_.refs_0_.table), channel_id=1, source_target_pairs={{0,192},{64,0},{128,64},{192,128},{1,193},{65,1},{129,65},{193,129... | collective-permute-start | bytes 786440 | tf_op jit(solution)/shard_map/ppermute | solution.py:319
  9.2 1.0 fusion
  10.2 0.7 fusion.8
  11.1 0.6 broadcast_add_fusion.src
  11.7 6.5 %pack_points.1 = bf16[512,16,512]{2,1,0:T(8,128)(2,1)} custom-call(s32[512]{0:T(512)} %broadcast_add_fusion.src, bf16[128,16,512]{2,1,0:T(8,128)(2,1)} %bitcast.56), custom_call_target="tpu_custom_call" | custom-call | tf_op jit(solution)/shard_map/pack_points/pallas_call | solution.py:83
  18.2 2.0 collective-permute-done.1.refs_1_.refs_2_
  20.2 13.9 %all-to-all-start = ((bf16[64,128,512]{2,1,0:T(8,128)(2,1)}), bf16[64,128,512]{2,1,0:T(8,128)(2,1)}, u32[]{:S(2)}, u32[]{:S(2)}) async-start(bf16[64,128,512]{2,1,0:T(8,128)(2,1)} %bitcast.55), calls=%async_computation | async-start | bytes 16777216 | tf_op jit(solution)/shard_map/all_to_all | solution.py:327
  34.1 1.4 collective-permute-start.2
  35.9 105.4 %all-to-all-done.source = bf16[64,128,512]{2,1,0:T(8,128)(2,1)} async-done(((bf16[64,128,512]{2,1,0:T(8,128)(2,1)}), bf16[64,128,512]{2,1,0:T(8,128)(2,1)}, u32[]{:S(2)}, u32[]{:S(2)}) %all-to-all-start) | async-done | bytes 8388640 | tf_op jit(solution)/shard_map/all_to_all | solution.py:327
  141.3 5.2 %keep_and_score.1 = (bf16[64,128,512]{2,1,0:T(8,128)(2,1)S(1)}, f32[64,128]{1,0:T(8,128)S(1)}) custom-call(s32[1]{0:T(128)} %bitcast.1.me, bf16[64,128,512]{2,1,0:T(8,128)(2,1)} %all-to-all-done.source, bf16[256,512]{1,0:T(8,128)(2,1)S(1)} %collective-permute-done.refs_0_, bf16[256,512]{1,0:T(8,128)(2,1)S(1)} %collective-permute-done.1.refs_1_.refs_2_, ...), custom_call_target="tpu_custom_call" | custom-call | tf_op jit(solution)/shard_map/keep_and_score/pallas_call | solution.py:177
  146.5 1.0 score_far.2
  147.5 19.7 %all_to_all.49 = f32[64,1,128]{2,1,0:T(1,128)S(1)} all-to-all(f32[64,1,128]{2,1,0:T(1,128)S(1)} %bitcast.48), channel_id=1, replica_groups=mesh['zh'=4,'zl'=2,'y'=4,'core'=2,'x'=4] {'zl','y','core','x'}, dimensions={0} | all-to-all | bytes 65536 | tf_op jit(solution)/shard_map/all_to_all | solution.py:327
  167.1 1.1 join_halves.2
  168.3 12.1 %all_to_all.50 = f32[64,1,128]{2,1,0:T(1,128)S(1)} all-to-all(f32[64,1,128]{2,1,0:T(1,128)S(1)} %bitcast.54), channel_id=1, replica_groups=mesh['zh'=4,'zl'=2,'y'=4,'core'=2,'x'=4] {'zl','y','core','x'}, dimensions={0} | all-to-all | bytes 65536 | tf_op jit(solution)/shard_map/all_to_all | solution.py:327
  180.4 4.0 %weigh_others.3 = bf16[3,272,512]{2,1,0:T(8,128)(2,1)S(1)} custom-call(s32[1]{0:T(128)} %bitcast.1.me, bf16[64,128,512]{2,1,0:T(8,128)(2,1)S(1)} %get-tuple-element.29.rows, bf16[256,512]{1,0:T(8,128)(2,1)S(1)} %collective-permute-done.refs_0_, bf16[256,512]{1,0:T(8,128)(2,1)S(1)} %collective-permute-done.2.refs_0_.refs_1_, ...), custom_call_target="tpu_custom_call" | custom-call | tf_op jit(solution)/shard_map/weigh_others/pallas_call | solution.py:121
  184.5 4.2 %collective-permute-start.3 = (bf16[272,512]{1,0:T(8,128)(2,1)S(1)}, bf16[272,512]{1,0:T(8,128)(2,1)S(1)}, u32[]{:S(2)}, u32[]{:S(2)}) collective-permute-start(bf16[272,512]{1,0:T(8,128)(2,1)S(1)} %get-tuple-element.50), channel_id=1, source_target_pairs={{0,128},{64,192},{128,0},{192,64},{1,129},{65,193},{129,1},{193,65... | collective-permute-start | bytes 835592 | tf_op jit(solution)/shard_map/ppermute | solution.py:319
  188.7 3.6 %collective-permute-start.5 = (bf16[272,512]{1,0:T(8,128)(2,1)S(1)}, bf16[272,512]{1,0:T(8,128)(2,1)S(1)}, u32[]{:S(2)}, u32[]{:S(2)}) collective-permute-start(bf16[272,512]{1,0:T(8,128)(2,1)S(1)} %get-tuple-element.48), channel_id=1, source_target_pairs={{0,192},{64,0},{128,64},{192,128},{1,193},{65,1},{129,65},{193,129... | collective-permute-start | bytes 835592 | tf_op jit(solution)/shard_map/ppermute | solution.py:319
  192.2 1.4 weigh_own.2
  193.6 8.5 %collective-permute-done.3.message = bf16[272,512]{1,0:T(8,128)(2,1)S(1)} collective-permute-done((bf16[272,512]{1,0:T(8,128)(2,1)S(1)}, bf16[272,512]{1,0:T(8,128)(2,1)S(1)}, u32[]{:S(2)}, u32[]{:S(2)}) %collective-permute-start.3) | collective-permute-done | bytes 278560 | tf_op jit(solution)/shard_map/ppermute | solution.py:319
  202.2 8.8 %collective-permute-done.4.m1 = bf16[272,512]{1,0:T(8,128)(2,1)S(1)} collective-permute-done((bf16[272,512]{1,0:T(8,128)(2,1)S(1)}, bf16[272,512]{1,0:T(8,128)(2,1)S(1)}, u32[]{:S(2)}, u32[]{:S(2)}) %collective-permute-start.4) | collective-permute-done | bytes 278560 | tf_op jit(solution)/shard_map/ppermute | solution.py:319
  211.2 0.4 collective-permute-start.6
  211.5 2.1 collective-permute-start.7
  213.6 1.9 collective-permute-start.8
  215.5 13.8 %collective-permute-done.6.refs_0_ = bf16[256,512]{1,0:T(8,128)(2,1)S(1)} collective-permute-done((bf16[256,512]{1,0:T(8,128)(2,1)S(1)}, bf16[256,512]{1,0:T(8,128)(2,1)S(1)}, u32[]{:S(2)}, u32[]{:S(2)}) %collective-permute-start.6) | collective-permute-done | bytes 262176 | tf_op jit(solution)/shard_map/ppermute | solution.py:319
  229.4 2.4 score_near.1.refs_1_
  231.8 5.1 %collective-permute-done.8.refs_0_ = bf16[256,512]{1,0:T(8,128)(2,1)S(1)} collective-permute-done((bf16[256,512]{1,0:T(8,128)(2,1)S(1)}, bf16[256,512]{1,0:T(8,128)(2,1)S(1)}, u32[]{:S(2)}, u32[]{:S(2)}) %collective-permute-start.8) | collective-permute-done | bytes 262176 | tf_op jit(solution)/shard_map/ppermute | solution.py:319
  236.9 1.0 score_far.3
  237.9 16.4 %all_to_all.51 = f32[64,1,128]{2,1,0:T(1,128)S(1)} all-to-all(f32[64,1,128]{2,1,0:T(1,128)S(1)} %bitcast.49), channel_id=1, replica_groups=mesh['zh'=4,'zl'=2,'y'=4,'core'=2,'x'=4] {'zl','y','core','x'}, dimensions={0} | all-to-all | bytes 65536 | tf_op jit(solution)/shard_map/all_to_all | solution.py:327
  254.3 0.7 join_halves.3
  255.0 12.2 %all_to_all.52 = f32[64,1,128]{2,1,0:T(1,128)S(1)} all-to-all(f32[64,1,128]{2,1,0:T(1,128)S(1)} %bitcast.53), channel_id=1, replica_groups=mesh['zh'=4,'zl'=2,'y'=4,'core'=2,'x'=4] {'zl','y','core','x'}, dimensions={0} | all-to-all | bytes 65536 | tf_op jit(solution)/shard_map/all_to_all | solution.py:327
  267.1 1.4 weigh_others.4
  268.5 2.8 collective-permute-start.9
  271.3 2.6 weigh_others.5
  274.0 0.3 collective-permute-start.10
  274.3 3.4 %collective-permute-start.11 = (bf16[272,512]{1,0:T(8,128)(2,1)S(1)}, bf16[272,512]{1,0:T(8,128)(2,1)S(1)}, u32[]{:S(2)}, u32[]{:S(2)}) collective-permute-start(bf16[272,512]{1,0:T(8,128)(2,1)S(1)} %get-tuple-element.51), channel_id=1, source_target_pairs={{0,192},{64,0},{128,64},{192,128},{1,193},{65,1},{129,65},{193,129... | collective-permute-start | bytes 835592 | tf_op jit(solution)/shard_map/ppermute | solution.py:319
  277.6 1.4 weigh_own.3
  279.0 7.6 %collective-permute-done.9.message = bf16[272,512]{1,0:T(8,128)(2,1)S(1)} collective-permute-done((bf16[272,512]{1,0:T(8,128)(2,1)S(1)}, bf16[272,512]{1,0:T(8,128)(2,1)S(1)}, u32[]{:S(2)}, u32[]{:S(2)}) %collective-permute-start.9) | collective-permute-done | bytes 278560 | tf_op jit(solution)/shard_map/ppermute | solution.py:319
  286.6 2.8 collective-permute-done.10.m1
  289.5 6.9 %collective-permute-done.11.m2 = bf16[272,512]{1,0:T(8,128)(2,1)S(1)} collective-permute-done((bf16[272,512]{1,0:T(8,128)(2,1)S(1)}, bf16[272,512]{1,0:T(8,128)(2,1)S(1)}, u32[]{:S(2)}, u32[]{:S(2)}) %collective-permute-start.11) | collective-permute-done | bytes 278560 | tf_op jit(solution)/shard_map/ppermute | solution.py:319
  296.6 0.4 collective-permute-start.12
  296.9 1.9 collective-permute-start.13
  298.8 0.8 collective-permute-start.14
  299.6 0.7 reshape.251
  300.3 5.4 %collective-permute-done.12.refs_1_ = bf16[256,512]{1,0:T(8,128)(2,1)S(1)} collective-permute-done((bf16[256,512]{1,0:T(8,128)(2,1)S(1)}, bf16[256,512]{1,0:T(8,128)(2,1)S(1)}, u32[]{:S(2)}, u32[]{:S(2)}) %collective-permute-start.12) | collective-permute-done | bytes 262176 | tf_op jit(solution)/shard_map/ppermute | solution.py:319
  305.7 4.7 %collective-permute-done.13.refs_2_ = bf16[256,512]{1,0:T(8,128)(2,1)S(1)} collective-permute-done((bf16[256,512]{1,0:T(8,128)(2,1)S(1)}, bf16[256,512]{1,0:T(8,128)(2,1)S(1)}, u32[]{:S(2)}, u32[]{:S(2)}) %collective-permute-start.13) | collective-permute-done | bytes 262176 | tf_op jit(solution)/shard_map/ppermute | solution.py:319
  310.4 0.8 collective-permute-done.14.refs_3_
  311.3 1.0 place_blocks.1
  (22 shorter events, 1.2 us)
Async XLA Ops:
  2.3 15.9 %collective-permute-start = (bf16[256,512]{1,0:T(8,128)(2,1)}, bf16[256,512]{1,0:T(8,128)(2,1)S(1)}, u32[]{:S(2)}, u32[]{:S(2)}) collective-permute-start(bf16[256,512]{1,0:T(8,128)(2,1)} %fetch_own.1.refs_2_.refs_0_.table), channel_id=1, source_target_pairs={{0,192},{64,0},{128,64},{192,128},{1,193},{65,1},{129,65},{193,129... | collective-permute-start | bytes 786440 | tf_op jit(solution)/shard_map/ppermute | solution.py:319
  9.2 10.9 %collective-permute-start.1 = (bf16[256,512]{1,0:T(8,128)(2,1)}, bf16[256,512]{1,0:T(8,128)(2,1)S(1)}, u32[]{:S(2)}, u32[]{:S(2)}) collective-permute-start(bf16[256,512]{1,0:T(8,128)(2,1)} %fetch_own.1.refs_2_.refs_0_.table), channel_id=1, source_target_pairs={{0,64},{64,128},{128,192},{192,0},{1,65},{65,129},{129,193},{193,1... | collective-permute-start | bytes 786440 | tf_op jit(solution)/shard_map/ppermute | solution.py:319
  20.2 13.9 %copy-start = (bf16[256,512]{1,0:T(8,128)(2,1)S(1)}, bf16[256,512]{1,0:T(8,128)(2,1)}, u32[]{:S(2)}) copy-start(bf16[256,512]{1,0:T(8,128)(2,1)} %fetch_own.1.refs_2_.refs_0_.table) | copy-start | bytes 786436
  20.2 15.3 %copy-start.1 = (s32[128,2]{0,1:T(2,128)S(1)}, s32[128,2]{0,1:T(2,128)}, u32[]{:S(2)}) copy-start(s32[128,2]{0,1:T(2,128)} %param.5) | copy-start | bytes 3076
  20.2 121.1 %all-to-all-start = ((bf16[64,128,512]{2,1,0:T(8,128)(2,1)}), bf16[64,128,512]{2,1,0:T(8,128)(2,1)}, u32[]{:S(2)}, u32[]{:S(2)}) async-start(bf16[64,128,512]{2,1,0:T(8,128)(2,1)} %bitcast.55), calls=%async_computation | async-start | bytes 16777216 | tf_op jit(solution)/shard_map/all_to_all | solution.py:327
  34.1 112.4 %collective-permute-start.2 = (bf16[256,512]{1,0:T(8,128)(2,1)S(1)}, bf16[256,512]{1,0:T(8,128)(2,1)S(1)}, u32[]{:S(2)}, u32[]{:S(2)}) collective-permute-start(bf16[256,512]{1,0:T(8,128)(2,1)S(1)} %copy-done), channel_id=1, source_target_pairs={{0,128},{64,192},{128,0},{192,64},{1,129},{65,193},{129,1},{193,65... | collective-permute-start | bytes 786440 | tf_op jit(solution)/shard_map/ppermute | solution.py:319
  184.5 17.7 %collective-permute-start.3 = (bf16[272,512]{1,0:T(8,128)(2,1)S(1)}, bf16[272,512]{1,0:T(8,128)(2,1)S(1)}, u32[]{:S(2)}, u32[]{:S(2)}) collective-permute-start(bf16[272,512]{1,0:T(8,128)(2,1)S(1)} %get-tuple-element.50), channel_id=1, source_target_pairs={{0,128},{64,192},{128,0},{192,64},{1,129},{65,193},{129,1},{193,65... | collective-permute-start | bytes 835592 | tf_op jit(solution)/shard_map/ppermute | solution.py:319
  188.7 22.3 %collective-permute-start.4 = (bf16[272,512]{1,0:T(8,128)(2,1)S(1)}, bf16[272,512]{1,0:T(8,128)(2,1)S(1)}, u32[]{:S(2)}, u32[]{:S(2)}) collective-permute-start(bf16[272,512]{1,0:T(8,128)(2,1)S(1)} %get-tuple-element.49), channel_id=1, source_target_pairs={{0,64},{64,128},{128,192},{192,0},{1,65},{65,129},{129,193},{193,1... | collective-permute-start | bytes 835592 | tf_op jit(solution)/shard_map/ppermute | solution.py:319
  188.7 22.3 %collective-permute-start.5 = (bf16[272,512]{1,0:T(8,128)(2,1)S(1)}, bf16[272,512]{1,0:T(8,128)(2,1)S(1)}, u32[]{:S(2)}, u32[]{:S(2)}) collective-permute-start(bf16[272,512]{1,0:T(8,128)(2,1)S(1)} %get-tuple-element.48), channel_id=1, source_target_pairs={{0,192},{64,0},{128,64},{192,128},{1,193},{65,1},{129,65},{193,129... | collective-permute-start | bytes 835592 | tf_op jit(solution)/shard_map/ppermute | solution.py:319
  211.2 18.2 %collective-permute-start.6 = (bf16[256,512]{1,0:T(8,128)(2,1)S(1)}, bf16[256,512]{1,0:T(8,128)(2,1)S(1)}, u32[]{:S(2)}, u32[]{:S(2)}) collective-permute-start(bf16[256,512]{1,0:T(8,128)(2,1)S(1)} %new_centres.2.refs_2_.refs_0_.table), channel_id=1, source_target_pairs={{0,192},{64,0},{128,64},{192,128},{1,193},{65,1},{129,65},{193,129... | collective-permute-start | bytes 786440 | tf_op jit(solution)/shard_map/ppermute | solution.py:319
  211.5 17.8 %collective-permute-start.7 = (bf16[256,512]{1,0:T(8,128)(2,1)S(1)}, bf16[256,512]{1,0:T(8,128)(2,1)S(1)}, u32[]{:S(2)}, u32[]{:S(2)}) collective-permute-start(bf16[256,512]{1,0:T(8,128)(2,1)S(1)} %new_centres.2.refs_2_.refs_0_.table), channel_id=1, source_target_pairs={{0,64},{64,128},{128,192},{192,0},{1,65},{65,129},{129,193},{193,1... | collective-permute-start | bytes 786440 | tf_op jit(solution)/shard_map/ppermute | solution.py:319
  213.6 23.3 %collective-permute-start.8 = (bf16[256,512]{1,0:T(8,128)(2,1)S(1)}, bf16[256,512]{1,0:T(8,128)(2,1)S(1)}, u32[]{:S(2)}, u32[]{:S(2)}) collective-permute-start(bf16[256,512]{1,0:T(8,128)(2,1)S(1)} %new_centres.2.refs_2_.refs_0_.table), channel_id=1, source_target_pairs={{0,128},{64,192},{128,0},{192,64},{1,129},{65,193},{129,1},{193,65... | collective-permute-start | bytes 786440 | tf_op jit(solution)/shard_map/ppermute | solution.py:319
  268.5 18.1 %collective-permute-start.9 = (bf16[272,512]{1,0:T(8,128)(2,1)S(1)}, bf16[272,512]{1,0:T(8,128)(2,1)S(1)}, u32[]{:S(2)}, u32[]{:S(2)}) collective-permute-start(bf16[272,512]{1,0:T(8,128)(2,1)S(1)} %bitcast.47), channel_id=1, source_target_pairs={{0,128},{64,192},{128,0},{192,64},{1,129},{65,193},{129,1},{193,65... | collective-permute-start | bytes 835592 | tf_op jit(solution)/shard_map/ppermute | solution.py:319
  274.0 15.5 %collective-permute-start.10 = (bf16[272,512]{1,0:T(8,128)(2,1)S(1)}, bf16[272,512]{1,0:T(8,128)(2,1)S(1)}, u32[]{:S(2)}, u32[]{:S(2)}) collective-permute-start(bf16[272,512]{1,0:T(8,128)(2,1)S(1)} %get-tuple-element.52), channel_id=1, source_target_pairs={{0,64},{64,128},{128,192},{192,0},{1,65},{65,129},{129,193},{193,1... | collective-permute-start | bytes 835592 | tf_op jit(solution)/shard_map/ppermute | solution.py:319
  274.3 22.1 %collective-permute-start.11 = (bf16[272,512]{1,0:T(8,128)(2,1)S(1)}, bf16[272,512]{1,0:T(8,128)(2,1)S(1)}, u32[]{:S(2)}, u32[]{:S(2)}) collective-permute-start(bf16[272,512]{1,0:T(8,128)(2,1)S(1)} %get-tuple-element.51), channel_id=1, source_target_pairs={{0,192},{64,0},{128,64},{192,128},{1,193},{65,1},{129,65},{193,129... | collective-permute-start | bytes 835592 | tf_op jit(solution)/shard_map/ppermute | solution.py:319
  296.6 9.1 %collective-permute-start.12 = (bf16[256,512]{1,0:T(8,128)(2,1)S(1)}, bf16[256,512]{1,0:T(8,128)(2,1)S(1)}, u32[]{:S(2)}, u32[]{:S(2)}) collective-permute-start(bf16[256,512]{1,0:T(8,128)(2,1)S(1)} %new_centres.3.refs_0_), channel_id=1, source_target_pairs={{0,1},{1,2},{2,3},{3,0},{4,5},{5,6},{6,7},{7,4},{8,9},{9,10},{10,1... | collective-permute-start | bytes 786440 | tf_op jit(solution)/shard_map/ppermute | solution.py:319
  296.9 13.5 %collective-permute-start.13 = (bf16[256,512]{1,0:T(8,128)(2,1)S(1)}, bf16[256,512]{1,0:T(8,128)(2,1)S(1)}, u32[]{:S(2)}, u32[]{:S(2)}) collective-permute-start(bf16[256,512]{1,0:T(8,128)(2,1)S(1)} %new_centres.3.refs_0_), channel_id=1, source_target_pairs={{0,2},{1,3},{2,0},{3,1},{4,6},{5,7},{6,4},{7,5},{8,10},{9,11},{10,... | collective-permute-start | bytes 786440 | tf_op jit(solution)/shard_map/ppermute | solution.py:319
  298.8 12.4 %collective-permute-start.14 = (bf16[256,512]{1,0:T(8,128)(2,1)S(1)}, bf16[256,512]{1,0:T(8,128)(2,1)S(1)}, u32[]{:S(2)}, u32[]{:S(2)}) collective-permute-start(bf16[256,512]{1,0:T(8,128)(2,1)S(1)} %new_centres.3.refs_0_), channel_id=1, source_target_pairs={{0,3},{1,0},{2,1},{3,2},{4,7},{5,4},{6,5},{7,6},{8,11},{9,8},{10,9... | collective-permute-start | bytes 786440 | tf_op jit(solution)/shard_map/ppermute | solution.py:319
